TPU v7x, 32 devices: a whole 2x2x4 slice. The times are simulated.
32 devices in a mesh: img: 8 (over z, y), band: 4 (over x, core).
Axes of the slice: x: 2, y: 2, z: 4, core: 2. Of those that a mesh axis runs over, the one named last changes fastest.
Arguments:
- image_tokens: bfloat16 [16, 64, 64, 768], P('img', 'band'), may hold values from -6 to 6
- pad_offsets: int32 [16, 2], P('img'), may hold values from 0 to 6
- ln1_gain: bfloat16 [768], P('img'), may hold values from 0.099609375 to 1.8984375
- ln1_bias: bfloat16 [768], P('img'), may hold values from -1.5 to 1.5
- w_qkv: bfloat16 [768, 2304], P('band', 'img'), may hold values from -0.21875 to 0.21875
- q_bias: bfloat16 [768], P('img'), may hold values from -2.5 to 2.5
- v_bias: bfloat16 [768], P('img'), may hold values from -1.5 to 1.5
- rel_rows: bfloat16 [27, 64], P(None, 'band'), may hold values from -0.5 to 0.5
- rel_cols: bfloat16 [27, 64], P(None, 'band'), may hold values from -0.5 to 0.5
- w_proj: bfloat16 [768, 768], P('band', 'img'), may hold values from -1.25 to 1.25
- proj_bias: bfloat16 [768], P('img'), may hold values from -1.5 to 1.5
- ln2_gain: bfloat16 [768], P('img'), may hold values from 0.099609375 to 1.8984375
- ln2_bias: bfloat16 [768], P('img'), may hold values from -1.5 to 1.5
- w_fc1: bfloat16 [768, 3072], P('band', 'img'), may hold values from -0.21875 to 0.21875
- fc1_bias: bfloat16 [3072], P('img'), may hold values from -1.5 to 1.5
- w_fc2: bfloat16 [3072, 768], P('img', 'band'), may hold values from -0.21875 to 0.21875
- fc2_bias: bfloat16 [768], P('img'), may hold values from -1.5 to 1.5
- out_grad: bfloat16 [16, 64, 64, 768], P('img', 'band'), may hold values from -6 to 6
Outputs:
- output: bfloat16 [16, 64, 64, 768], P('img', 'band')
- input_grad: float32 [16, 64, 64, 768], P('img', 'band')
- d_ln1_gain: float32 [768], P('img')
- d_ln1_bias: float32 [768], P('img')
- d_w_qkv: float32 [768, 2304], P('band', 'img')
- d_q_bias: float32 [768], P('img')
- d_v_bias: float32 [768], P('img')
- d_rel_rows: float32 [27, 64], P(None, 'band')
- d_rel_cols: float32 [27, 64], P(None, 'band')
- d_w_proj: float32 [768, 768], P('band', 'img')
- d_proj_bias: float32 [768], P('img')
- d_ln2_gain: float32 [768], P('img')
- d_ln2_bias: float32 [768], P('img')
- d_w_fc1: float32 [768, 3072], P('band', 'img')
- d_fc1_bias: float32 [3072], P('img')
- d_w_fc2: float32 [3072, 768], P('img', 'band')
- d_fc2_bias: float32 [768], P('img')
Inputs may be any that keep to these rules, and one draw needn't show every extreme that they name: pad_offsets[b, 0] zero rows lie above image b and pad_offsets[b, 1] zero columns to its left in its 70 x 70 grid.
All inputs are finite; a program needn't handle non-finite values.
Results may differ from a plain program's by a relative error of at most 0.018.
Values may be sent and summed in bfloat16 or wider, within the bound.
A program may use at most 384 MiB of HBM per device.

v0:
```python
import jax
import jax.numpy as jnp
from jax import lax
from jax.sharding import PartitionSpec as P

D = 768
HEADS = 12
HEAD = 64
WIN = 14
SIDE = 64
GRID = 5
WINDOWS = 25
RELS = 27


EPSILON = 1e-06
HIGHEST_PRECISION = lax.Precision.HIGHEST


def normalize(values):
    average = jnp.mean(values, axis=-1, keepdims=True)
    centred = values - average
    inverse = lax.rsqrt(jnp.mean(centred * centred, axis=-1, keepdims=True) + EPSILON)
    return (centred * inverse, inverse)


def norm_backward(grad_normed, unit_rows, inverse, gain_row):
    scaled = grad_normed * gain_row
    first_mean = jnp.mean(scaled, axis=-1, keepdims=True)
    second_mean = jnp.mean(scaled * unit_rows, axis=-1, keepdims=True)
    return inverse * (scaled - first_mean - unit_rows * second_mean)


def exact_gelu(values):
    return jax.nn.gelu(values, approximate=False)


def offset_onehot():
    positions = jnp.arange(WIN, dtype=jnp.int32)
    offset_index = (positions[:, None] - positions[None, :] + (WIN - 1)).reshape(-1)
    return (offset_index[:, None] == jnp.arange(RELS, dtype=jnp.int32)[None, :]).astype(jnp.float32)


def widen_tables(rows_table, cols_table):
    rows_wide = jnp.broadcast_to(rows_table[:, None, :, None, :], (WIN, WIN, WIN, WIN, HEAD))
    cols_wide = jnp.broadcast_to(cols_table[None, :, None, :, :], (WIN, WIN, WIN, WIN, HEAD))
    return (
        rows_wide.reshape(WIN * WIN, WIN * WIN, HEAD),
        cols_wide.reshape(WIN * WIN, WIN * WIN, HEAD),
    )


def route_tables(image_ids, top_rows, band_index, band_count, band_rows):
    win_cap = (WINDOWS + band_count - 1) // band_count
    seg_cap = (GRID + band_count - 1) // band_count * band_rows
    piece_count = band_rows * GRID

    def per_image(image_id, top_row):
        order_index = jnp.arange(piece_count, dtype=jnp.int32)
        source_ids = jnp.arange(band_count, dtype=jnp.int32)
        real_rows = source_ids[:, None] * band_rows + (order_index // GRID)[None, :]
        window_index = (real_rows + top_row) // WIN * GRID + (order_index % GRID)[None, :]
        target_band = (image_id + window_index) % band_count
        hit_table = (target_band[:, :, None] == source_ids[None, None, :]).astype(jnp.int32)
        rank_table = jnp.sum(
            hit_table * (jnp.cumsum(hit_table, axis=1, dtype=jnp.int32) - 1), axis=2
        )
        own_source = source_ids == band_index
        send_slot = jnp.sum(
            jnp.where(own_source[:, None], target_band * seg_cap + rank_table, 0), axis=0
        )
        slot_index = jnp.arange(band_count * seg_cap, dtype=jnp.int32)
        send_table = slot_index[:, None] == send_slot[None, :]
        first_owned = (band_index - image_id) % band_count
        held_windows = first_owned + jnp.arange(win_cap, dtype=jnp.int32) * band_count
        inner_rows = jnp.arange(WIN, dtype=jnp.int32)
        padded_rows = (held_windows // GRID * WIN)[:, None] + inner_rows[None, :]
        image_rows = padded_rows - top_row
        is_valid = (held_windows < WINDOWS)[:, None] & (image_rows >= 0) & (image_rows < SIDE)
        clipped_rows = jnp.clip(image_rows, 0, SIDE - 1)
        source_band = clipped_rows // band_rows
        piece_index = clipped_rows % band_rows * GRID + (held_windows % GRID)[:, None]
        lookup_key = (source_band * piece_count + piece_index).reshape(-1)
        key_range = jnp.arange(band_count * piece_count, dtype=jnp.int32)
        found_rank = jnp.sum(
            jnp.where(
                lookup_key[:, None] == key_range[None, :], rank_table.reshape(-1)[None, :], 0
            ),
            axis=1,
        )
        take_slot = source_band.reshape(-1) * seg_cap + found_rank
        take_table = (slot_index[None, :] == take_slot[:, None]) & is_valid.reshape(-1)[:, None]
        return (send_table.astype(jnp.bfloat16), take_table.astype(jnp.bfloat16))

    return jax.vmap(per_image)(image_ids, top_rows)


def to_pieces(band_tokens, left_cols):

    def place(image_rows, left_col):
        canvas = jnp.zeros((image_rows.shape[0], GRID * WIN, image_rows.shape[2]), image_rows.dtype)
        return lax.dynamic_update_slice(canvas, image_rows, (jnp.int32(0), left_col, jnp.int32(0)))

    wide_rows = jax.vmap(place)(band_tokens, left_cols)
    return wide_rows.reshape(
        band_tokens.shape[0], band_tokens.shape[1] * GRID, WIN * band_tokens.shape[3]
    )


def from_pieces(piece_rows, left_cols, band_rows):
    wide_rows = piece_rows.reshape(piece_rows.shape[0], band_rows, GRID * WIN, D)

    def crop(image_rows, left_col):
        return lax.dynamic_slice(
            image_rows, (jnp.int32(0), left_col, jnp.int32(0)), (band_rows, SIDE, D)
        )

    return jax.vmap(crop)(wide_rows, left_cols)


def pack_pieces(send_table, piece_rows, band_count):
    packed = jnp.einsum(
        "bjs,bsf->bjf", send_table, piece_rows, preferred_element_type=jnp.float32
    ).astype(jnp.bfloat16)
    return packed.reshape(packed.shape[0], band_count, -1, packed.shape[2])


def unpack_windows(take_table, received):
    flat_rows = received.reshape(received.shape[0], -1, received.shape[3])
    return jnp.einsum(
        "bqj,bjf->bqf", take_table, flat_rows, preferred_element_type=jnp.float32
    ).astype(jnp.bfloat16)


def pack_windows(take_table, window_rows, band_count):
    packed = jnp.einsum(
        "bqj,bqf->bjf", take_table, window_rows, preferred_element_type=jnp.float32
    ).astype(jnp.bfloat16)
    return packed.reshape(packed.shape[0], band_count, -1, packed.shape[2])


def unpack_pieces(send_table, received):
    flat_rows = received.reshape(received.shape[0], -1, received.shape[3])
    return jnp.einsum(
        "bjs,bjf->bsf", send_table, flat_rows, preferred_element_type=jnp.float32
    ).astype(jnp.bfloat16)


def scores_of(flat_queries, key_rows, rows_wide, cols_wide):
    direct = jnp.einsum(
        "nqhc,nkhc->nhqk", flat_queries, key_rows, preferred_element_type=jnp.float32
    ) * HEAD ** (-0.5)
    along_rows = jnp.einsum(
        "nqhc,qkc->nhqk", flat_queries, rows_wide, preferred_element_type=jnp.float32
    )
    along_cols = jnp.einsum(
        "nqhc,qkc->nhqk", flat_queries, cols_wide, preferred_element_type=jnp.float32
    )
    return direct + along_rows + along_cols


def shards(
    image_tokens,
    pad_offsets,
    ln1_gain,
    ln1_bias,
    w_qkv,
    q_bias,
    v_bias,
    rel_rows,
    rel_cols,
    w_proj,
    proj_bias,
    ln2_gain,
    ln2_bias,
    w_fc1,
    fc1_bias,
    w_fc2,
    fc2_bias,
    out_grad,
):
    band_part = (
        lax.all_gather(w_qkv, "band", axis=0, tiled=True),
        lax.all_gather(w_proj, "band", axis=0, tiled=True),
        lax.all_gather(w_fc1, "band", axis=0, tiled=True),
        lax.all_gather(w_fc2, "band", axis=1, tiled=True),
        lax.all_gather(rel_rows, "band", axis=1, tiled=True),
        lax.all_gather(rel_cols, "band", axis=1, tiled=True),
    )
    (
        qkv_full,
        proj_full,
        fc1_full,
        fc2_full,
        gain_one,
        shift_one,
        query_bias,
        value_bias,
        proj_shift,
        gain_two,
        shift_two,
        fc1_shift,
        fc2_shift,
    ) = (
        lax.all_gather(band_part[0], "img", axis=1, tiled=True),
        lax.all_gather(band_part[1], "img", axis=1, tiled=True),
        lax.all_gather(band_part[2], "img", axis=1, tiled=True),
        lax.all_gather(band_part[3], "img", axis=0, tiled=True),
        lax.all_gather(ln1_gain, "img", axis=0, tiled=True),
        lax.all_gather(ln1_bias, "img", axis=0, tiled=True),
        lax.all_gather(q_bias, "img", axis=0, tiled=True),
        lax.all_gather(v_bias, "img", axis=0, tiled=True),
        lax.all_gather(proj_bias, "img", axis=0, tiled=True),
        lax.all_gather(ln2_gain, "img", axis=0, tiled=True),
        lax.all_gather(ln2_bias, "img", axis=0, tiled=True),
        lax.all_gather(fc1_bias, "img", axis=0, tiled=True),
        lax.all_gather(fc2_bias, "img", axis=0, tiled=True),
    )
    rows_full = band_part[4]
    cols_full = band_part[5]
    img_dev = image_tokens.shape[0]
    band_rows = image_tokens.shape[1]
    band_count = lax.axis_size("band")
    band_index = lax.axis_index("band")
    image_ids = lax.axis_index("img") * img_dev + jnp.arange(img_dev, dtype=jnp.int32)
    top_rows = pad_offsets[:, 0]
    left_cols = pad_offsets[:, 1]
    send_table, take_table = route_tables(image_ids, top_rows, band_index, band_count, band_rows)
    token_count = img_dev * band_rows * SIDE
    tokens = image_tokens.astype(jnp.float32).reshape(token_count, D)
    unit_one, inverse_one = normalize(tokens)
    gain_one_wide = gain_one.astype(jnp.float32)
    normed_one = (unit_one * gain_one_wide + shift_one.astype(jnp.float32)).astype(jnp.bfloat16)
    outgoing = pack_pieces(
        send_table,
        to_pieces(normed_one.reshape(img_dev, band_rows, SIDE, D), left_cols),
        band_count,
    )
    incoming = lax.all_to_all(outgoing, "band", split_axis=1, concat_axis=1, tiled=True)
    window_tokens = unpack_windows(take_table, incoming).reshape(-1, D)
    window_count = window_tokens.shape[0] // (WIN * WIN)
    bias_row = jnp.concatenate([query_bias, jnp.zeros_like(query_bias), value_bias]).astype(
        jnp.float32
    )
    projected = (
        jnp.dot(window_tokens, qkv_full, preferred_element_type=jnp.float32) + bias_row
    ).astype(jnp.bfloat16)
    flat_queries = projected[:, :D].reshape(window_count, WIN * WIN, HEADS, HEAD)
    key_rows = projected[:, D : 2 * D].reshape(window_count, WIN * WIN, HEADS, HEAD)
    values = projected[:, 2 * D :].reshape(window_count, WIN * WIN, HEADS, HEAD)
    offsets = offset_onehot()
    rows_table = (
        jnp.dot(offsets, rows_full.astype(jnp.float32), precision=HIGHEST_PRECISION)
        .reshape(WIN, WIN, HEAD)
        .astype(jnp.bfloat16)
    )
    cols_table = (
        jnp.dot(offsets, cols_full.astype(jnp.float32), precision=HIGHEST_PRECISION)
        .reshape(WIN, WIN, HEAD)
        .astype(jnp.bfloat16)
    )
    rows_wide, cols_wide = widen_tables(rows_table, cols_table)
    scores = scores_of(flat_queries, key_rows, rows_wide, cols_wide)
    row_peak = jnp.max(scores, axis=-1, keepdims=True)
    log_total = row_peak + jnp.log(jnp.sum(jnp.exp(scores - row_peak), axis=-1, keepdims=True))
    attention_low = jnp.exp(scores - log_total).astype(jnp.bfloat16)
    attended_windows = jnp.einsum(
        "nhqk,nkhc->nqhc", attention_low, values, preferred_element_type=jnp.float32
    ).astype(jnp.bfloat16)
    returning = pack_windows(take_table, attended_windows.reshape(img_dev, -1, WIN * D), band_count)
    arrived = lax.all_to_all(returning, "band", split_axis=1, concat_axis=1, tiled=True)
    attended = from_pieces(unpack_pieces(send_table, arrived), left_cols, band_rows).reshape(
        token_count, D
    )
    mixed_rows = jnp.dot(
        attended, proj_full, preferred_element_type=jnp.float32
    ) + proj_shift.astype(jnp.float32)
    hidden = tokens + mixed_rows
    unit_two, inverse_two = normalize(hidden)
    gain_two_wide = gain_two.astype(jnp.float32)
    normed_two = (unit_two * gain_two_wide + shift_two.astype(jnp.float32)).astype(jnp.bfloat16)
    pre_act = jnp.dot(normed_two, fc1_full, preferred_element_type=jnp.float32) + fc1_shift.astype(
        jnp.float32
    )
    activated, gelu_pull = jax.vjp(exact_gelu, pre_act)
    act_low = activated.astype(jnp.bfloat16)
    output = (
        hidden
        + jnp.dot(act_low, fc2_full, preferred_element_type=jnp.float32)
        + fc2_shift.astype(jnp.float32)
    ).astype(jnp.bfloat16)
    again_band = (
        lax.all_gather(w_qkv, "band", axis=0, tiled=True),
        lax.all_gather(w_proj, "band", axis=0, tiled=True),
        lax.all_gather(w_fc1, "band", axis=0, tiled=True),
        lax.all_gather(w_fc2, "band", axis=1, tiled=True),
    )
    qkv_back, proj_back, fc1_back, fc2_back = (
        lax.all_gather(again_band[0], "img", axis=1, tiled=True),
        lax.all_gather(again_band[1], "img", axis=1, tiled=True),
        lax.all_gather(again_band[2], "img", axis=1, tiled=True),
        lax.all_gather(again_band[3], "img", axis=0, tiled=True),
    )
    cotangent = out_grad.reshape(token_count, D)
    grad_fc2 = jnp.einsum("tf,td->fd", act_low, cotangent, preferred_element_type=jnp.float32)
    grad_fc2_bias = jnp.sum(cotangent.astype(jnp.float32), axis=0)
    grad_act = jnp.einsum("td,fd->tf", cotangent, fc2_back, preferred_element_type=jnp.float32)
    grad_pre = gelu_pull(grad_act)[0].astype(jnp.bfloat16)
    grad_fc1 = jnp.einsum("td,tf->df", normed_two, grad_pre, preferred_element_type=jnp.float32)
    grad_fc1_bias = jnp.sum(grad_pre.astype(jnp.float32), axis=0)
    grad_normed_two = jnp.einsum(
        "tf,df->td", grad_pre, fc1_back, preferred_element_type=jnp.float32
    )
    grad_gain_two = jnp.sum(grad_normed_two * unit_two, axis=0)
    grad_shift_two = jnp.sum(grad_normed_two, axis=0)
    grad_hidden = cotangent.astype(jnp.float32) + norm_backward(
        grad_normed_two, unit_two, inverse_two, gain_two_wide
    )
    grad_mixed = grad_hidden.astype(jnp.bfloat16)
    grad_proj = jnp.einsum("td,te->de", attended, grad_mixed, preferred_element_type=jnp.float32)
    grad_proj_bias = jnp.sum(grad_mixed.astype(jnp.float32), axis=0)
    grad_attended = jnp.einsum(
        "te,de->td", grad_mixed, proj_back, preferred_element_type=jnp.float32
    ).astype(jnp.bfloat16)
    grad_going = pack_pieces(
        send_table,
        to_pieces(grad_attended.reshape(img_dev, band_rows, SIDE, D), left_cols),
        band_count,
    )
    grad_coming = lax.all_to_all(grad_going, "band", split_axis=1, concat_axis=1, tiled=True)
    grad_windows = unpack_windows(take_table, grad_coming).reshape(
        window_count, WIN * WIN, HEADS, HEAD
    )
    scores_again = scores_of(flat_queries, key_rows, rows_wide, cols_wide)
    weights_again = jnp.exp(scores_again - log_total)
    grad_values = jnp.einsum(
        "nhqk,nqhc->nkhc",
        weights_again.astype(jnp.bfloat16),
        grad_windows,
        preferred_element_type=jnp.float32,
    ).astype(jnp.bfloat16)
    grad_probs = jnp.einsum(
        "nqhc,nkhc->nhqk", grad_windows, values, preferred_element_type=jnp.float32
    )
    centre = jnp.sum(grad_probs * weights_again, axis=-1, keepdims=True)
    grad_scores = (weights_again * (grad_probs - centre)).astype(jnp.bfloat16)
    grad_queries = jnp.einsum(
        "nhqk,nkhc->nqhc", grad_scores, key_rows, preferred_element_type=jnp.float32
    ) * HEAD ** (-0.5)
    grad_queries = grad_queries + jnp.einsum(
        "nhqk,qkc->nqhc", grad_scores, rows_wide, preferred_element_type=jnp.float32
    )
    grad_queries = grad_queries + jnp.einsum(
        "nhqk,qkc->nqhc", grad_scores, cols_wide, preferred_element_type=jnp.float32
    )
    grad_keys = (
        jnp.einsum("nhqk,nqhc->nkhc", grad_scores, flat_queries, preferred_element_type=jnp.float32)
        * HEAD ** (-0.5)
    ).astype(jnp.bfloat16)
    grad_wide = jnp.einsum(
        "nhqk,nqhc->qkc", grad_scores, flat_queries, preferred_element_type=jnp.float32
    )
    grad_grid = grad_wide.reshape(WIN, WIN, WIN, WIN, HEAD)
    grad_rows_grid = jnp.sum(grad_grid, axis=(1, 3))
    grad_cols_grid = jnp.sum(grad_grid, axis=(0, 2))
    grad_rel_rows = jnp.dot(
        offsets.T, grad_rows_grid.reshape(WIN * WIN, HEAD), precision=HIGHEST_PRECISION
    )
    grad_rel_cols = jnp.dot(
        offsets.T, grad_cols_grid.reshape(WIN * WIN, HEAD), precision=HIGHEST_PRECISION
    )
    grad_projected = jnp.concatenate(
        [
            grad_queries.reshape(-1, D).astype(jnp.bfloat16),
            grad_keys.reshape(-1, D),
            grad_values.reshape(-1, D),
        ],
        axis=1,
    )
    grad_qkv = jnp.einsum(
        "td,te->de", window_tokens, grad_projected, preferred_element_type=jnp.float32
    )
    grad_query_bias = jnp.sum(grad_projected[:, :D].astype(jnp.float32), axis=0)
    grad_value_bias = jnp.sum(grad_projected[:, 2 * D :].astype(jnp.float32), axis=0)
    grad_window_tokens = jnp.einsum(
        "te,de->td", grad_projected, qkv_back, preferred_element_type=jnp.float32
    ).astype(jnp.bfloat16)
    grad_return = pack_windows(
        take_table, grad_window_tokens.reshape(img_dev, -1, WIN * D), band_count
    )
    grad_home = lax.all_to_all(grad_return, "band", split_axis=1, concat_axis=1, tiled=True)
    grad_normed_one = (
        from_pieces(unpack_pieces(send_table, grad_home), left_cols, band_rows)
        .reshape(token_count, D)
        .astype(jnp.float32)
    )
    grad_gain_one = jnp.sum(grad_normed_one * unit_one, axis=0)
    grad_shift_one = jnp.sum(grad_normed_one, axis=0)
    input_grad = grad_hidden + norm_backward(grad_normed_one, unit_one, inverse_one, gain_one_wide)
    summed_img = (
        lax.psum_scatter(
            grad_qkv.astype(jnp.bfloat16), "img", scatter_dimension=1, tiled=True
        ).astype(jnp.float32),
        lax.psum_scatter(
            grad_proj.astype(jnp.bfloat16), "img", scatter_dimension=1, tiled=True
        ).astype(jnp.float32),
        lax.psum_scatter(
            grad_fc1.astype(jnp.bfloat16), "img", scatter_dimension=1, tiled=True
        ).astype(jnp.float32),
        lax.psum_scatter(
            grad_fc2.astype(jnp.bfloat16), "img", scatter_dimension=0, tiled=True
        ).astype(jnp.float32),
    )
    summed = (
        lax.psum_scatter(
            summed_img[0].astype(jnp.bfloat16), "band", scatter_dimension=0, tiled=True
        ).astype(jnp.float32),
        lax.psum_scatter(
            summed_img[1].astype(jnp.bfloat16), "band", scatter_dimension=0, tiled=True
        ).astype(jnp.float32),
        lax.psum_scatter(
            summed_img[2].astype(jnp.bfloat16), "band", scatter_dimension=0, tiled=True
        ).astype(jnp.float32),
        lax.psum_scatter(
            summed_img[3].astype(jnp.bfloat16), "band", scatter_dimension=1, tiled=True
        ).astype(jnp.float32),
    )
    small_sums = lax.psum(
        (
            grad_gain_one,
            grad_shift_one,
            grad_query_bias,
            grad_value_bias,
            grad_rel_rows,
            grad_rel_cols,
            grad_proj_bias,
            grad_gain_two,
            grad_shift_two,
            grad_fc1_bias,
            grad_fc2_bias,
        ),
        ("img", "band"),
    )
    img_count = lax.axis_size("img")
    img_index = lax.axis_index("img")

    def img_share(vector):
        share_len = vector.shape[0] // img_count
        return lax.dynamic_slice_in_dim(vector, img_index * share_len, share_len, 0)

    def band_share(table):
        share_len = table.shape[1] // band_count
        return lax.dynamic_slice_in_dim(table, band_index * share_len, share_len, 1)

    return (
        output.reshape(img_dev, band_rows, SIDE, D),
        input_grad.reshape(img_dev, band_rows, SIDE, D),
        img_share(small_sums[0]),
        img_share(small_sums[1]),
        summed[0],
        img_share(small_sums[2]),
        img_share(small_sums[3]),
        band_share(small_sums[4]),
        band_share(small_sums[5]),
        summed[1],
        img_share(small_sums[6]),
        img_share(small_sums[7]),
        img_share(small_sums[8]),
        summed[2],
        img_share(small_sums[9]),
        summed[3],
        img_share(small_sums[10]),
    )


def solution(mesh):
    return jax.shard_map(
        shards,
        mesh=mesh,
        in_specs=(
            P("img", "band", None, None),
            P("img", None),
            P("img"),
            P("img"),
            P("band", "img"),
            P("img"),
            P("img"),
            P(None, "band"),
            P(None, "band"),
            P("band", "img"),
            P("img"),
            P("img"),
            P("img"),
            P("band", "img"),
            P("img"),
            P("img", "band"),
            P("img"),
            P("img", "band", None, None),
        ),
        out_specs=(
            P("img", "band", None, None),
            P("img", "band", None, None),
            P("img"),
            P("img"),
            P("band", "img"),
            P("img"),
            P("img"),
            P(None, "band"),
            P(None, "band"),
            P("band", "img"),
            P("img"),
            P("img"),
            P("img"),
            P("band", "img"),
            P("img"),
            P("img", "band"),
            P("img"),
        ),
        check_vma=False,
    )
```

profile of v0, /device:TPU:0, one launch (start us, length us, event | category | flops | bytes accessed | tf_op | source)
XLA Modules:
  0.0 1666.7 jit_solution(15445600881858257819)
XLA Ops:
  28.7 38.8 %all-reduce.9 = (bf16[768]{0:T(1024)(128)(2,1)S(1)}, bf16[768]{0:T(1024)(128)(2,1)S(1)}, bf16[768]{0:T(1024)(128)(2,1)S(1)}, bf16[768]{0:T(1024)(128)(2,1)S(1)},...) all-reduce(bf16[768]{0:T(1024)(128)(2,1)S(1)} %dynamic-update-slice, ...), channel_id=1, replica_groups=mesh['img'=8,'band'=4] {'img'}, use_global_device_ids=true, to_apply=%add.1 | all-reduce | flops 6144 | bytes 24576
  80.4 42.5 %while.2 = (s32[]{:T(128)}, bf16[2,16,70,768]{3,2,1,0:T(8,128)(2,1)}, s32[2,4]{1,0:T(2,128)S(1)}, bf16[2,16,64,768]{3,1,2,0:T(8,128)(2,1)}, s32[]{:T(128)}, /*index=5*/s32[4]{0:T(128)S(1)}, s32[]{:T(128)}) while((s32[]{:T(128)}, bf16[2,16,70,768]{3,2,1,0:T(8,128)(2,1)}, s32[2,4]{1,0:T(2,128)S(1)}, bf16[2,16,64,768]{3,1,2,0:T(8,128)(2,1)}, s32[]{:T(128)}, ...), condition=%wide.while_cond, body=%wide.while_body.sunk | while | flops 786461 | bytes 11010243 | solution.py:102
  142.9 64.0 %all_gather.73 = bf16[768,96]{1,0:T(8,128)(2,1)S(1)} all-gather(bf16[192,96]{1,0:T(8,128)(2,1)S(1)} %copy-done.36), channel_id=1, replica_groups=mesh['img'=8,'band'=4] {'band'}, dimensions={0}, use_global_device_ids=true | all-gather | bytes 184320 | tf_op jit(solution)/shard_map/all_gather | solution.py:184
  317.0 19.2 %reshape.664 = bf16[14,196,12,64]{1,0,3,2:T(8,128)(2,1)} reshape(bf16[2744,768]{0,1:T(8,128)(2,1)} %copy.379) | data formatting | bytes 8429568 | tf_op jit(solution)/shard_map/reshape | solution.py:248
  354.1 19.5 %fusion.14 = f32[196,196,14,12]{1,2,3,0:T(8,128)} fusion(bf16[14,196,12,64]{3,0,2,1:T(8,128)(2,1)} %copy.385, bf16[196,196,64]{2,1,0:T(8,128)(2,1)} %reshape.666), kind=kOutput, calls=%fused_computation.55 | convolution fusion | flops 826097664 | bytes 34947584 | tf_op jit(solution)/shard_map/nqhc,qkc->nhqk/dot_general | solution.py:153
  373.7 44.4 %copy.386 = f32[196,196,14,12]{0,1,3,2:T(8,128)} copy(f32[196,196,14,12]{1,2,3,0:T(8,128)} %fusion.14) | data formatting | bytes 51631104 | tf_op jit(solution)/shard_map/nqhc,qkc->nhqk/dot_general | solution.py:153
  418.0 19.7 %fusion.10 = f32[196,196,14,12]{1,2,3,0:T(8,128)} fusion(bf16[14,196,12,64]{3,0,2,1:T(8,128)(2,1)} %copy.385, bf16[196,196,64]{2,1,0:T(8,128)(2,1)} %reshape.667), kind=kOutput, calls=%fused_computation.51 | convolution fusion | flops 826097664 | bytes 34947584 | tf_op jit(solution)/shard_map/nqhc,qkc->nhqk/dot_general | solution.py:156
  437.8 44.3 %copy.390 = f32[196,196,14,12]{0,1,3,2:T(8,128)} copy(f32[196,196,14,12]{1,2,3,0:T(8,128)} %fusion.10) | data formatting | bytes 51631104 | tf_op jit(solution)/shard_map/nqhc,qkc->nhqk/dot_general | solution.py:156
  537.6 38.8 %fusion.83 = (f32[14,12,196]{2,1,0:T(8,128)S(1)}, f32[14,12,196,196]{2,3,1,0:T(8,128)}) fusion(f32[196,196,14,12]{0,1,3,2:T(8,128)} %copy.390, f32[196,196,14,12]{0,1,3,2:T(8,128)} %copy.386, bf16[14,196,12,64]{1,3,2,0:T(8,128)(2,1)} %copy.382, bf16[14,196,12,64]{1,0,3,2:T(8,128)(2,1)} %reshape.664), kind=kOutput, calls=%fused_computation.208 | convolution fusion | flops 851880320 | bytes 86007936 | tf_op jit(solution)/shard_map/nqhc,nkhc->nhqk/dot_general | solution.py:150
  653.3 66.6 %all_gather.81 = bf16[384,768]{0,1:T(8,128)(2,1)} all-gather(bf16[384,192]{0,1:T(8,128)(2,1)S(1)} %copy-done.21), channel_id=1, replica_groups=mesh['img'=8,'band'=4] {'band'}, dimensions={1}, use_global_device_ids=true | all-gather | bytes 737280 | tf_op jit(solution)/shard_map/all_gather | solution.py:186
  728.2 26.1 %all-gather = bf16[8,1,384]{2,1,0:T(2,128)(2,1)S(1)} all-gather(bf16[1,1,384]{2,1,0:T(2,128)(2,1)S(1)} %reshape.797), channel_id=1, replica_groups=mesh['img'=8,'band'=4] {'img'}, dimensions={0}, use_global_device_ids=true | all-gather | bytes 6912 | tf_op jit(solution)/shard_map/all_gather | solution.py:216
  786.1 70.6 %multiply_convert_fusion.1 = (bf16[2048,3072]{1,0:T(8,128)(2,1)}, f32[2048,3072]{1,0:T(8,128)}, f32[2048,3072]{1,0:T(8,128)}) fusion(f32[3072]{0:T(1024)S(1)} %bitcast.195, bf16[768,3072]{1,0:T(8,128)(2,1)} %all-gather.10.cloned.1.call-done, f32[2048,768]{1,0:T(8,128)} %copy-done.3, f32[768]{0:T(1024)S(1)} %convert_element_type.228, ...), kind=kOutput, calls=%fused_computation.21 | convolution fusion | flops 10086776832 | bytes 73959424 | tf_op jit(solution)/shard_map/dot_general | solution.py:282
  856.7 28.5 %convert_reduce_fusion = (f32[3072]{0:T(1024)}, bf16[2048,3072]{1,0:T(8,128)(2,1)}) fusion(f32[2048,3072]{1,0:T(8,128)} %get-tuple-element.230, bf16[2048,768]{1,0:T(8,128)(2,1)S(1)} %bitcast.185, bf16[3072,768]{0,1:T(8,128)(2,1)} %all-gather.12.cloned.1.call-done, f32[2048,3072]{1,0:T(8,128)} %get-tuple-element.251, f32[3072]{0:T(1024)S(1)} %bitcast.196), kind=kOutput, calls=%fused_computation.19 | convolution fusion | flops 9770628096 | bytes 70803456 | tf_op jit(solution)/shard_map/td,fd->tf/dot_general | solution.py:307
  885.2 20.0 %multiply_reduce_fusion.1 = (f32[768]{0:T(1024)}, f32[2048]{0:T(1024)S(1)}, f32[2048]{0:T(1024)S(1)}, f32[768]{0:T(1024)}, f32[2048,768]{1,0:T(8,128)}) fusion(f32[2048,768]{1,0:T(8,128)} %copy-done.3, f32[2048]{0:T(1024)S(1)} %add_rsqrt_fusion.1, f32[2048]{0:T(1024)S(1)} %broadcast_multiply_fusion.5, f32[768]{0:T(1024)S(1)} %convert_element_type.227, ...), kind=kOutput, calls=%fused_computation.68 | convolution fusion | flops 9677826048 | bytes 29926400 | tf_op jit(solution)/shard_map/tf,df->td/dot_general | solution.py:311
  917.6 60.3 %reduce-scatter.19.cloned.1.call-done = bf16[768,96]{0,1:T(8,128)(2,1)} async-done(((bf16[768,768]{0,1:T(8,128)(2,1)}), bf16[768,96]{0,1:T(8,128)(2,1)}) %reduce-scatter.19.cloned.1.call-update) | async-done | bytes 147472 | tf_op jit(solution)/shard_map/reduce_scatter | solution.py:404
  1006.3 40.2 %while.3 = (s32[]{:T(128)}, bf16[2,16,70,768]{3,2,1,0:T(8,128)(2,1)}, s32[2,4]{1,0:T(2,128)S(1)}, bf16[2,16,64,768]{3,2,1,0:T(8,128)(2,1)}, s32[]{:T(128)}, /*index=5*/s32[4]{0:T(128)S(1)}, s32[]{:T(128)}) while((s32[]{:T(128)}, bf16[2,16,70,768]{3,2,1,0:T(8,128)(2,1)}, s32[2,4]{1,0:T(2,128)S(1)}, bf16[2,16,64,768]{3,2,1,0:T(8,128)(2,1)}, ...), condition=%wide.while_cond.1, body=%wide.while_body.1.sunk | while | flops 786461 | bytes 7864515 | solution.py:102
  1105.4 18.9 %all-to-all-done.2 = bf16[2,4,32,10752]{3,2,0,1:T(8,128)(2,1)} async-done(((bf16[2,4,32,10752]{3,2,0,1:T(8,128)(2,1)}), bf16[2,4,32,10752]{3,2,0,1:T(8,128)(2,1)}, u32[]{:S(2)}, u32[]{:S(2)}) %all-to-all-start.2) | async-done | bytes 5505056 | tf_op jit(solution)/shard_map/all_to_all | solution.py:330
  1162.1 29.9 %multiply_reduce_fusion = (f32[14,12,196]{2,1,0:T(8,128)S(1)}, f32[14,12,196,196]{2,3,1,0:T(8,128)}) fusion(f32[14,12,196,196]{2,3,1,0:T(8,128)} %get-tuple-element.248, f32[14,12,196]{2,1,0:T(8,128)S(1)} %copy-done.9, bf16[14,196,12,64]{1,3,2,0:T(8,128)(2,1)} %copy.401, bf16[14,196,12,64]{1,3,2,0:T(8,128)(2,1)} %copy.391), kind=kOutput, calls=%fused_computation.13 | convolution fusion | flops 845426432 | bytes 60324096 | tf_op jit(solution)/shard_map/nqhc,nkhc->nhqk/dot_general | solution.py:342
  1192.1 29.2 %multiply_convert_fusion = bf16[14,12,196,196]{2,3,1,0:T(8,128)(2,1)} fusion(f32[14,12,196,196]{2,3,1,0:T(8,128)} %get-tuple-element.254, f32[14,12,196,196]{2,3,1,0:T(8,128)} %get-tuple-element.248, f32[14,12,196]{2,1,0:T(8,128)S(1)} %get-tuple-element.253, f32[14,12,196]{2,1,0:T(8,128)S(1)} %copy-done.9), kind=kLoop, calls=%fused_computation.12 | loop fusion | flops 25815552 | bytes 64802304 | tf_op jit(solution)/shard_map/convert_element_type | solution.py:346
  1221.2 30.1 %copy.406 = bf16[14,12,196,196]{3,0,1,2:T(8,128)(2,1)} copy(bf16[14,12,196,196]{2,3,1,0:T(8,128)(2,1)} %multiply_convert_fusion) | data formatting | bytes 25815552 | tf_op jit(solution)/shard_map/convert_element_type | solution.py:346
  1357.7 19.0 %convert_reduce_fusion.2 = (f32[12,64]{1,0:T(8,128)S(1)}, bf16[14,196,12,64]{1,3,2,0:T(8,128)(2,1)}) fusion(f32[196,64,14,12]{0,1,3,2:T(8,128)} %copy.410, f32[196,64,14,12]{0,1,3,2:T(8,128)} %copy.407, bf16[14,196,12,64]{1,3,2,0:T(8,128)(2,1)} %copy.382, bf16[14,12,196,196]{2,3,1,0:T(8,128)(2,1)} %multiply_convert_fusion), kind=kOutput, calls=%fused_computation.47 | convolution fusion | flops 838741248 | bytes 38199552 | tf_op jit(solution)/shard_map/nhqk,nkhc->nqhc/dot_general | solution.py:347
  1489.9 20.2 %convolution_bitcast_fusion = f32[196,196,64]{2,1,0:T(8,128)} fusion(bf16[14,12,196,196]{3,0,1,2:T(8,128)(2,1)} %copy.406, bf16[14,196,12,64]{3,0,2,1:T(8,128)(2,1)} %copy.385), kind=kOutput, calls=%fused_computation.57 | convolution fusion | flops 826097664 | bytes 26957056 | tf_op jit(solution)/shard_map/nhqk,nqhc->qkc/dot_general | solution.py:360
  1510.1 22.1 %reshape.687 = f32[14,14,14,14,64]{4,3,2,1,0:T(8,128)} reshape(f32[196,196,64]{2,1,0:T(8,128)} %convolution_bitcast_fusion) | data formatting | bytes 19668992 | tf_op jit(solution)/shard_map/reshape | solution.py:363
  1585.5 41.3 %all-reduce.8 = (f32[768]{0:T(1024)S(1)}, f32[768]{0:T(1024)S(1)}, f32[768]{0:T(1024)S(1)}, f32[768]{0:T(1024)S(1)}, f32[27,64]{0,1:T(8,128)S(1)}, /*index=5*/f3...) all-reduce(f32[768]{0:T(1024)S(1)} %get-tuple-element.184, ...), channel_id=1, replica_groups=mesh['img'=8,'band'=4] {'img','band'}, use_global_device_ids=true, to_apply=%region_18.19 | all-reduce | flops 12672 | bytes 101376 | tf_op jit(solution)/shard_map/psum | solution.py:428
  (408 shorter events, 879.1 us)
Async XLA Ops:
  7.2 67.7 %copy-start.64 = (s32[3]{0:T(128)S(1)}, s32[3]{0:T(128)}, u32[]{:S(2)}) copy-start(s32[3]{0:T(128)} %constant.100.clone.1) | copy-start | bytes 40
  7.2 64.7 %copy-start = (bf16[2,16,64,768]{3,2,1,0:T(8,128)(2,1)S(1)}, bf16[2,16,64,768]{3,2,1,0:T(8,128)(2,1)}, u32[]{:S(2)}) copy-start(bf16[2,16,64,768]{3,2,1,0:T(8,128)(2,1)} %param.18) | copy-start | bytes 9437188
  7.2 66.9 %copy-start.56 = (s32[2,2]{1,0:T(2,128)S(1)}, s32[2,2]{1,0:T(2,128)}, u32[]{:S(2)}) copy-start(s32[2,2]{1,0:T(2,128)} %param.19) | copy-start | bytes 52
  7.2 285.1 %all-gather.6.cloned.1.call-start = ((), (), s32[]{:S(2)}) async-start(), calls=%async_computation.12 | async-start | bytes 3981312 | tf_op jit(solution)/shard_map/all_gather | solution.py:205
  137.6 70.2 %copy-start.20 = (bf16[192,384]{1,0:T(8,128)(2,1)S(1)}, bf16[192,384]{1,0:T(8,128)(2,1)}, u32[]{:S(2)}) copy-start(bf16[192,384]{1,0:T(8,128)(2,1)} %param.31) | copy-start | bytes 442372
  137.6 81.8 %copy-start.54 = (bf16[27,16]{0,1:T(8,128)(2,1)S(1)}, bf16[27,16]{0,1:T(8,128)(2,1)}, u32[]{:S(2)}) copy-start(bf16[27,16]{0,1:T(8,128)(2,1)} %param.25) | copy-start | bytes 2596
  137.6 137.4 %all-to-all-start = ((bf16[2,4,32,10752]{3,2,0,1:T(8,128)(2,1)}), bf16[2,4,32,10752]{3,2,0,1:T(8,128)(2,1)}, u32[]{:S(2)}, u32[]{:S(2)}) async-start(bf16[2,4,32,10752]{3,2,0,1:T(8,128)(2,1)} %copy.375), calls=%async_computation | async-start | bytes 11010048 | tf_op jit(solution)/shard_map/all_to_all | solution.py:239
  142.8 632.7 %all-gather.8.cloned.1.call-start = ((), (), s32[]{:S(2)}) async-start(), calls=%async_computation.13 | async-start | bytes 1327104 | tf_op jit(solution)/shard_map/all_gather | solution.py:206
  207.7 578.4 %all-gather.10.cloned.1.call-start = ((), (), s32[]{:S(2)}) async-start(), calls=%async_computation.14 | async-start | bytes 5308416 | tf_op jit(solution)/shard_map/all_gather | solution.py:207
  647.8 72.1 %copy-start.60 = (bf16[768]{0:T(1024)(128)(2,1)S(1)}, bf16[768]{0:T(1024)(128)(2,1)}, u32[]{:S(2)}) copy-start(bf16[768]{0:T(1024)(128)(2,1)} %get-tuple-element.223) | copy-start | bytes 4612
  647.8 72.2 %copy-start.1 = (bf16[2,16,64,768]{3,2,1,0:T(8,128)(2,1)S(1)}, bf16[2,16,64,768]{3,2,1,0:T(8,128)(2,1)}, u32[]{:S(2)}) copy-start(bf16[2,16,64,768]{3,2,1,0:T(8,128)(2,1)} %param.18) | copy-start | bytes 9437188
  647.8 107.1 %all-to-all-start.1 = ((bf16[2,4,32,10752]{3,2,0,1:T(8,128)(2,1)}), bf16[2,4,32,10752]{3,2,0,1:T(8,128)(2,1)}, u32[]{:S(2)}, u32[]{:S(2)}) async-start(bf16[2,4,32,10752]{3,2,0,1:T(8,128)(2,1)} %copy.394), calls=%async_computation.1 | async-start | bytes 11010048 | tf_op jit(solution)/shard_map/all_to_all | solution.py:271
  653.3 203.5 %all-gather.12.cloned.1.call-start = ((), (), s32[]{:S(2)}) async-start(), calls=%async_computation.15 | async-start | bytes 5308416 | tf_op jit(solution)/shard_map/all_gather | solution.py:208
  719.9 258.0 %reduce-scatter.19.cloned.1.call-start = ((), (), s32[]{:S(2)}) async-start(), calls=%async_computation.17 | async-start | bytes 1327104 | tf_op jit(solution)/shard_map/reduce_scatter | solution.py:404
  786.1 70.6 %copy-start.7 = (bf16[2,16,64,768]{3,2,1,0:T(8,128)(2,1)S(1)}, bf16[2,16,64,768]{3,2,1,0:T(8,128)(2,1)}, u32[]{:S(2)}) copy-start(bf16[2,16,64,768]{3,2,1,0:T(8,128)(2,1)} %param.35) | copy-start | bytes 9437188
  917.4 186.3 %reduce-scatter.27.cloned.1.call-start = ((), (), s32[]{:S(2)}) async-start(), calls=%async_computation.21 | async-start | bytes 245760
  979.7 552.5 %reduce-scatter.23.cloned.1.call-start = ((), (), s32[]{:S(2)}) async-start(), calls=%async_computation.19 | async-start | bytes 5308416 | tf_op jit(solution)/shard_map/reduce_scatter | solution.py:410
  1056.9 67.5 %all-to-all-start.2 = ((bf16[2,4,32,10752]{3,2,0,1:T(8,128)(2,1)}), bf16[2,4,32,10752]{3,2,0,1:T(8,128)(2,1)}, u32[]{:S(2)}, u32[]{:S(2)}) async-start(bf16[2,4,32,10752]{3,2,0,1:T(8,128)(2,1)} %copy.399), calls=%async_computation.2 | async-start | bytes 11010048 | tf_op jit(solution)/shard_map/all_to_all | solution.py:330
  1062.1 515.3 %reduce-scatter.29.cloned.1.call-start = ((), (), s32[]{:S(2)}) async-start(), calls=%async_computation.22 | async-start | bytes 5308416
  1086.8 546.9 %reduce-scatter.17.cloned.1.call-start = ((), (), s32[]{:S(2)}) async-start(), calls=%async_computation.16 | async-start | bytes 3981312 | tf_op jit(solution)/shard_map/reduce_scatter | solution.py:401
  1484.6 67.5 %all-to-all-start.3 = ((bf16[2,4,32,10752]{3,2,0,1:T(8,128)(2,1)}), bf16[2,4,32,10752]{3,2,0,1:T(8,128)(2,1)}, u32[]{:S(2)}, u32[]{:S(2)}) async-start(bf16[2,4,32,10752]{3,2,0,1:T(8,128)(2,1)} %copy.418), calls=%async_computation.3 | async-start | bytes 11010048 | tf_op jit(solution)/shard_map/all_to_all | solution.py:391
  1489.9 156.3 %reduce-scatter.31.cloned.1.call-start = ((), (), s32[]{:S(2)}) async-start(), calls=%async_computation.23 | async-start | bytes 737280
  1534.4 113.6 %reduce-scatter.21.cloned.1.call-start = ((), (), s32[]{:S(2)}) async-start(), calls=%async_computation.18 | async-start | bytes 737280 | tf_op jit(solution)/shard_map/reduce_scatter | solution.py:421
  1579.5 78.3 %reduce-scatter.25.cloned.1.call-start = ((), (), s32[]{:S(2)}) async-start(), calls=%async_computation.20 | async-start | bytes 737280
  (61 other events, 690.7 us)
Sparse Core Ops, SparseCore 0:
  20.2 66.0 all-gather.5
  207.8 37.1 all-gather.7
  247.1 79.7 all-gather.9
  720.1 77.8 all-gather.11
  917.5 60.3 reduce-scatter.18
  980.8 18.7 reduce-scatter.26
  1003.2 95.2 reduce-scatter.22
  1102.1 94.9 reduce-scatter.28
  1452.3 77.6 reduce-scatter.16
  1534.5 21.6 reduce-scatter.30
  1579.6 20.3 reduce-scatter.20
  1635.9 21.8 reduce-scatter.24
where the time goes:
time: 1690 us; the launch traced here: 1670 us
  local copies, waits for them, and re-layouts  655 us (39%)
  matrix products  485 us (29%)
  blocking collectives  267 us (16%)
  other arithmetic  129 us (8%)
  waiting for transfers between devices  93 us (6%)
  starting transfers between devices  21.7 us (1%)
    dot_general x1, matrix products, shards(): jnp.dot(normed_two, fc1_full, preferred_element_type=jnp.float32)  70.6 us
    all_gather x1, blocking collectives, shards(): lax.all_gather(w_fc2, 'band', axis=1, tiled=True)  66.6 us
    all_gather x1, blocking collectives, shards(): lax.all_gather(w_proj, 'band', axis=0, tiled=True)  64 us
    reduce_scatter x1, waiting for transfers between devices, shards(): lax.psum_scatter(grad_proj.astype(jnp.bfloat16), 'img', scatter_dimension...  60.3 us
    scatter x14, local copies, waits for them, and re-layouts  51.7 us
    dot_general x1, local copies, waits for them, and re-layouts, scores_of(): jnp.einsum('nqhc,qkc->nhqk', flat_queries, rows_wide, preferred_element_t...  44.4 us
    dot_general x1, local copies, waits for them, and re-layouts, scores_of(): jnp.einsum('nqhc,qkc->nhqk', flat_queries, cols_wide, preferred_element_t...  44.3 us
    unnamed x171, local copies, waits for them, and re-layouts  43.8 us
  transfers between devices with their start and end apart: 16, of which 4 were waited for; matrix products, arithmetic and copies ran while one was open for 72% of the time, Pallas kernels for 0%

commit v1 on v0

v1 whole, which is shorter than its diff:
```python
import functools
import numpy as np
import jax
import jax.numpy as jnp
from jax import lax
from jax.sharding import PartitionSpec as P
from jax.experimental import pallas as pl
from jax.experimental.pallas import tpu as pltpu

D = 768
HEADS = 12
HEAD = 64
FF = 3072
WIN = 14
SIDE = 64
GRID = 5
WINDOWS = 25
RELS = 27
STRIDE = 16
TW = WIN * STRIDE
PAIRS = HEADS // 2
LANES = 128
EPSILON = 1e-06
F32 = jnp.float32
BF16 = jnp.bfloat16
VMEM_LIMIT = 60 * 1024 * 1024
NT = (((1,), (1,)), ((), ()))


def mm(a, b):
    return jnp.dot(a, b, preferred_element_type=F32)


def mm_nt(a, b):
    return lax.dot_general(a, b, NT, preferred_element_type=F32)


def iota(shape, dim):
    return lax.broadcasted_iota(jnp.int32, shape, dim)


def token_target(meta_ref, w):
    t = iota((TW, 1), 0)
    a, b = t >> 4, t & 15
    col = meta_ref[w, 1] + b
    row = meta_ref[w, 2] + a
    ok = (b < WIN) & (col >= 0) & (col < SIDE) & (row >= 0) & (row < SIDE) & (meta_ref[w, 3] > 0)
    return jnp.where(ok, ((a & 3) << 6) + col, -1)


def take_window(target, rows_ref):
    picks = jnp.where(iota((TW, 256), 1) == target, 1.0, 0.0).astype(BF16)
    parts = []
    for q in range(3):
        src = rows_ref[4 * q : 4 * q + 4].reshape(256, D)
        parts.append(mm(picks[64 * q : 64 * q + 64], src))
    src = rows_ref[12:14].reshape(128, D)
    parts.append(mm(picks[192:224, :128], src))
    return jnp.concatenate(parts, axis=0)


def norm(values):
    mean = jnp.sum(values, axis=-1, keepdims=True) * (1.0 / D)
    centred = values - mean
    inverse = lax.rsqrt(jnp.sum(centred * centred, axis=-1, keepdims=True) * (1.0 / D) + EPSILON)
    return centred * inverse, inverse


def norm_back(grad, unit, inverse, gain):
    s = grad * gain
    m1 = jnp.sum(s, axis=-1, keepdims=True) * (1.0 / D)
    m2 = jnp.sum(s * unit, axis=-1, keepdims=True) * (1.0 / D)
    return inverse * (s - m1 - unit * m2)


def fold8(x):
    return jnp.sum(x.reshape(x.shape[0] // 8, 8, x.shape[1]), axis=0)


def roll_rows(x, sign):
    out = []
    for a in range(WIN):
        piece = x[STRIDE * a : STRIDE * a + STRIDE]
        by = (sign * (13 - a)) % LANES
        out.append(pltpu.roll(piece, by, 1) if by else piece)
    return jnp.concatenate(out, axis=0)


def roll_cols(x, first):
    out = []
    for a in range(WIN):
        piece = x[STRIDE * a : STRIDE * a + STRIDE]
        out.append(pltpu.roll(piece, first, 1, stride=1, stride_axis=0))
    return jnp.concatenate(out, axis=0)


def attn_fwd_pair(q, k8, v, table, keys_a, keys_b, p_ref, p):
    lane = iota((TW, LANES), 1)
    low_half = lane < 64
    rc = mm(q, table)
    both = jnp.where((lane & 31) < 16, roll_rows(rc[:, :LANES], -1), roll_cols(rc[:, LANES:], 3))
    high = both.astype(BF16)
    rest = (both - high.astype(F32)).astype(BF16)
    extra = jnp.where((lane & 63) < 32, high, rest)
    extra = jnp.where((lane & 63) == 14, jnp.ones_like(extra), extra)
    left = jnp.concatenate([q, extra], axis=1)
    zero = jnp.zeros_like(k8)
    wide_v = jnp.concatenate([v, jnp.ones_like(v)], axis=1)
    outs, invs = [], []
    for h in range(2):
        keys = jnp.concatenate(
            [jnp.where(low_half if h == 0 else ~low_half, k8, zero), (keys_a, keys_b)[h]], axis=1
        )
        s = mm_nt(left, keys)
        e = jnp.exp(s - jnp.max(s, axis=-1, keepdims=True)).astype(BF16)
        p_ref[2 * p + h] = e
        o = mm(e, wide_v)
        inv = 1.0 / o[:, LANES:]
        outs.append(o[:, :LANES] * inv)
        invs.append(inv)
    att = jnp.where(low_half, outs[0], outs[1]).astype(BF16)
    inv = jnp.where(low_half, invs[0], invs[1])
    return att, inv


def fwd_kernel(
    meta_ref, rows_ref, gain_ref, shift_ref, wqkv_ref, bias_ref, table_ref, ka_ref, kb_ref,
    x_ref, n_ref, qkv_ref, p_ref, inv_ref, att_ref,
):
    w = pl.program_id(0)
    target = token_target(meta_ref, w)
    x = take_window(target, rows_ref)
    x_ref[...] = x.astype(BF16)
    unit, _ = norm(x)
    normed = jnp.where(target >= 0, unit * gain_ref[...] + shift_ref[...], 0.0).astype(BF16)
    n_ref[...] = normed
    for c in range(9):
        cols = slice(256 * c, 256 * c + 256)
        y = mm(normed, wqkv_ref[:, cols]) + bias_ref[:, cols]
        if 3 <= c < 6:
            y = y.astype(BF16).astype(F32) * 0.125
        qkv_ref[:, cols] = y.astype(BF16)

    for p in range(PAIRS):
        a = slice(LANES * p, LANES * p + LANES)
        q = qkv_ref[:, LANES * p : LANES * p + LANES]
        k8 = qkv_ref[:, D + LANES * p : D + LANES * p + LANES]
        v = qkv_ref[:, 2 * D + LANES * p : 2 * D + LANES * p + LANES]
        att, inv = attn_fwd_pair(q, k8, v, table_ref[...], ka_ref[...], kb_ref[...], p_ref, p)
        att_ref[:, a] = att
        inv_ref[:, a] = inv


def rows_spec(rows):
    return pl.BlockSpec(
        (pl.Element(rows), pl.Element(SIDE), pl.Element(D)), lambda w, meta: (meta[w, 0], 0, 0)
    )


def whole(shape, buffers=1):
    zeros = (0,) * len(shape)
    return pl.BlockSpec(shape, lambda w, meta: zeros, pipeline_mode=pl.Buffered(buffers))


def per_window(*tail):
    zeros = (0,) * len(tail)
    return pl.BlockSpec((None,) + tail, lambda w, meta: (w,) + zeros)


def key_constants():
    t = np.arange(TW)
    kr, kc = t >> 4, t & 15
    real = kc < WIN
    base = np.zeros((TW, 64), np.float32)
    for off in (0, 32):
        base[t[real], off + kr[real]] = 1.0
        base[t[real], off + 16 + kc[real]] = 1.0
    back = np.zeros_like(base)
    back[t[real], kr[real]] = 1.0
    back[t[real], 16 + 13 - kc[real]] = 1.0
    base[~real, 14] = -1e30
    none = np.zeros_like(base)
    ka = np.concatenate([base, none], 1)
    kb = np.concatenate([none, base], 1)
    back = np.concatenate([back, back], 1)
    return jnp.asarray(ka, BF16), jnp.asarray(kb, BF16), jnp.asarray(back, BF16)


def rel_table(rel_rows, rel_cols, forward):
    def wide(rel):
        turned = jnp.pad(rel.T, ((0, 0), (0, 32 - RELS)))
        twice = jnp.concatenate([turned, turned], axis=1)
        none = jnp.zeros_like(twice)
        return jnp.concatenate(
            [jnp.concatenate([twice, none], 1), jnp.concatenate([none, twice], 1)], 0
        )

    return jnp.concatenate([wide(rel_rows[::-1]), wide(rel_cols[::-1] if forward else rel_cols)], axis=1)


def attention_forward(meta, ext, gain, shift, wqkv, bias, table, ka, kb):
    cap = meta.shape[0]
    sds = jax.ShapeDtypeStruct
    return pl.pallas_call(
        fwd_kernel,
        grid_spec=pltpu.PrefetchScalarGridSpec(
            num_scalar_prefetch=1,
            grid=(cap,),
            in_specs=[
                rows_spec(WIN), whole((1, D)), whole((1, D)), whole((D, 3 * D)), whole((1, 3 * D)),
                whole((LANES, 256)), whole((TW, LANES)), whole((TW, LANES)),
            ],
            out_specs=[
                per_window(TW, D), per_window(TW, D), per_window(TW, 3 * D),
                per_window(HEADS, TW, TW), per_window(TW, D), per_window(TW, D),
            ],
        ),
        out_shape=[
            sds((cap, TW, D), BF16), sds((cap, TW, D), BF16), sds((cap, TW, 3 * D), BF16),
            sds((cap, HEADS, TW, TW), BF16), sds((cap, TW, D), F32), sds((cap, TW, D), BF16),
        ],
        compiler_params=pltpu.CompilerParams(vmem_limit_bytes=VMEM_LIMIT),
        cost_estimate=pl.CostEstimate(flops=40_000_000_000, bytes_accessed=80_000_000, transcendentals=8_000_000),
    )(meta, ext, gain, shift, wqkv, bias, table, ka, kb)


def phi_parts(u):
    e = jnp.exp(u * u * -0.5)
    t = 1.0 / (1.0 + (0.3275911 * 0.7071067811865476) * jnp.abs(u))
    poly = t * (0.254829592 + t * (-0.284496736 + t * (1.421413741 + t * (-1.453152027 + t * 1.061405429))))
    tail = 0.5 * poly * e
    return jnp.where(u >= 0, 1.0 - tail, tail), e * 0.3989422804014327


def mlp_kernel(
    meta_ref, grows_ref, x_ref, att_ref, wproj_ref, pbias_ref, gain_ref, shift_ref, ff_ref, b1_ref, b2_ref,
    out_ref, g_ref, n2_ref, act_ref, dpre_ref, dmix_ref, datt_ref, sums_ref, sum1_ref,
    acc_ref, dn_ref,
):
    w = pl.program_id(0)

    @pl.when(w == 0)
    def _():
        sums_ref[...] = jnp.zeros_like(sums_ref)
        sum1_ref[...] = jnp.zeros_like(sum1_ref)

    target = token_target(meta_ref, w)
    g = take_window(target, grows_ref)
    gb = g.astype(BF16)
    g_ref[...] = gb
    sums_ref[0] += fold8(g)
    hidden = x_ref[...].astype(F32) + mm(att_ref[...], wproj_ref[...]) + pbias_ref[...]
    unit, inverse = norm(hidden)
    n2 = (unit * gain_ref[...] + shift_ref[...]).astype(BF16)
    n2_ref[...] = n2
    acc_ref[...] = hidden + b2_ref[...]
    parts, chunk = ff_ref.shape[0], ff_ref.shape[2] // 2
    for c in range(parts):
        cols = slice(chunk * c, chunk * c + chunk)
        w1, w2t = ff_ref[c, :, :chunk], ff_ref[c, :, chunk:]
        u = mm(n2, w1) + b1_ref[:, cols]
        dact = mm(gb, w2t)
        cdf, pdf = phi_parts(u)
        act = (u * cdf).astype(BF16)
        act_ref[:, cols] = act
        acc_ref[...] += mm_nt(act, w2t)
        dpre32 = dact * (cdf + u * pdf)
        dpre = dpre32.astype(BF16)
        dpre_ref[:, cols] = dpre
        sum1_ref[:, cols] += fold8(dpre32)
        step = mm_nt(dpre, w1)
        if c == 0:
            dn_ref[...] = step
        else:
            dn_ref[...] += step
    out_ref[...] = acc_ref[...].astype(BF16)
    dn = dn_ref[...]
    sums_ref[1] += fold8(dn * unit)
    sums_ref[2] += fold8(dn)
    dh = g + norm_back(dn, unit, inverse, gain_ref[...])
    dmix = dh.astype(BF16)
    dmix_ref[...] = dmix
    sums_ref[3] += fold8(dh)
    datt_ref[...] = mm_nt(dmix, wproj_ref[...]).astype(BF16)


def feed_forward(meta, gext, x, att, wproj, pbias, gain, shift, ff, b1, b2):
    cap = meta.shape[0]
    sds = jax.ShapeDtypeStruct
    return pl.pallas_call(
        mlp_kernel,
        grid_spec=pltpu.PrefetchScalarGridSpec(
            num_scalar_prefetch=1,
            grid=(cap,),
            in_specs=[
                rows_spec(WIN), per_window(TW, D), per_window(TW, D), whole((D, D)), whole((1, D)), whole((1, D)),
                whole((1, D)), whole(ff.shape), whole((1, FF)), whole((1, D)),
            ],
            out_specs=[
                per_window(TW, D), per_window(TW, D), per_window(TW, D), per_window(TW, FF), per_window(TW, FF),
                per_window(TW, D), per_window(TW, D), whole((4, 8, D)), whole((8, FF)),
            ],
            scratch_shapes=[pltpu.VMEM((TW, D), F32), pltpu.VMEM((TW, D), F32)],
        ),
        out_shape=[
            sds((cap, TW, D), BF16), sds((cap, TW, D), BF16), sds((cap, TW, D), BF16), sds((cap, TW, FF), BF16),
            sds((cap, TW, FF), BF16), sds((cap, TW, D), BF16), sds((cap, TW, D), BF16), sds((4, 8, D), F32),
            sds((8, FF), F32),
        ],
        compiler_params=pltpu.CompilerParams(vmem_limit_bytes=VMEM_LIMIT),
        cost_estimate=pl.CostEstimate(flops=60_000_000_000, bytes_accessed=80_000_000, transcendentals=8_000_000),
    )(meta, gext, x, att, wproj, pbias, gain, shift, ff, b1, b2)


def attn_bwd_kernel(
    meta_ref, qkv_ref, p_ref, inv_ref, att_ref, datt_ref, table_ref, kback_ref,
    dqkv_ref, rel_ref, bias_ref,
):
    w = pl.program_id(0)

    @pl.when(w == 0)
    def _():
        rel_ref[...] = jnp.zeros_like(rel_ref)
        bias_ref[...] = jnp.zeros_like(bias_ref)

    lane = iota((TW, LANES), 1)
    low_half = lane < 64
    onehot = kback_ref[...]
    for p in range(PAIRS):
        q = qkv_ref[:, LANES * p : LANES * p + LANES]
        k8 = qkv_ref[:, D + LANES * p : D + LANES * p + LANES]
        v = qkv_ref[:, 2 * D + LANES * p : 2 * D + LANES * p + LANES]
        cols = slice(LANES * p, LANES * p + LANES)
        da = datt_ref[:, cols].astype(F32) * inv_ref[:, cols]
        da_low = da.astype(BF16)
        prod = da_low.astype(F32) * att_ref[:, cols].astype(F32)
        keys = jnp.concatenate([k8, onehot], axis=1)
        da_t = da.T.astype(BF16)
        q_t = q.astype(F32).T.astype(BF16)
        zero = jnp.zeros_like(v)
        dqx, dv_t, dk_t = [], [], []
        for h in range(2):
            mine = low_half if h == 0 else ~low_half
            centre = jnp.sum(jnp.where(mine, prod, 0.0), axis=-1, keepdims=True)
            dp = mm_nt(da_low, jnp.where(mine, v, zero))
            e = p_ref[2 * p + h]
            ds = (e.astype(F32) * (dp - centre)).astype(BF16)
            dqx.append(mm(ds, keys))
            dv_t.append(mm(da_t[64 * h : 64 * h + 64], e))
            dk_t.append(mm(q_t[64 * h : 64 * h + 64], ds))
        dq = jnp.where(low_half, dqx[0][:, :LANES], dqx[1][:, :LANES])
        drc = jnp.where(low_half, dqx[0][:, LANES:], dqx[1][:, LANES:])
        part = lane & 63
        rows = roll_rows(jnp.where(part < 16, drc, 0.0), 1)
        cols_part = roll_cols(jnp.where((part >= 16) & (part < 32), drc, 0.0), LANES - 16)
        skew = jnp.concatenate([rows, cols_part], axis=1).astype(BF16)
        dq = dq + mm_nt(skew, table_ref[...])
        rel_ref[...] += mm(q_t, skew)
        dv = jnp.concatenate(dv_t, axis=0).T
        dk = (jnp.concatenate(dk_t, axis=0) * 0.125).T
        dqkv_ref[:, cols] = dq.astype(BF16)
        dqkv_ref[:, D + LANES * p : D + LANES * p + LANES] = dk.astype(BF16)
        dqkv_ref[:, 2 * D + LANES * p : 2 * D + LANES * p + LANES] = dv.astype(BF16)
        bias_ref[0, :, cols] += fold8(dq)
        bias_ref[1, :, cols] += fold8(dv)


def attention_backward(meta, qkv, p, inv, att, datt, table, kback):
    cap = meta.shape[0]
    sds = jax.ShapeDtypeStruct
    return pl.pallas_call(
        attn_bwd_kernel,
        grid_spec=pltpu.PrefetchScalarGridSpec(
            num_scalar_prefetch=1,
            grid=(cap,),
            in_specs=[
                per_window(TW, 3 * D), per_window(HEADS, TW, TW), per_window(TW, D), per_window(TW, D),
                per_window(TW, D), whole((LANES, 256)), whole((TW, LANES)),
            ],
            out_specs=[per_window(TW, 3 * D), whole((LANES, 256)), whole((2, 8, D))],
        ),
        out_shape=[sds((cap, TW, 3 * D), BF16), sds((LANES, 256), F32), sds((2, 8, D), F32)],
        compiler_params=pltpu.CompilerParams(vmem_limit_bytes=VMEM_LIMIT),
        cost_estimate=pl.CostEstimate(flops=60_000_000_000, bytes_accessed=80_000_000, transcendentals=0),
    )(meta, qkv, p, inv, att, datt, table, kback)


def rel_from(acc):
    def one(block):
        own = block[:64, :32] + block[64:, 64:96]
        return own[:, :RELS].T

    return one(acc[:, :LANES])[::-1], one(acc[:, LANES:])


def put_window(target, y, acc_ref, row0):
    picks = jnp.where(iota((TW, 256), 1) == target, 1.0, 0.0).astype(BF16)
    for q in range(4):
        n = 4 if q < 3 else 2
        t = slice(64 * q, 64 * q + STRIDE * n)
        part = lax.dot_general(
            picks[t, : 64 * n], y[t], (((0,), (0,)), ((), ())), preferred_element_type=F32
        )
        acc_ref[pl.ds(row0 + 4 * q, n)] += part.reshape(n, SIDE, D)


def scatter_kernel(meta_ref, y_ref, ext_ref, acc_ref):
    w = pl.program_id(0)

    @pl.when(w == 0)
    def _():
        acc_ref[...] = jnp.zeros_like(acc_ref)

    put_window(token_target(meta_ref, w), y_ref[...], acc_ref, meta_ref[w, 0])

    @pl.when(w == pl.num_programs(0) - 1)
    def _():
        def copy(i, _):
            ext_ref[i] = acc_ref[i].astype(BF16)
            return 0
        lax.fori_loop(0, ext_ref.shape[0], copy, 0)


def scatter(meta, y, ext_rows):
    cap = meta.shape[0]
    return pl.pallas_call(
        scatter_kernel,
        grid_spec=pltpu.PrefetchScalarGridSpec(
            num_scalar_prefetch=1,
            grid=(cap,),
            in_specs=[per_window(TW, D)],
            out_specs=whole((ext_rows, SIDE, D)),
            scratch_shapes=[pltpu.VMEM((ext_rows, SIDE, D), F32)],
        ),
        out_shape=jax.ShapeDtypeStruct((ext_rows, SIDE, D), BF16),
        compiler_params=pltpu.CompilerParams(vmem_limit_bytes=VMEM_LIMIT),
        cost_estimate=pl.CostEstimate(flops=5_000_000_000, bytes_accessed=20_000_000, transcendentals=0),
    )(meta, y)


def last_kernel(
    meta_ref, dqkv_ref, wqkv_ref, x_ref, dmix_ref, gain_ref, ext_ref, sums_ref, acc_ref,
):
    w = pl.program_id(0)

    @pl.when(w == 0)
    def _():
        acc_ref[...] = jnp.zeros_like(acc_ref)
        sums_ref[...] = jnp.zeros_like(sums_ref)

    target = token_target(meta_ref, w)
    dn = jnp.zeros((TW, D), F32)
    for c in range(3):
        cols = slice(D * c, D * c + D)
        dn = dn + mm_nt(dqkv_ref[:, cols], wqkv_ref[:, cols])
    dn = jnp.where(target >= 0, dn, 0.0)
    unit, inverse = norm(x_ref[...].astype(F32))
    sums_ref[0] += fold8(dn * unit)
    sums_ref[1] += fold8(dn)
    grad = dmix_ref[...].astype(F32) + norm_back(dn, unit, inverse, gain_ref[...])
    put_window(target, grad.astype(BF16), acc_ref, meta_ref[w, 0])

    @pl.when(w == pl.num_programs(0) - 1)
    def _():
        def copy(i, _):
            ext_ref[i] = acc_ref[i].astype(BF16)
            return 0
        lax.fori_loop(0, ext_ref.shape[0], copy, 0)


def last_norm(meta, dqkv, wqkv, x, dmix, gain, ext_rows):
    cap = meta.shape[0]
    sds = jax.ShapeDtypeStruct
    return pl.pallas_call(
        last_kernel,
        grid_spec=pltpu.PrefetchScalarGridSpec(
            num_scalar_prefetch=1,
            grid=(cap,),
            in_specs=[
                per_window(TW, 3 * D), whole((D, 3 * D)), per_window(TW, D), per_window(TW, D), whole((1, D)),
            ],
            out_specs=[whole((ext_rows, SIDE, D)), whole((2, 8, D))],
            scratch_shapes=[pltpu.VMEM((ext_rows, SIDE, D), F32)],
        ),
        out_shape=[sds((ext_rows, SIDE, D), BF16), sds((2, 8, D), F32)],
        compiler_params=pltpu.CompilerParams(vmem_limit_bytes=VMEM_LIMIT),
        cost_estimate=pl.CostEstimate(flops=15_000_000_000, bytes_accessed=30_000_000, transcendentals=0),
    )(meta, dqkv, wqkv, x, dmix, gain)


def window_plan(images, bands):
    lists = [[] for _ in range(bands)]
    if images == 2 and bands == 4:
        cuts = ((0, 8, 15, 20, 25), (0, 5, 10, 17, 25))
    else:
        cuts = [
            [(WINDOWS * b + (bands - 1 if m % 2 else 0)) // bands for b in range(bands + 1)] for m in range(images)
        ]
    for m in range(images):
        for b in range(bands):
            lists[b] += [(m, w) for w in range(cuts[m][b], min(cuts[m][b + 1], WINDOWS))]
    cap = max(len(item) for item in lists)
    return np.array([item + [(0, -1)] * (cap - len(item)) for item in lists], np.int32)


HALO = 12


def near(images, bands, band_rows):
    return images == 2 and bands == 4 and band_rows == 16


CORE = [(0, 1), (1, 0), (2, 3), (3, 2)]
CROSS = [(1, 2), (2, 1)]


def extend(rows, band):
    images, band_rows = rows.shape[:2]
    if not near(images, lax.axis_size("band"), band_rows):
        full = lax.all_gather(rows, "band", axis=1, tiled=True)
        return jnp.pad(full, ((0, 0), (6, 6), (0, 0), (0, 0)))
    odd = band % 2 == 1
    top, bottom = rows[:, :HALO], rows[:, -HALO:]
    from_core = lax.ppermute(jnp.where(odd, top, bottom), "band", CORE)
    from_cross = lax.ppermute(jnp.where(odd, bottom[1], top[0]), "band", CROSS)
    zero = jnp.zeros_like(from_cross)
    above = jnp.where(odd, from_core, jnp.stack([zero, from_cross]))
    below = jnp.where(odd, jnp.stack([from_cross, zero]), from_core)
    return jnp.concatenate([above, rows, below], axis=1)


def collect(ext, band, images, band_rows):
    if not near(images, lax.axis_size("band"), band_rows):
        return lax.psum_scatter(ext[:, 6:-6], "band", scatter_dimension=1, tiled=True).astype(F32)
    odd = band % 2 == 1
    above, below = ext[:, :HALO], ext[:, -HALO:]
    from_core = lax.ppermute(jnp.where(odd, above, below), "band", CORE).astype(F32)
    from_cross = lax.ppermute(jnp.where(odd, below[0], above[1]), "band", CROSS).astype(F32)
    zero = jnp.zeros_like(from_cross)
    top = jnp.where(odd, from_core, jnp.stack([from_cross, zero]))
    bottom = jnp.where(odd, jnp.stack([zero, from_cross]), from_core)
    own = ext[:, HALO:-HALO].astype(F32)
    rest = band_rows - HALO
    return own + jnp.pad(top, ((0, 0), (0, rest), (0, 0), (0, 0))) + jnp.pad(bottom, ((0, 0), (rest, 0), (0, 0), (0, 0)))


def shards(
    image_tokens, pad_offsets, ln1_gain, ln1_bias, w_qkv, q_bias, v_bias, rel_rows, rel_cols, w_proj, proj_bias,
    ln2_gain, ln2_bias, w_fc1, fc1_bias, w_fc2, fc2_bias, out_grad,
):
    images, band_rows = image_tokens.shape[:2]
    bands, groups = lax.axis_size("band"), lax.axis_size("img")
    band, group = lax.axis_index("band"), lax.axis_index("img")
    axes = ("img", "band")

    part, wide = w_qkv.shape
    small = jnp.concatenate(
        [
            ln1_gain, ln1_bias, q_bias, v_bias, proj_bias, ln2_gain, ln2_bias, fc2_bias, fc1_bias,
            rel_rows.reshape(-1), rel_cols.reshape(-1),
        ]
    )
    small_rows = -(-small.shape[0] // (wide * 8)) * 8
    small = jnp.pad(small, (0, small_rows * wide - small.shape[0])).reshape(small_rows, wide)
    first = lax.all_gather(jnp.concatenate([w_qkv, small], axis=0), axes, axis=0, tiled=False)
    first = first.reshape(groups, bands, part + small_rows, wide)
    second = lax.all_gather(
        jnp.concatenate([w_fc1, w_fc2.T, w_proj], axis=1), axes, axis=0, tiled=False
    ).reshape(groups, bands * part, -1)
    wqkv = first[:, :, :part].transpose(1, 2, 0, 3).reshape(D, 3 * D)
    tail = first[:, :, part:].reshape(groups, bands, small_rows * wide)
    share = D // groups
    vectors = tail[:, 0, : 8 * share].reshape(groups, 8, share).transpose(1, 0, 2).reshape(8, 1, D).astype(F32)
    fc1_shift = tail[:, 0, 8 * share : 8 * share + FF // groups].reshape(1, FF).astype(F32)
    at = 8 * share + FF // groups
    rels = tail[0, :, at : at + 2 * RELS * (HEAD // bands)].reshape(bands, 2, RELS, HEAD // bands)
    rels = rels.transpose(1, 2, 0, 3).reshape(2, RELS, HEAD)
    gain1, shift1, qb, vb, pb, gain2, shift2, b2 = [vectors[i] for i in range(8)]
    bias = jnp.concatenate([qb, jnp.zeros_like(qb), vb], axis=1)
    inner = FF // groups
    ff = second[:, :, : 2 * inner]
    wproj = second[:, :, 2 * inner :].transpose(1, 0, 2).reshape(D, D)

    plan = jnp.asarray(window_plan(images, bands))[band]
    image, window = plan[:, 0], plan[:, 1]
    close = near(images, bands, band_rows)
    ext_per = band_rows + 2 * HALO if close else bands * band_rows + 12
    base = band_rows * band - HALO if close else -6
    live = window >= 0
    spot = jnp.maximum(window, 0)
    offsets = pad_offsets[image]
    row = spot // GRID * WIN - offsets[:, 0]
    col = spot % GRID * WIN - offsets[:, 1]
    meta = jnp.stack(
        [jnp.where(live, image * ext_per + row - base, 0), col, row, live.astype(jnp.int32)], axis=1
    ).astype(jnp.int32)
    cap = meta.shape[0]
    ext_rows = images * ext_per

    ka, kb, kback = key_constants()
    ext = extend(image_tokens, band).reshape(ext_rows, SIDE, D)
    x, normed1, qkv, probs, inv, att = attention_forward(
        meta, ext, gain1, shift1, wqkv, bias, rel_table(rels[0], rels[1], True), ka, kb
    )
    gext = extend(out_grad, band).reshape(ext_rows, SIDE, D)
    out_win, g, normed2, act, d_pre, d_mixed, d_att, sums, sum_fc1 = feed_forward(
        meta, gext, x, att, wproj, pb, gain2, shift2, ff, fc1_shift, b2
    )
    out_ext = scatter(meta, out_win, ext_rows).reshape(images, ext_per, SIDE, D)
    output = collect(out_ext, band, images, band_rows).astype(BF16)

    def flat(a):
        return a.reshape(cap * TW, a.shape[-1])

    def weight_grad(left, right):
        return jnp.einsum("td,te->de", flat(left), flat(right), preferred_element_type=F32).astype(BF16)

    d_fc1 = weight_grad(normed2, d_pre)
    d_fc2 = weight_grad(act, g)
    d_proj = weight_grad(att, d_mixed)
    d_qkv, rel_acc, bias_sums = attention_backward(
        meta, qkv, probs, inv, att, d_att, rel_table(rels[0], rels[1], False), kback
    )
    d_wqkv = weight_grad(normed1, d_qkv)
    in_ext, sums1 = last_norm(meta, d_qkv, wqkv, x, d_mixed, gain1, ext_rows)
    input_grad = collect(in_ext.reshape(images, ext_per, SIDE, D), band, images, band_rows)

    def reduce(grad, rows_axis, cols_axis):
        grad = lax.psum_scatter(grad, cols_axis, scatter_dimension=1, tiled=True)
        return lax.psum_scatter(grad, rows_axis, scatter_dimension=0, tiled=True).astype(F32)

    d_rel_rows, d_rel_cols = rel_from(rel_acc)
    total = lax.psum(
        (jnp.sum(sums1, 1), jnp.sum(bias_sums, 1), jnp.sum(sums, 1), jnp.sum(sum_fc1, 0), d_rel_rows, d_rel_cols), axes
    )

    def img_share(vector):
        n = vector.shape[0] // groups
        return lax.dynamic_slice_in_dim(vector, group * n, n, 0)

    def band_share(table):
        n = table.shape[1] // bands
        return lax.dynamic_slice_in_dim(table, band * n, n, 1)

    return (
        output,
        input_grad,
        img_share(total[0][0]),
        img_share(total[0][1]),
        reduce(d_wqkv, "band", "img"),
        img_share(total[1][0]),
        img_share(total[1][1]),
        band_share(total[4]),
        band_share(total[5]),
        reduce(d_proj, "band", "img"),
        img_share(total[2][3]),
        img_share(total[2][1]),
        img_share(total[2][2]),
        reduce(d_fc1, "band", "img"),
        img_share(total[3]),
        reduce(d_fc2, "img", "band"),
        img_share(total[2][0]),
    )


def solution(mesh):
    tokens, vector, matrix = P("img", "band", None, None), P("img"), P("band", "img")
    table, wide = P(None, "band"), P("img", "band")
    return jax.shard_map(
        shards,
        mesh=mesh,
        in_specs=(
            tokens, P("img", None), vector, vector, matrix, vector, vector, table, table, matrix, vector, vector,
            vector, matrix, vector, wide, vector, tokens,
        ),
        out_specs=(
            tokens, tokens, vector, vector, matrix, vector, vector, table, table, matrix, vector, vector, vector,
            matrix, vector, wide, vector,
        ),
        check_vma=False,
    )
```

time: 1690 us -> 788 us (0.47)
  local copies, waits for them, and re-layouts: 655 us -> 80 us
  matrix products: 485 us -> 67.1 us
  Pallas kernels: 0 us -> 298 us
  blocking collectives: 267 us -> 43.9 us
  waiting for transfers between devices: 93 us -> 201 us
  other arithmetic: 129 us -> 62.4 us
    dot_general x35 -> x4, matrix products: 485 us -> 67.1 us  [weight_grad(): jnp.einsum('td,te->de', flat(left), flat(right), preferred_element_type=F32)]
    pallas_call x0 -> x5, Pallas kernels: none -> 298 us  [the longest x1 131 us: feed_forward(): pl.pallas_call(mlp_kernel, grid_spec=pltpu.PrefetchScalarGridSpec(num_sca...]
    reshape x28 -> x7, local copies, waits for them, and re-layouts: 280 us -> 10.1 us  [the longest x1 8 us: shards(): wqkv = first[:, :, :part].transpose(1, 2, 0, 3).reshape(D, 3 * D)]
    all_gather x7 -> x0, blocking collectives: 186 us -> none  [the longest x1 66.6 us: shards(): lax.all_gather(w_fc2, 'band', axis=1, tiled=True)]
    dot_general x4 -> x0, local copies, waits for them, and re-layouts: 124 us -> none  [the longest x1 44.4 us: scores_of(): jnp.einsum('nqhc,qkc->nhqk', flat_queries, rows_wide, preferred_element_t...]
    convert_element_type x12 -> x1, local copies, waits for them, and re-layouts: 93.8 us -> 0.08 us  [shards(): tail[:, 0, :8 * share].reshape(groups, 8, share).transpose(1, 0, 2)]
    unnamed x16 -> x14, waiting for transfers between devices: 8.32 us -> 93.1 us
    scatter x14 -> x0, local copies, waits for them, and re-layouts: 51.7 us -> none
  transfers between devices with their start and end apart: 16 -> 18, of which waited for: 4 -> 7; matrix products, arithmetic and copies ran while one was open for 72% -> 23% of each run, Pallas kernels for 0% -> 21%
where the time goes in v1:
time: 788 us; the launch traced here: 778 us
  Pallas kernels  298 us (38%)
  waiting for transfers between devices  201 us (26%)
  local copies, waits for them, and re-layouts  80 us (10%)
  matrix products  67.1 us (9%)
  other arithmetic  62.4 us (8%)
  blocking collectives  43.9 us (6%)
  between operations  15 us (2%)
  starting transfers between devices  10.2 us (1%)
    pallas_call x1, Pallas kernels, feed_forward(): pl.pallas_call(mlp_kernel, grid_spec=pltpu.PrefetchScalarGridSpec(num_sca...  131 us
    unnamed x14, waiting for transfers between devices  93.1 us
    dot_general x4, matrix products, weight_grad(): jnp.einsum('td,te->de', flat(left), flat(right), preferred_element_type=F32)  67.1 us
    pallas_call x1, Pallas kernels, attention_backward(): pl.pallas_call(attn_bwd_kernel, grid_spec=pltpu.PrefetchScalarGridSpec(nu...  56 us
    pallas_call x1, Pallas kernels, attention_forward(): pl.pallas_call(fwd_kernel, grid_spec=pltpu.PrefetchScalarGridSpec(num_sca...  52 us
    psum x1, blocking collectives, shards(): lax.psum((jnp.sum(sums1, 1), jnp.sum(bias_sums, 1), jnp.sum(sums, 1), jnp...  43.9 us
    pallas_call x1, Pallas kernels, last_norm(): pl.pallas_call(last_kernel, grid_spec=pltpu.PrefetchScalarGridSpec(num_sc...  41.9 us
    all_gather x1, waiting for transfers between devices, shards(): lax.all_gather(jnp.concatenate([w_qkv, small], axis=0), axes, axis=0, til...  38.2 us
  transfers between devices with their start and end apart: 18, of which 7 were waited for; matrix products, arithmetic and copies ran while one was open for 23% of the time, Pallas kernels for 21%

profile of v1, /device:TPU:0, one launch (start us, length us, event | category | flops | bytes accessed | tf_op | source)
XLA Modules:
  0.0 778.3 jit_solution(8154030082742481171)
XLA Ops:
  10.0 6.1 concatenate.68
  19.1 4.2 slice_select_fusion.2
  46.7 38.2 %all-gather.8.cloned.1.call-done = bf16[32,200,288]{1,2,0:T(8,128)(2,1)} async-done(((bf16[1,200,288]{1,2,0:T(8,128)(2,1)}), bf16[32,200,288]{1,2,0:T(8,128)(2,1)}) %all-gather.8.cloned.1.call-update) | async-done | bytes 3686416 | tf_op jit(solution)/shard_map/all_gather | solution.py:565
  90.9 8.4 %copy.125 = bf16[8,4,192,288]{3,0,2,1:T(8,128)(2,1)} copy(bf16[8,4,192,288]{2,3,1,0:T(8,128)(2,1)} %bitcast.98) | data formatting | bytes 7077888
  99.3 8.0 %reshape.152.wqkv_ref = bf16[768,2304]{1,0:T(8,128)(2,1)} reshape(bf16[4,192,8,288]{3,2,1,0:T(8,128)(2,1)} %bitcast.88) | data formatting | bytes 7077888 | tf_op jit(solution)/shard_map/reshape | solution.py:570
  112.7 52.0 %shard_map.341 = (bf16[13,224,768]{2,1,0:T(8,128)(2,1)}, bf16[13,224,768]{2,1,0:T(8,128)(2,1)}, bf16[13,224,2304]{2,1,0:T(8,128)(2,1)}, bf16[13,12,224,224]{3,2,...) custom-call(s32[13,4]{1,0:T(8,128)} %pad_add_fusion.1.meta_ref, ...), custom_call_target="tpu_custom_call" | custom-call | flops 40000000000 | bytes 80000000 | tf_op jit(solution)/shard_map/pallas_call | solution.py:204
  164.6 10.9 %all-gather.6.cloned.1.call-done = bf16[6144,864]{1,0:T(8,128)(2,1)} async-done(((bf16[192,864]{1,0:T(8,128)(2,1)}), bf16[6144,864]{1,0:T(8,128)(2,1)}) %all-gather.6.cloned.1.call-update) | async-done | bytes 10616848 | tf_op jit(solution)/shard_map/all_gather | solution.py:567
  175.6 7.9 %slice.256.ff_ref = bf16[8,768,768]{2,1,0:T(8,128)(2,1)} slice(bf16[8,768,864]{2,1,0:T(8,128)(2,1)} %bitcast.95), slice={[0:8], [0:768], [0:768]} | slice | bytes 18874368 | tf_op jit(solution)/shard_map/slice | solution.py:581
  187.2 131.5 %shard_map.342 = (bf16[13,224,768]{2,1,0:T(8,128)(2,1)}, bf16[13,224,768]{2,1,0:T(8,128)(2,1)}, bf16[13,224,768]{2,1,0:T(8,128)(2,1)}, bf16[13,224,3072]{2,1,0:T...) custom-call(s32[13,4]{1,0:T(8,128)} %pad_add_fusion.1.meta_ref, ...), custom_call_target="tpu_custom_call" | custom-call | flops 60000002048 | bytes 80000000 | tf_op jit(solution)/shard_map/pallas_call | solution.py:290
  318.7 8.5 %bitcast_convert_fusion.3 = bf16[768,768]{0,1:T(8,128)(2,1)} fusion(bf16[13,224,768]{2,1,0:T(8,128)(2,1)} %get-tuple-element.38.att_ref, bf16[13,224,768]{2,1,0:T(8,128)(2,1)} %get-tuple-element.45.dmix_ref), kind=kOutput, calls=%fused_computation.14 | convolution fusion | flops 3435724800 | bytes 10125312 | tf_op jit(solution)/shard_map/td,te->de/dot_general | solution.py:616
  327.3 56.0 %shard_map.344 = (bf16[13,224,2304]{2,1,0:T(8,128)(2,1)}, f32[128,256]{1,0:T(8,128)}, f32[2,8,768]{2,1,0:T(8,128)}) custom-call(s32[13,4]{1,0:T(8,128)} %pad_add_fusion.1.meta_ref, bf16[13,224,2304]{2,1,0:T(8,128)(2,1)} %get-tuple-element.40.qkv_ref, bf16[13,12,224,224]{3,2,1,0:T(8,128)(2,1)} %get-tuple-element.41.p_ref, ...), custom_call_target="tpu_custom_call" | custom-call | flops 60000002048 | bytes 80000000 | tf_op jit(solution)/shard_map/pallas_call | solution.py:371
  383.3 17.2 %bitcast_convert_fusion.2 = bf16[768,2304]{0,1:T(8,128)(2,1)} fusion(bf16[13,224,768]{2,1,0:T(8,128)(2,1)} %get-tuple-element.48, bf16[13,224,2304]{2,1,0:T(8,128)(2,1)} %get-tuple-element.44.dqkv_ref), kind=kOutput, calls=%fused_computation.5 | convolution fusion | flops 10307174400 | bytes 21430272 | tf_op jit(solution)/shard_map/td,te->de/dot_general | solution.py:616
  400.5 20.7 %bitcast_convert_fusion.1 = bf16[768,3072]{1,0:T(8,128)(2,1)} fusion(bf16[13,224,768]{2,1,0:T(8,128)(2,1)} %get-tuple-element.52, bf16[13,224,3072]{2,1,0:T(8,128)(2,1)} %get-tuple-element.53), kind=kOutput, calls=%fused_computation.2 | convolution fusion | flops 13742899200 | bytes 27082752 | tf_op jit(solution)/shard_map/td,te->de/dot_general | solution.py:616
  421.2 6.7 copy.119
  428.0 20.6 %bitcast_convert_fusion = bf16[3072,768]{0,1:T(8,128)(2,1)} fusion(bf16[13,224,3072]{2,1,0:T(8,128)(2,1)} %get-tuple-element.55, bf16[13,224,768]{2,1,0:T(8,128)(2,1)} %get-tuple-element.56), kind=kOutput, calls=%fused_computation.1 | convolution fusion | flops 13742899200 | bytes 27082752 | tf_op jit(solution)/shard_map/td,te->de/dot_general | solution.py:616
  450.9 41.9 %shard_map.345 = (bf16[80,64,768]{2,1,0:T(8,128)(2,1)}, f32[2,8,768]{2,1,0:T(8,128)}) custom-call(s32[13,4]{1,0:T(8,128)} %pad_add_fusion.1.meta_ref, bf16[13,224,2304]{2,1,0:T(8,128)(2,1)} %get-tuple-element.44.dqkv_ref, bf16[768,2304]{1,0:T(8,128)(2,1)} %reshape.152.wqkv_ref, bf16[13,224,768]{2,1,0:T(8,128)(2,1)} %get-tuple-element.37.x_ref, ...), custom_call_target="tpu_custom_call" | custom-call | flops 15000000512 | bytes 30000000 | tf_op jit(solution)/shard_map/pallas_call | solution.py:474
  506.3 17.0 %shard_map.343 = bf16[80,64,768]{2,1,0:T(8,128)(2,1)} custom-call(s32[13,4]{1,0:T(8,128)} %pad_add_fusion.1.meta_ref, bf16[13,224,768]{2,1,0:T(8,128)(2,1)} %get-tuple-element.39.y_ref), custom_call_target="tpu_custom_call" | custom-call | flops 5000000000 | bytes 20000000 | tf_op jit(solution)/shard_map/pallas_call | solution.py:426
  530.0 4.0 slice_select_fusion.1
  534.8 43.9 %all-reduce.16 = (f32[2,768]{1,0:T(2,128)}, f32[2,768]{1,0:T(2,128)}, f32[27,64]{0,1:T(8,128)}, f32[27,64]{0,1:T(8,128)}, f32[4,768]{1,0:T(4,128)}, /*index=5*/f32[3072]{0:T(1024)}) all-reduce(f32[2,768]{1,0:T(2,128)} %reduce_sum.36, f32[2,768]{1,0:T(2,128)} %reduce_sum.37, ...), channel_id=1, replica_groups=mesh['img'=8,'band'=4] {'img','band'}, use_global_device_ids=true, to_apply=%region_1.2 | all-reduce | flops 12672 | bytes 101376 | tf_op jit(solution)/shard_map/psum | solution.py:633
  591.9 36.3 %reduce-scatter.23.cloned.1.call-done = bf16[3072,192]{0,1:T(8,128)(2,1)} async-done(((bf16[3072,768]{0,1:T(8,128)(2,1)}), bf16[3072,192]{0,1:T(8,128)(2,1)}) %reduce-scatter.23.cloned.1.call-update) | async-done | bytes 1179664 | tf_op jit(solution)/shard_map/reduce_scatter | solution.py:629
  642.2 6.0 pad_add_fusion
  652.7 23.1 %reduce-scatter.25.cloned.1.call-done = bf16[192,288]{1,0:T(8,128)(2,1)} async-done(((bf16[768,288]{1,0:T(8,128)(2,1)}), bf16[192,288]{1,0:T(8,128)(2,1)}) %reduce-scatter.25.cloned.1.call-update) | async-done | bytes 110608
  677.7 22.9 %reduce-scatter.21.cloned.1.call-done = bf16[192,384]{1,0:T(8,128)(2,1)} async-done(((bf16[768,384]{1,0:T(8,128)(2,1)}), bf16[192,384]{1,0:T(8,128)(2,1)}) %reduce-scatter.21.cloned.1.call-update) | async-done | bytes 147472 | tf_op jit(solution)/shard_map/reduce_scatter | solution.py:630
  702.3 66.9 %reduce-scatter.31.cloned.1.call-done = bf16[384,192]{1,0:T(8,128)(2,1)} async-done(((bf16[3072,192]{1,0:T(8,128)(2,1)}), bf16[384,192]{1,0:T(8,128)(2,1)}) %reduce-scatter.31.cloned.1.call-update) | async-done | bytes 147472
  (160 shorter events, 104.3 us)
Async XLA Ops:
  7.2 25.3 %copy-start = (s32[2,2]{1,0:T(2,128)S(1)}, s32[2,2]{1,0:T(2,128)}, u32[]{:S(2)}) copy-start(s32[2,2]{1,0:T(2,128)} %param.23) | copy-start | bytes 52
  7.2 77.7 %all-gather.8.cloned.1.call-start = ((), (), s32[]{:S(2)}) async-start(), calls=%async_computation.13 | async-start | bytes 4866048 | tf_op jit(solution)/shard_map/all_gather | solution.py:565
  17.2 158.4 %all-gather.6.cloned.1.call-start = ((), (), s32[]{:S(2)}) async-start(), calls=%async_computation.12 | async-start | bytes 11354112 | tf_op jit(solution)/shard_map/all_gather | solution.py:567
  19.0 485.4 %reduce-scatter.19.cloned.1.call-start = ((), (), s32[]{:S(2)}) async-start(), calls=%async_computation.9 | async-start | bytes 1327104 | tf_op jit(solution)/shard_map/reduce_scatter | solution.py:629
  19.1 4.7 copy-start.3
  23.3 10.6 %collective-permute-start.2 = (bf16[2,12,64,768]{3,2,1,0:T(8,128)(2,1)}, bf16[2,12,64,768]{3,2,1,0:T(8,128)(2,1)}, u32[]{:S(2)}, u32[]{:S(2)}) collective-permute-start(bf16[2,12,64,768]{3,2,1,0:T(8,128)(2,1)} %slice_select_fusion.2), channel_id=1, source_target_pairs={{0,1},{1,0},{2,3},{3,2},{4,5},{5,4},{6,7},{7,6},{8,9},{9,8},{10,11... | collective-permute-start | bytes 7077896 | tf_op jit(solution)/shard_map/ppermute | solution.py:524
  25.4 11.1 %collective-permute-start = (bf16[2,12,64,768]{3,2,1,0:T(8,128)(2,1)}, bf16[2,12,64,768]{3,2,1,0:T(8,128)(2,1)}, u32[]{:S(2)}, u32[]{:S(2)}) collective-permute-start(bf16[2,12,64,768]{3,2,1,0:T(8,128)(2,1)} %slice_select_fusion.3), channel_id=1, source_target_pairs={{0,1},{1,0},{2,3},{3,2},{4,5},{5,4},{6,7},{7,6},{8,9},{9,8},{10,11... | collective-permute-start | bytes 7077896 | tf_op jit(solution)/shard_map/ppermute | solution.py:524
  27.0 6.9 collective-permute-start.3
  29.8 6.7 collective-permute-start.1
  327.2 200.6 %reduce-scatter.17.cloned.1.call-start = ((), (), s32[]{:S(2)}) async-start(), calls=%async_computation.8 | async-start | bytes 3981312 | tf_op jit(solution)/shard_map/reduce_scatter | solution.py:629
  400.4 182.2 %reduce-scatter.29.cloned.1.call-start = ((), (), s32[]{:S(2)}) async-start(), calls=%async_computation.16 | async-start | bytes 5308416
  427.9 200.2 %reduce-scatter.23.cloned.1.call-start = ((), (), s32[]{:S(2)}) async-start(), calls=%async_computation.11 | async-start | bytes 5898240 | tf_op jit(solution)/shard_map/reduce_scatter | solution.py:629
  448.7 202.4 %reduce-scatter.27.cloned.1.call-start = ((), (), s32[]{:S(2)}) async-start(), calls=%async_computation.15 | async-start | bytes 245760
  450.9 43.3 %copy-start.8 = (f32[2,8,768]{2,1,0:T(8,128)S(1)}, f32[2,8,768]{2,1,0:T(8,128)}, u32[]{:S(2)}) copy-start(f32[2,8,768]{2,1,0:T(8,128)} %get-tuple-element.49) | copy-start | bytes 147460
  450.9 43.9 %copy-start.7 = (f32[4,8,768]{2,1,0:T(8,128)S(1)}, f32[4,8,768]{2,1,0:T(8,128)}, u32[]{:S(2)}) copy-start(f32[4,8,768]{2,1,0:T(8,128)} %get-tuple-element.51) | copy-start | bytes 294916
  450.9 43.9 %copy-start.6 = (f32[8,3072]{1,0:T(8,128)S(1)}, f32[8,3072]{1,0:T(8,128)}, u32[]{:S(2)}) copy-start(f32[8,3072]{1,0:T(8,128)} %get-tuple-element.54) | copy-start | bytes 294916
  498.3 132.7 %collective-permute-start.7 = (bf16[12,64,768]{2,1,0:T(8,128)(2,1)}, bf16[12,64,768]{2,1,0:T(8,128)(2,1)S(1)}, u32[]{:S(2)}, u32[]{:S(2)}) collective-permute-start(bf16[12,64,768]{2,1,0:T(8,128)(2,1)} %fusion), channel_id=1, source_target_pairs={{1,2},{2,1},{5,6},{6,5},{9,10},{10,9},{13,14},{14,13},{17,18},{18,... | collective-permute-start | bytes 3538952 | tf_op jit(solution)/shard_map/ppermute | solution.py:538
  501.7 137.5 %collective-permute-start.6 = (bf16[2,12,64,768]{3,2,1,0:T(8,128)(2,1)S(1)}, bf16[2,12,64,768]{3,2,1,0:T(8,128)(2,1)}, u32[]{:S(2)}, u32[]{:S(2)}) collective-permute-start(bf16[2,12,64,768]{3,2,1,0:T(8,128)(2,1)S(1)} %slice_select_fusion), channel_id=1, source_target_pairs={{0,1},{1,0},{2,3},{3,2},{4,5},{5,4},{6,7},{7,6},{8,9},{9,8},{10,11... | collective-permute-start | bytes 7077896 | tf_op jit(solution)/shard_map/ppermute | solution.py:537
  506.2 169.6 %reduce-scatter.25.cloned.1.call-start = ((), (), s32[]{:S(2)}) async-start(), calls=%async_computation.14 | async-start | bytes 737280
  526.1 105.1 %collective-permute-start.5 = (bf16[12,64,768]{2,1,0:T(8,128)(2,1)}, bf16[12,64,768]{2,1,0:T(8,128)(2,1)}, u32[]{:S(2)}, u32[]{:S(2)}) collective-permute-start(bf16[12,64,768]{2,1,0:T(8,128)(2,1)} %fusion.1), channel_id=1, source_target_pairs={{1,2},{2,1},{5,6},{6,5},{9,10},{10,9},{13,14},{14,13},{17,18},{18,... | collective-permute-start | bytes 3538952 | tf_op jit(solution)/shard_map/ppermute | solution.py:538
  529.9 170.7 %reduce-scatter.21.cloned.1.call-start = ((), (), s32[]{:S(2)}) async-start(), calls=%async_computation.10 | async-start | bytes 737280 | tf_op jit(solution)/shard_map/reduce_scatter | solution.py:630
  534.0 98.7 %collective-permute-start.4 = (bf16[2,12,64,768]{3,2,1,0:T(8,128)(2,1)}, bf16[2,12,64,768]{3,2,1,0:T(8,128)(2,1)}, u32[]{:S(2)}, u32[]{:S(2)}) collective-permute-start(bf16[2,12,64,768]{3,2,1,0:T(8,128)(2,1)} %slice_select_fusion.1), channel_id=1, source_target_pairs={{0,1},{1,0},{2,3},{3,2},{4,5},{5,4},{6,7},{7,6},{8,9},{9,8},{10,11... | collective-permute-start | bytes 7077896 | tf_op jit(solution)/shard_map/ppermute | solution.py:537
  584.8 184.4 %reduce-scatter.31.cloned.1.call-start = ((), (), s32[]{:S(2)}) async-start(), calls=%async_computation.17 | async-start | bytes 1769472
  642.2 128.8 %copy-start.1 = (s32[2,2]{1,0:T(2,128)S(1)}, s32[2,2]{1,0:T(2,128)}, u32[]{:S(2)}) copy-start(s32[2,2]{1,0:T(2,128)} %param.23) | copy-start | bytes 52
  (3 other events, 7.1 us)
Sparse Core Ops, SparseCore 0:
  17.3 67.5 all-gather.7
  87.8 87.7 all-gather.5
  327.3 62.5 reduce-scatter.18
  400.6 77.6 reduce-scatter.16
  481.7 95.9 reduce-scatter.28
  580.7 47.4 reduce-scatter.22
  631.3 19.6 reduce-scatter.26
  653.7 22.0 reduce-scatter.24
  678.5 22.0 reduce-scatter.20
  704.3 64.8 reduce-scatter.30

commit v2 on v1

--- a/solution.py
+++ b/solution.py
@@ -312,11 +312,153 @@
     )(meta, gext, x, att, wproj, pbias, gain, shift, ff, b1, b2)
 
 
+MESH = pl.DeviceIdType.MESH
+SHARD_ROWS = 192
+SHARD_COLS = 384
+
+
+def place():
+    img, band = lax.axis_index("img"), lax.axis_index("band")
+    return {"zh": img // 4, "zl": img // 2 % 2, "y": img % 2, "x": band // 2, "c": band % 2}
+
+
+def partner(dim):
+    img, band = lax.axis_index("img"), lax.axis_index("band")
+    at = place()[dim]
+    step = {"zh": 4, "zl": 2, "y": 1, "x": 2, "c": 1}[dim]
+    move = step - 2 * step * at
+    return (img, band + move) if dim in ("x", "c") else (img + move, band)
+
+
+def greet():
+    barrier = pltpu.get_barrier_semaphore()
+    for dim in ("c", "x", "y", "zh", "zl"):
+        pl.semaphore_signal(barrier, inc=1, device_id=partner(dim), device_id_type=MESH)
+    pl.semaphore_wait(barrier, 5)
+
+
+class Halving:
+    AXES = ("x", "zh", "zl", "y")
+
+    def __init__(self, source, own, got, sems, order, rows):
+        self.source, self.own, self.got, self.sems, self.order, self.rows = source, own, got, sems, order, rows
+        self.at = place()
+
+    @staticmethod
+    def scratch(rows):
+        shapes = [(2, 2, 2, 2), (2, 2, 2, 2), (2, 2, 2), (2, 2), (2,), (1,)]
+        return [pltpu.VMEM(s + (rows, SHARD_COLS), BF16) for s in shapes] + [pltpu.SemaphoreType.DMA((11,))]
+
+    def first(self):
+        c = self.at["c"]
+        send, recv, local = self.sems.at[0], self.sems.at[1], self.sems.at[10]
+        for x in range(2):
+            for img in range(8):
+                spot = (x, img // 4, img // 2 % 2, img % 2)
+                pltpu.make_async_remote_copy(
+                    src_ref=self.source(x, img, 1 - c), dst_ref=self.got[0].at[spot], send_sem=send, recv_sem=recv,
+                    device_id=partner("c"), device_id_type=MESH,
+                ).start()
+                pltpu.make_async_copy(self.source(x, img, c), self.own.at[spot], local).start()
+
+    def first_done(self):
+        send, recv, local = self.sems.at[0], self.sems.at[1], self.sems.at[10]
+        whole = pltpu.make_async_remote_copy(
+            src_ref=self.got[0], dst_ref=self.got[0], send_sem=send, recv_sem=recv,
+            device_id=partner("c"), device_id_type=MESH,
+        )
+        whole.wait_send()
+        whole.wait_recv()
+        pltpu.make_async_copy(self.got[0], self.own, local).wait()
+
+        def add(i, _):
+            spot = (i // 8, i // 4 % 2, i // 2 % 2, i % 2)
+            self.own[spot] = (self.own[spot].astype(F32) + self.got[0][spot].astype(F32)).astype(BF16)
+            return 0
+
+        lax.fori_loop(0, 16, add, 0)
+
+    def index(self, k, dim=None):
+        spot = []
+        for axis in self.AXES:
+            if axis == dim:
+                spot.append(1 - self.at[axis])
+            elif axis in self.order[:k]:
+                spot.append(self.at[axis])
+            else:
+                spot.append(slice(None))
+        return tuple(spot)
+
+    def copy(self, k):
+        dim = self.order[k]
+        src = self.own.at[self.index(k, dim)]
+        dst = self.got[k + 1].at[0] if k == 3 else self.got[k + 1]
+        return pltpu.make_async_remote_copy(
+            src_ref=src, dst_ref=dst, send_sem=self.sems.at[2 + 2 * k], recv_sem=self.sems.at[3 + 2 * k],
+            device_id=partner(dim), device_id_type=MESH,
+        )
+
+    def step(self, k):
+        self.copy(k).start()
+
+    def step_done(self, k):
+        self.copy(k).wait()
+        done = self.order[: k + 1]
+        free = [axis for axis in self.AXES if axis not in done]
+        count = 2 ** len(free)
+
+        def add(i, _):
+            bits = {axis: (i // 2 ** (len(free) - 1 - j)) % 2 for j, axis in enumerate(free)}
+            spot = tuple(bits[axis] if axis in bits else self.at[axis] for axis in self.AXES)
+            self.own[spot] = (self.own[spot].astype(F32) + self.got[k + 1][tuple(bits[axis] for axis in free)].astype(F32)).astype(BF16)
+            return 0
+
+        if k < 3:
+            lax.fori_loop(0, count, add, 0)
+
+    def result(self):
+        spot = tuple(self.at[axis] for axis in self.AXES)
+        return self.own[spot].astype(F32) + self.got[4][0].astype(F32)
+
+
+def timeline(w, moments):
+    for when, bodies in moments.items():
+        @pl.when(w == when)
+        def _(bodies=bodies):
+            for body in bodies:
+                body()
+
+
 def attn_bwd_kernel(
-    meta_ref, qkv_ref, p_ref, inv_ref, att_ref, datt_ref, table_ref, kback_ref,
-    dqkv_ref, rel_ref, bias_ref,
+    meta_ref, qkv_ref, p_ref, inv_ref, att_ref, datt_ref, table_ref, kback_ref, *rest,
 ):
     w = pl.program_id(0)
+    if len(rest) == 3:
+        dqkv_ref, rel_ref, bias_ref = rest
+        streams = None
+    else:
+        fc1_ref, fc2_ref, dqkv_ref, rel_ref, bias_ref, sum1_ref, sum2_ref = rest[:7]
+        streams = []
+        for n, (ref, order) in enumerate(((fc1_ref, ("x", "y", "zh", "zl")), (fc2_ref, ("y", "zh", "zl", "x")))):
+            own, *got, sems = rest[7 + 7 * n : 14 + 7 * n]
+
+            def source(x, img, c, ref=ref):
+                row = pl.multiple_of((2 * x + c) * SHARD_ROWS, SHARD_ROWS)
+                return ref.at[pl.ds(row, SHARD_ROWS), pl.ds(img * SHARD_COLS, SHARD_COLS)]
+
+            streams.append(Halving(source, own, got, sems, order, SHARD_ROWS))
+        one, two = streams
+        timeline(
+            w,
+            {
+                0: [greet, one.first, two.first],
+                3: [one.first_done, lambda: one.step(0), two.first_done, lambda: two.step(0)],
+                9: [
+                    lambda: one.step_done(0), lambda: one.step(1), lambda: two.step_done(0), lambda: two.step(1),
+                ],
+                12: [lambda: one.step_done(1), lambda: one.step(2)],
+            },
+        )
 
     @pl.when(w == 0)
     def _():
@@ -364,10 +506,27 @@
         bias_ref[0, :, cols] += fold8(dq)
         bias_ref[1, :, cols] += fold8(dv)
 
-
-def attention_backward(meta, qkv, p, inv, att, datt, table, kback):
+    if streams:
+        @pl.when(w == pl.num_programs(0) - 1)
+        def _():
+            one.step_done(2)
+            one.step(3)
+            two.step_done(1)
+            two.step(2)
+            one.step_done(3)
+            sum1_ref[...] = one.result()
+            two.step_done(2)
+            two.step(3)
+            two.step_done(3)
+            sum2_ref[...] = two.result()
+
+
+def attention_backward(meta, qkv, p, inv, att, datt, table, kback, grads=()):
     cap = meta.shape[0]
     sds = jax.ShapeDtypeStruct
+    anywhere = pl.BlockSpec(memory_space=pl.ANY)
+    shard = (SHARD_ROWS, SHARD_COLS)
+    extra = dict(collective_id=1, has_side_effects=True) if grads else {}
     return pl.pallas_call(
         attn_bwd_kernel,
         grid_spec=pltpu.PrefetchScalarGridSpec(
@@ -376,13 +535,15 @@
             in_specs=[
                 per_window(TW, 3 * D), per_window(HEADS, TW, TW), per_window(TW, D), per_window(TW, D),
                 per_window(TW, D), whole((LANES, 256)), whole((TW, LANES)),
-            ],
-            out_specs=[per_window(TW, 3 * D), whole((LANES, 256)), whole((2, 8, D))],
+            ] + [anywhere] * len(grads),
+            out_specs=[per_window(TW, 3 * D), whole((LANES, 256)), whole((2, 8, D))] + [whole(shard)] * len(grads),
+            scratch_shapes=Halving.scratch(SHARD_ROWS) * len(grads),
         ),
-        out_shape=[sds((cap, TW, 3 * D), BF16), sds((LANES, 256), F32), sds((2, 8, D), F32)],
-        compiler_params=pltpu.CompilerParams(vmem_limit_bytes=VMEM_LIMIT),
+        out_shape=[sds((cap, TW, 3 * D), BF16), sds((LANES, 256), F32), sds((2, 8, D), F32)]
+        + [sds(shard, F32)] * len(grads),
+        compiler_params=pltpu.CompilerParams(vmem_limit_bytes=VMEM_LIMIT, **extra),
         cost_estimate=pl.CostEstimate(flops=60_000_000_000, bytes_accessed=80_000_000, transcendentals=0),
-    )(meta, qkv, p, inv, att, datt, table, kback)
+    )(meta, qkv, p, inv, att, datt, table, kback, *grads)
 
 
 def rel_from(acc):
@@ -615,11 +776,12 @@
     def weight_grad(left, right):
         return jnp.einsum("td,te->de", flat(left), flat(right), preferred_element_type=F32).astype(BF16)
 
+    fused = close and groups == 8
+    d_fc2 = weight_grad(g, act)
     d_fc1 = weight_grad(normed2, d_pre)
-    d_fc2 = weight_grad(act, g)
     d_proj = weight_grad(att, d_mixed)
-    d_qkv, rel_acc, bias_sums = attention_backward(
-        meta, qkv, probs, inv, att, d_att, rel_table(rels[0], rels[1], False), kback
+    d_qkv, rel_acc, bias_sums, *done = attention_backward(
+        meta, qkv, probs, inv, att, d_att, rel_table(rels[0], rels[1], False), kback, (d_fc1, d_fc2) if fused else ()
     )
     d_wqkv = weight_grad(normed1, d_qkv)
     in_ext, sums1 = last_norm(meta, d_qkv, wqkv, x, d_mixed, gain1, ext_rows)
@@ -629,6 +791,7 @@
         grad = lax.psum_scatter(grad, cols_axis, scatter_dimension=1, tiled=True)
         return lax.psum_scatter(grad, rows_axis, scatter_dimension=0, tiled=True).astype(F32)
 
+    g_fc1, g_fc2 = done if fused else (reduce(d_fc1, "band", "img"), reduce(d_fc2, "band", "img"))
     d_rel_rows, d_rel_cols = rel_from(rel_acc)
     total = lax.psum(
         (jnp.sum(sums1, 1), jnp.sum(bias_sums, 1), jnp.sum(sums, 1), jnp.sum(sum_fc1, 0), d_rel_rows, d_rel_cols), axes
@@ -656,9 +819,9 @@
         img_share(total[2][3]),
         img_share(total[2][1]),
         img_share(total[2][2]),
-        reduce(d_fc1, "band", "img"),
+        g_fc1,
         img_share(total[3]),
-        reduce(d_fc2, "img", "band"),
+        g_fc2.T,
         img_share(total[2][0]),
     )
 

time: 788 us -> 693 us (0.88)
  waiting for transfers between devices: 201 us -> 61.2 us
  Pallas kernels: 298 us -> 344 us
  other arithmetic: 62.4 us -> 74.4 us
  local copies, waits for them, and re-layouts: 80 us -> 68.7 us
    unnamed x14 -> x8, waiting for transfers between devices: 93.1 us -> 12.1 us
    pallas_call x1, Pallas kernels: 56 us -> 102 us  [attention_backward(): pl.pallas_call(attn_bwd_kernel, grid_spec=pltpu.PrefetchScalarGridSpec(nu...]
    reduce_scatter x3 -> x2, waiting for transfers between devices: 36.3 us -> 0.02 us  [reduce(): grad = lax.psum_scatter(grad, cols_axis, scatter_dimension=1, tiled=True)]
    reduce_scatter x1 -> x0, waiting for transfers between devices: 22.9 us -> none  [reduce(): lax.psum_scatter(grad, rows_axis, scatter_dimension=0, tiled=True)]
    unnamed x34 -> x50, local copies, waits for them, and re-layouts: 32.3 us -> 21.1 us
    select_n x2, other arithmetic: 5.73 us -> 14.7 us  [collect(): top = jnp.where(odd, from_core, jnp.stack([from_cross, zero]))]
  transfers between devices with their start and end apart: 18 -> 14, of which waited for: 7 -> 3; matrix products, arithmetic and copies ran while one was open for 23% -> 25% of each run, Pallas kernels for 21% -> 31%
where the time goes in v2:
time: 693 us; the launch traced here: 683 us
  Pallas kernels  344 us (50%)
  other arithmetic  74.4 us (11%)
  local copies, waits for them, and re-layouts  68.7 us (10%)
  matrix products  65.5 us (9%)
  waiting for transfers between devices  61.2 us (9%)
  blocking collectives  45 us (6%)
  between operations  15 us (2%)
  starting transfers between devices  9.39 us (1%)
    pallas_call x1, Pallas kernels, feed_forward(): pl.pallas_call(mlp_kernel, grid_spec=pltpu.PrefetchScalarGridSpec(num_sca...  131 us
    pallas_call x1, Pallas kernels, attention_backward(): pl.pallas_call(attn_bwd_kernel, grid_spec=pltpu.PrefetchScalarGridSpec(nu...  102 us
    dot_general x4, matrix products, weight_grad(): jnp.einsum('td,te->de', flat(left), flat(right), preferred_element_type=F32)  65.5 us
    pallas_call x1, Pallas kernels, attention_forward(): pl.pallas_call(fwd_kernel, grid_spec=pltpu.PrefetchScalarGridSpec(num_sca...  52 us
    psum x1, blocking collectives, shards(): lax.psum((jnp.sum(sums1, 1), jnp.sum(bias_sums, 1), jnp.sum(sums, 1), jnp...  45 us
    pallas_call x1, Pallas kernels, last_norm(): pl.pallas_call(last_kernel, grid_spec=pltpu.PrefetchScalarGridSpec(num_sc...  41.8 us
    all_gather x1, waiting for transfers between devices, shards(): lax.all_gather(jnp.concatenate([w_qkv, small], axis=0), axes, axis=0, til...  38.2 us
    unnamed x50, local copies, waits for them, and re-layouts  21.1 us
  transfers between devices with their start and end apart: 14, of which 3 were waited for; matrix products, arithmetic and copies ran while one was open for 25% of the time, Pallas kernels for 31%

profile of v2, /device:TPU:0, one launch (start us, length us, event | category | flops | bytes accessed | tf_op | source)
XLA Modules:
  0.0 683.4 jit_solution(2718236310181189898)
XLA Ops:
  10.0 6.1 concatenate.68
  19.1 4.2 slice_select_fusion.2
  46.7 38.2 %all-gather.8.cloned.1.call-done = bf16[32,200,288]{1,2,0:T(8,128)(2,1)} async-done(((bf16[1,200,288]{1,2,0:T(8,128)(2,1)}), bf16[32,200,288]{1,2,0:T(8,128)(2,1)}) %all-gather.8.cloned.1.call-update) | async-done | bytes 3686416 | tf_op jit(solution)/shard_map/all_gather | solution.py:726
  90.9 8.4 %copy.121 = bf16[8,4,192,288]{3,0,2,1:T(8,128)(2,1)} copy(bf16[8,4,192,288]{2,3,1,0:T(8,128)(2,1)} %bitcast.97) | data formatting | bytes 7077888
  99.3 8.0 %reshape.152.wqkv_ref = bf16[768,2304]{1,0:T(8,128)(2,1)} reshape(bf16[4,192,8,288]{3,2,1,0:T(8,128)(2,1)} %bitcast.85) | data formatting | bytes 7077888 | tf_op jit(solution)/shard_map/reshape | solution.py:731
  112.7 52.0 %shard_map.341 = (bf16[13,224,768]{2,1,0:T(8,128)(2,1)}, bf16[13,224,768]{2,1,0:T(8,128)(2,1)}, bf16[13,224,2304]{2,1,0:T(8,128)(2,1)}, bf16[13,12,224,224]{3,2,...) custom-call(s32[13,4]{1,0:T(8,128)} %pad_add_fusion.1.meta_ref, bf16[80,64,768]{2,1,0:T(8,128)(2,1)} %bitcast.99, ...), custom_call_target="tpu_custom_call" | custom-call | flops 40000000000 | bytes 80000000 | tf_op jit(solution)/shard_map/pallas_call | solution.py:204
  164.6 10.9 %all-gather.6.cloned.1.call-done = bf16[6144,864]{1,0:T(8,128)(2,1)} async-done(((bf16[192,864]{1,0:T(8,128)(2,1)}), bf16[6144,864]{1,0:T(8,128)(2,1)}) %all-gather.6.cloned.1.call-update) | async-done | bytes 10616848 | tf_op jit(solution)/shard_map/all_gather | solution.py:728
  175.6 7.9 %slice.256.ff_ref = bf16[8,768,768]{2,1,0:T(8,128)(2,1)} slice(bf16[8,768,864]{2,1,0:T(8,128)(2,1)} %bitcast.94), slice={[0:8], [0:768], [0:768]} | slice | bytes 18874368 | tf_op jit(solution)/shard_map/slice | solution.py:742
  187.2 131.4 %shard_map.342 = (bf16[13,224,768]{2,1,0:T(8,128)(2,1)}, bf16[13,224,768]{2,1,0:T(8,128)(2,1)}, bf16[13,224,768]{2,1,0:T(8,128)(2,1)}, bf16[13,224,3072]{2,1,0:T...) custom-call(s32[13,4]{1,0:T(8,128)} %pad_add_fusion.1.meta_ref, ...), custom_call_target="tpu_custom_call" | custom-call | flops 60000002048 | bytes 80000000 | tf_op jit(solution)/shard_map/pallas_call | solution.py:290
  318.6 8.6 %bitcast_convert_fusion.3 = bf16[768,768]{0,1:T(8,128)(2,1)} fusion(bf16[13,224,768]{2,1,0:T(8,128)(2,1)} %get-tuple-element.40.att_ref, bf16[13,224,768]{2,1,0:T(8,128)(2,1)} %get-tuple-element.51.dmix_ref), kind=kOutput, calls=%fused_computation.14 | convolution fusion | flops 3435724800 | bytes 10125312 | tf_op jit(solution)/shard_map/td,te->de/dot_general | solution.py:777
  327.3 20.9 %bitcast_convert_fusion.rest_1_ = bf16[768,3072]{1,0:T(8,128)(2,1)} fusion(bf16[13,224,768]{2,1,0:T(8,128)(2,1)} %get-tuple-element.48, bf16[13,224,3072]{2,1,0:T(8,128)(2,1)} %get-tuple-element.49), kind=kOutput, calls=%fused_computation.1 | convolution fusion | flops 13742899200 | bytes 27082752 | tf_op jit(solution)/shard_map/td,te->de/dot_general | solution.py:777
  348.2 18.9 %bitcast_convert_fusion.1.rest_0_ = bf16[768,3072]{1,0:T(8,128)(2,1)} fusion(bf16[13,224,768]{2,1,0:T(8,128)(2,1)} %get-tuple-element.46, bf16[13,224,3072]{2,1,0:T(8,128)(2,1)S(1)} %bitcast.112), kind=kOutput, calls=%fused_computation.2 | convolution fusion | flops 13742899200 | bytes 27082752 | tf_op jit(solution)/shard_map/td,te->de/dot_general | solution.py:777
  367.1 102.0 %shard_map.344 = (bf16[13,224,2304]{2,1,0:T(8,128)(2,1)}, f32[128,256]{1,0:T(8,128)}, f32[2,8,768]{2,1,0:T(8,128)}, f32[192,384]{1,0:T(8,128)}, f32[192,384]{1,0:T(8,128)}) custom-call(s32[13,4]{1,0:T(8,128)} %pad_add_fusion.1.meta_ref, bf16[13,224,2304]{2,1,0:T(8,128)(2,1)} %get-tuple-element.42.qkv_ref, ...), custom_call_target="tpu_custom_call" | custom-call | flops 60000002048 | bytes 80000000 | tf_op jit(solution)/shard_map/pallas_call | solution.py:530
  469.1 17.1 %bitcast_convert_fusion.2 = bf16[768,2304]{0,1:T(8,128)(2,1)} fusion(bf16[13,224,768]{2,1,0:T(8,128)(2,1)} %get-tuple-element.54, bf16[13,224,2304]{2,1,0:T(8,128)(2,1)} %get-tuple-element.50.dqkv_ref), kind=kOutput, calls=%fused_computation.5 | convolution fusion | flops 10307174400 | bytes 21430272 | tf_op jit(solution)/shard_map/td,te->de/dot_general | solution.py:777
  488.5 41.8 %shard_map.345 = (bf16[80,64,768]{2,1,0:T(8,128)(2,1)}, f32[2,8,768]{2,1,0:T(8,128)}) custom-call(s32[13,4]{1,0:T(8,128)} %pad_add_fusion.1.meta_ref, bf16[13,224,2304]{2,1,0:T(8,128)(2,1)} %get-tuple-element.50.dqkv_ref, bf16[768,2304]{1,0:T(8,128)(2,1)} %reshape.152.wqkv_ref, bf16[13,224,768]{2,1,0:T(8,128)(2,1)} %get-tuple-element.39.x_ref, ...), custom_call_target="tpu_custom_call" | custom-call | flops 15000000512 | bytes 30000000 | tf_op jit(solution)/shard_map/pallas_call | solution.py:635
  535.6 4.0 slice_select_fusion
  542.3 17.1 %shard_map.343 = bf16[80,64,768]{2,1,0:T(8,128)(2,1)} custom-call(s32[13,4]{1,0:T(8,128)} %pad_add_fusion.1.meta_ref, bf16[13,224,768]{2,1,0:T(8,128)(2,1)} %get-tuple-element.41.y_ref), custom_call_target="tpu_custom_call" | custom-call | flops 5000000000 | bytes 20000000 | tf_op jit(solution)/shard_map/pallas_call | solution.py:587
  562.8 4.1 slice_select_fusion.1
  568.0 45.0 %all-reduce.16 = (f32[2,768]{1,0:T(2,128)}, f32[2,768]{1,0:T(2,128)}, f32[27,64]{0,1:T(8,128)}, f32[27,64]{0,1:T(8,128)}, f32[4,768]{1,0:T(4,128)}, /*index=5*/f32[3072]{0:T(1024)}) all-reduce(f32[2,768]{1,0:T(2,128)} %reduce_sum.36, f32[2,768]{1,0:T(2,128)} %reduce_sum.37, ...), channel_id=1, replica_groups=mesh['img'=8,'band'=4] {'img','band'}, use_global_device_ids=true, to_apply=%region_1.2 | all-reduce | flops 12672 | bytes 101376 | tf_op jit(solution)/shard_map/psum | solution.py:796
  627.8 8.1 %convert_select_fusion.1 = (f32[2,12,64,768]{3,2,1,0:T(8,128)}, f32[2,12,64,768]{3,2,1,0:T(8,128)}) fusion(bf16[2,12,64,768]{3,2,1,0:T(8,128)(2,1)} %collective-permute-done.6, f32[1,12,64,768]{3,2,1,0:T(8,128)} %bitcast_convert_fusion.4, pred[]{:T(512)S(6)} %eq.13), kind=kLoop, calls=%fused_computation.9 | loop fusion | flops 3538944 | bytes 14155777 | tf_op jit(solution)/shard_map/jit(_where)/select_n | solution.py:701
  635.9 6.6 convert_select_fusion.3
  644.6 7.0 %add_convert_fusion = bf16[2,16,64,768]{3,2,1,0:T(8,128)(2,1)} fusion(f32[2,12,64,768]{3,2,1,0:T(8,128)} %get-tuple-element.166, f32[2,12,64,768]{3,2,1,0:T(8,128)} %get-tuple-element.165, bf16[2,40,64,768]{3,2,1,0:T(8,128)(2,1)} %bitcast.93), kind=kLoop, calls=%fused_computation.7 | loop fusion | flops 6291456 | bytes 15728640 | tf_op jit(solution)/shard_map/convert_element_type | solution.py:771
  651.7 7.5 %pad_add_fusion = f32[2,16,64,768]{3,2,1,0:T(8,128)} fusion(f32[2,12,64,768]{3,2,1,0:T(8,128)} %get-tuple-element.164, f32[2,12,64,768]{3,2,1,0:T(8,128)S(1)} %bitcast.87, bf16[2,40,64,768]{3,2,1,0:T(8,128)(2,1)} %bitcast.90), kind=kLoop, calls=%fused_computation.6 | loop fusion | flops 4718592 | bytes 18874368 | tf_op jit(solution)/shard_map/add | solution.py:705
  660.9 12.0 %reduce-scatter.13.cloned.1.call-done = bf16[192,288]{1,0:T(8,128)(2,1)} async-done(((bf16[768,288]{1,0:T(8,128)(2,1)}), bf16[192,288]{1,0:T(8,128)(2,1)}) %reduce-scatter.13.cloned.1.call-update) | async-done | bytes 110608
  (164 shorter events, 80.7 us)
Async XLA Ops:
  7.2 25.4 %copy-start = (s32[2,2]{1,0:T(2,128)S(1)}, s32[2,2]{1,0:T(2,128)}, u32[]{:S(2)}) copy-start(s32[2,2]{1,0:T(2,128)} %param.23) | copy-start | bytes 52
  7.2 77.7 %all-gather.8.cloned.1.call-start = ((), (), s32[]{:S(2)}) async-start(), calls=%async_computation.7 | async-start | bytes 4866048 | tf_op jit(solution)/shard_map/all_gather | solution.py:726
  17.2 158.4 %all-gather.6.cloned.1.call-start = ((), (), s32[]{:S(2)}) async-start(), calls=%async_computation.6 | async-start | bytes 11354112 | tf_op jit(solution)/shard_map/all_gather | solution.py:728
  19.0 607.0 %reduce-scatter.11.cloned.1.call-start = ((), (), s32[]{:S(2)}) async-start(), calls=%async_computation.5 | async-start | bytes 1327104 | tf_op jit(solution)/shard_map/reduce_scatter | solution.py:791
  23.3 10.6 %collective-permute-start.2 = (bf16[2,12,64,768]{3,2,1,0:T(8,128)(2,1)}, bf16[2,12,64,768]{3,2,1,0:T(8,128)(2,1)}, u32[]{:S(2)}, u32[]{:S(2)}) collective-permute-start(bf16[2,12,64,768]{3,2,1,0:T(8,128)(2,1)} %slice_select_fusion.2), channel_id=1, source_target_pairs={{0,1},{1,0},{2,3},{3,2},{4,5},{5,4},{6,7},{7,6},{8,9},{9,8},{10,11... | collective-permute-start | bytes 7077896 | tf_op jit(solution)/shard_map/ppermute | solution.py:685
  25.4 11.2 %collective-permute-start = (bf16[2,12,64,768]{3,2,1,0:T(8,128)(2,1)}, bf16[2,12,64,768]{3,2,1,0:T(8,128)(2,1)}, u32[]{:S(2)}, u32[]{:S(2)}) collective-permute-start(bf16[2,12,64,768]{3,2,1,0:T(8,128)(2,1)} %slice_select_fusion.3), channel_id=1, source_target_pairs={{0,1},{1,0},{2,3},{3,2},{4,5},{5,4},{6,7},{7,6},{8,9},{9,8},{10,11... | collective-permute-start | bytes 7077896 | tf_op jit(solution)/shard_map/ppermute | solution.py:685
  27.0 7.0 %collective-permute-start.3 = (bf16[12,64,768]{2,1,0:T(8,128)(2,1)}, bf16[12,64,768]{2,1,0:T(8,128)(2,1)}, u32[]{:S(2)}, u32[]{:S(2)}) collective-permute-start(bf16[12,64,768]{2,1,0:T(8,128)(2,1)} %select_bitcast_fusion), channel_id=1, source_target_pairs={{1,2},{2,1},{5,6},{6,5},{9,10},{10,9},{13,14},{14,13},{17,18},{18,... | collective-permute-start | bytes 3538952 | tf_op jit(solution)/shard_map/ppermute | solution.py:686
  29.8 6.7 collective-permute-start.1
  327.1 21.0 %slice-start.2 = ((s8[17891328]{0:T(1024)(128)(4,1)}), s8[1114112]{0:T(1024)(128)(4,1)S(1)}, s32[]{:S(2)}) async-start(s8[17891328]{0:T(1024)(128)(4,1)} %bitcast.111), calls=%async_computation.12 | async-start | bytes 2228224
  327.2 315.3 %reduce-scatter.9.cloned.1.call-start = ((), (), s32[]{:S(2)}) async-start(), calls=%async_computation.4 | async-start | bytes 3981312 | tf_op jit(solution)/shard_map/reduce_scatter | solution.py:791
  327.2 21.0 %slice-start.3 = ((s8[17891328]{0:T(1024)(128)(4,1)}), s8[4194304]{0:T(1024)(128)(4,1)S(1)}, s32[]{:S(2)}) async-start(s8[17891328]{0:T(1024)(128)(4,1)} %bitcast.111), calls=%async_computation.13 | async-start | bytes 8388608
  327.2 20.9 %slice-start.4 = ((s8[17891328]{0:T(1024)(128)(4,1)}), s8[4194304]{0:T(1024)(128)(4,1)S(1)}, s32[]{:S(2)}) async-start(s8[17891328]{0:T(1024)(128)(4,1)} %bitcast.111), calls=%async_computation.14 | async-start | bytes 8388608
  486.2 173.0 %reduce-scatter.15.cloned.1.call-start = ((), (), s32[]{:S(2)}) async-start(), calls=%async_computation.9 | async-start | bytes 245760
  488.5 43.2 %copy-start.10 = (f32[2,8,768]{2,1,0:T(8,128)S(1)}, f32[2,8,768]{2,1,0:T(8,128)}, u32[]{:S(2)}) copy-start(f32[2,8,768]{2,1,0:T(8,128)} %get-tuple-element.55) | copy-start | bytes 147460
  488.5 43.9 %copy-start.9 = (f32[4,8,768]{2,1,0:T(8,128)S(1)}, f32[4,8,768]{2,1,0:T(8,128)}, u32[]{:S(2)}) copy-start(f32[4,8,768]{2,1,0:T(8,128)} %get-tuple-element.57) | copy-start | bytes 294916
  488.5 43.9 %copy-start.8 = (f32[8,3072]{1,0:T(8,128)S(1)}, f32[8,3072]{1,0:T(8,128)}, u32[]{:S(2)}) copy-start(f32[8,3072]{1,0:T(8,128)} %get-tuple-element.59) | copy-start | bytes 294916
  534.8 89.2 %collective-permute-start.7 = (bf16[12,64,768]{2,1,0:T(8,128)(2,1)S(1)}, bf16[12,64,768]{2,1,0:T(8,128)(2,1)S(1)}, u32[]{:S(2)}, u32[]{:S(2)}) collective-permute-start(bf16[12,64,768]{2,1,0:T(8,128)(2,1)S(1)} %fusion), channel_id=1, source_target_pairs={{1,2},{2,1},{5,6},{6,5},{9,10},{10,9},{13,14},{14,13},{17,18},{18,... | collective-permute-start | bytes 3538952 | tf_op jit(solution)/shard_map/ppermute | solution.py:699
  539.6 88.2 %collective-permute-start.6 = (bf16[2,12,64,768]{3,2,1,0:T(8,128)(2,1)}, bf16[2,12,64,768]{3,2,1,0:T(8,128)(2,1)}, u32[]{:S(2)}, u32[]{:S(2)}) collective-permute-start(bf16[2,12,64,768]{3,2,1,0:T(8,128)(2,1)} %slice_select_fusion), channel_id=1, source_target_pairs={{0,1},{1,0},{2,3},{3,2},{4,5},{5,4},{6,7},{7,6},{8,9},{9,8},{10,11... | collective-permute-start | bytes 7077896 | tf_op jit(solution)/shard_map/ppermute | solution.py:698
  562.1 63.6 %collective-permute-start.5 = (bf16[12,64,768]{2,1,0:T(8,128)(2,1)}, bf16[12,64,768]{2,1,0:T(8,128)(2,1)S(1)}, u32[]{:S(2)}, u32[]{:S(2)}) collective-permute-start(bf16[12,64,768]{2,1,0:T(8,128)(2,1)} %fusion.1), channel_id=1, source_target_pairs={{1,2},{2,1},{5,6},{6,5},{9,10},{10,9},{13,14},{14,13},{17,18},{18,... | collective-permute-start | bytes 3538952 | tf_op jit(solution)/shard_map/ppermute | solution.py:699
  566.9 69.0 %collective-permute-start.4 = (bf16[2,12,64,768]{3,2,1,0:T(8,128)(2,1)}, bf16[2,12,64,768]{3,2,1,0:T(8,128)(2,1)}, u32[]{:S(2)}, u32[]{:S(2)}) collective-permute-start(bf16[2,12,64,768]{3,2,1,0:T(8,128)(2,1)} %slice_select_fusion.1), channel_id=1, source_target_pairs={{0,1},{1,0},{2,3},{3,2},{4,5},{5,4},{6,7},{7,6},{8,9},{9,8},{10,11... | collective-permute-start | bytes 7077896 | tf_op jit(solution)/shard_map/ppermute | solution.py:698
  627.8 45.1 %reduce-scatter.13.cloned.1.call-start = ((), (), s32[]{:S(2)}) async-start(), calls=%async_computation.8 | async-start | bytes 737280
  651.7 23.0 %copy-start.6 = (f32[192,384]{1,0:T(8,128)S(1)}, f32[192,384]{1,0:T(8,128)}, u32[]{:S(2)}) copy-start(f32[192,384]{1,0:T(8,128)} %get-tuple-element.220) | copy-start | bytes 884740
  651.7 23.7 %copy-start.5 = (f32[192,384]{1,0:T(8,128)S(1)}, f32[192,384]{1,0:T(8,128)}, u32[]{:S(2)}) copy-start(f32[192,384]{1,0:T(8,128)} %get-tuple-element.60) | copy-start | bytes 884740
  651.7 24.4 %copy-start.1 = (s32[2,2]{1,0:T(2,128)S(1)}, s32[2,2]{1,0:T(2,128)}, u32[]{:S(2)}) copy-start(s32[2,2]{1,0:T(2,128)} %param.23) | copy-start | bytes 52
  (8 other events, 67.8 us)
Sparse Core Ops, SparseCore 0:
  17.3 67.5 all-gather.7
  87.8 87.7 all-gather.5
  327.3 62.4 reduce-scatter.10
  486.4 78.2 reduce-scatter.8
  627.9 20.4 reduce-scatter.14
  650.8 22.0 reduce-scatter.12

commit v3 on v2

--- a/solution.py
+++ b/solution.py
@@ -284,7 +284,7 @@
     datt_ref[...] = mm_nt(dmix, wproj_ref[...]).astype(BF16)
 
 
-def feed_forward(meta, gext, x, att, wproj, pbias, gain, shift, ff, b1, b2):
+def feed_forward(meta, gext, x, att, wproj, pbias, gain, shift, ff, b1, b2, spare):
     cap = meta.shape[0]
     sds = jax.ShapeDtypeStruct
     return pl.pallas_call(
@@ -303,7 +303,7 @@
             scratch_shapes=[pltpu.VMEM((TW, D), F32), pltpu.VMEM((TW, D), F32)],
         ),
         out_shape=[
-            sds((cap, TW, D), BF16), sds((cap, TW, D), BF16), sds((cap, TW, D), BF16), sds((cap, TW, FF), BF16),
+            sds((cap + spare, TW, D), BF16), sds((cap, TW, D), BF16), sds((cap, TW, D), BF16), sds((cap, TW, FF), BF16),
             sds((cap, TW, FF), BF16), sds((cap, TW, D), BF16), sds((cap, TW, D), BF16), sds((4, 8, D), F32),
             sds((8, FF), F32),
         ],
@@ -330,11 +330,17 @@
     return (img, band + move) if dim in ("x", "c") else (img + move, band)
 
 
+def peers():
+    img, band = lax.axis_index("img"), lax.axis_index("band")
+    return [(img, (band + d) % 4) for d in range(1, 4)], [((img + d) % 8, band) for d in range(1, 8)]
+
+
 def greet():
     barrier = pltpu.get_barrier_semaphore()
-    for dim in ("c", "x", "y", "zh", "zl"):
-        pl.semaphore_signal(barrier, inc=1, device_id=partner(dim), device_id_type=MESH)
-    pl.semaphore_wait(barrier, 5)
+    near_by, far = peers()
+    for device in near_by + far:
+        pl.semaphore_signal(barrier, inc=1, device_id=device, device_id_type=MESH)
+    pl.semaphore_wait(barrier, 10)
 
 
 class Halving:
@@ -421,12 +427,74 @@
         return self.own[spot].astype(F32) + self.got[4][0].astype(F32)
 
 
+ORDERS = (("x", "y", "zh", "zl"), ("y", "x", "zh", "zl"))
+
+
 def timeline(w, moments):
     for when, bodies in moments.items():
         @pl.when(w == when)
         def _(bodies=bodies):
             for body in bodies:
                 body()
+
+
+NEAR_CORE = 7
+NEAR_CROSS = 5
+CROSS_ROWS = 160
+
+
+class Homeward:
+    def __init__(self, windows, everything, sems):
+        self.windows, self.all, self.sems = windows, everything, sems
+        self.cap = everything.shape[0] - NEAR_CORE - NEAR_CROSS
+        self.band = lax.axis_index("band")
+
+    def inner(self):
+        return (self.band == 1) | (self.band == 2)
+
+    def outer(self):
+        return (self.band == 0) | (self.band == 3)
+
+    def keep(self):
+        return pltpu.make_async_copy(self.windows, self.all.at[pl.ds(0, self.cap)], self.sems.at[4])
+
+    def to_core(self, first, count):
+        return pltpu.make_async_remote_copy(
+            src_ref=self.windows.at[pl.ds(first, count)], dst_ref=self.all.at[pl.ds(self.cap, count)],
+            send_sem=self.sems.at[0], recv_sem=self.sems.at[1], device_id=partner("c"), device_id_type=MESH,
+        )
+
+    def to_cross(self, sending):
+        img = lax.axis_index("img")
+        skip = (2 - self.band) if sending else (self.band - 1)
+        rows = pl.ds(pl.multiple_of(skip * (TW - CROSS_ROWS), TW - CROSS_ROWS), CROSS_ROWS)
+        return pltpu.make_async_remote_copy(
+            src_ref=self.windows.at[pl.ds(0, NEAR_CROSS), rows],
+            dst_ref=self.all.at[pl.ds(self.cap + NEAR_CORE, NEAR_CROSS), rows],
+            send_sem=self.sems.at[2], recv_sem=self.sems.at[3], device_id=(img, 3 - self.band), device_id_type=MESH,
+        )
+
+    def send_cross(self):
+        pl.when(self.inner())(lambda: self.to_cross(True).start())
+
+    def send_core_inner(self):
+        pl.when(self.inner())(lambda: self.to_core(NEAR_CROSS, NEAR_CORE).start())
+
+    def send_core_outer(self):
+        pl.when(self.outer())(lambda: self.to_core(0, 3).start())
+
+    def finish(self):
+        @pl.when(self.inner())
+        def _():
+            self.to_core(NEAR_CROSS, NEAR_CORE).wait_send()
+            self.to_core(0, 3).wait_recv()
+            self.to_cross(True).wait_send()
+            self.to_cross(False).wait_recv()
+
+        @pl.when(self.outer())
+        def _():
+            self.to_core(0, 3).wait_send()
+            self.to_core(NEAR_CROSS, NEAR_CORE).wait_recv()
 
 
 def attn_bwd_kernel(
@@ -437,26 +505,41 @@
         dqkv_ref, rel_ref, bias_ref = rest
         streams = None
     else:
-        fc1_ref, fc2_ref, dqkv_ref, rel_ref, bias_ref, sum1_ref, sum2_ref = rest[:7]
+        fc1_ref, fc2_ref, _, dqkv_ref, rel_ref, bias_ref, sum1_ref, sum2_ref, all_ref = rest[:9]
+        half = SHARD_ROWS // 2
         streams = []
-        for n, (ref, order) in enumerate(((fc1_ref, ("x", "y", "zh", "zl")), (fc2_ref, ("y", "zh", "zl", "x")))):
-            own, *got, sems = rest[7 + 7 * n : 14 + 7 * n]
-
-            def source(x, img, c, ref=ref):
-                row = pl.multiple_of((2 * x + c) * SHARD_ROWS, SHARD_ROWS)
-                return ref.at[pl.ds(row, SHARD_ROWS), pl.ds(img * SHARD_COLS, SHARD_COLS)]
-
-            streams.append(Halving(source, own, got, sems, order, SHARD_ROWS))
-        one, two = streams
+        for n in range(4):
+            own, *got, sems = rest[9 + 7 * n : 16 + 7 * n]
+
+            def source(x, img, c, ref=(fc1_ref, fc2_ref)[n // 2], n=n):
+                row = pl.multiple_of((2 * x + c) * SHARD_ROWS + n % 2 * half, half)
+                return ref.at[pl.ds(row, half), pl.ds(img * SHARD_COLS, SHARD_COLS)]
+
+            streams.append(Halving(source, own, got, sems, ORDERS[n % 2], half))
+        ones, twos = streams[:2], streams[2:]
+        back = Homeward(all_ref, all_ref, rest[37])
+
+        def each(group, name, *args):
+            def body():
+                for stream in group:
+                    getattr(stream, name)(*args)
+            return body
+
         timeline(
             w,
             {
-                0: [greet, one.first, two.first],
-                3: [one.first_done, lambda: one.step(0), two.first_done, lambda: two.step(0)],
-                9: [
-                    lambda: one.step_done(0), lambda: one.step(1), lambda: two.step_done(0), lambda: two.step(1),
+                0: [greet, each(streams, "first")],
+                2: [
+                    each(ones, "first_done"), each(ones, "step", 0), each(twos, "first_done"),
+                    back.send_core_inner, back.send_core_outer,
                 ],
-                12: [lambda: one.step_done(1), lambda: one.step(2)],
+                5: [each(ones, "step_done", 0), each(ones, "step", 1)],
+                7: [each(ones, "step_done", 1), each(ones, "step", 2), each(twos, "step", 0)],
+                10: [
+                    each(ones, "step_done", 2), each(ones, "step", 3), each(twos, "step_done", 0), each(twos, "step", 1),
+                    back.send_cross,
+                ],
+                12: [each(ones, "step_done", 3), each(twos, "step_done", 1), each(twos, "step", 2)],
             },
         )
 
@@ -509,41 +592,44 @@
     if streams:
         @pl.when(w == pl.num_programs(0) - 1)
         def _():
-            one.step_done(2)
-            one.step(3)
-            two.step_done(1)
-            two.step(2)
-            one.step_done(3)
-            sum1_ref[...] = one.result()
-            two.step_done(2)
-            two.step(3)
-            two.step_done(3)
-            sum2_ref[...] = two.result()
-
-
-def attention_backward(meta, qkv, p, inv, att, datt, table, kback, grads=()):
+            sum1_ref[:half] = ones[0].result()
+            sum1_ref[half:] = ones[1].result()
+            each(twos, "step_done", 2)()
+            each(twos, "step", 3)()
+            back.finish()
+            each(twos, "step_done", 3)()
+            sum2_ref[:half] = twos[0].result()
+            sum2_ref[half:] = twos[1].result()
+
+
+def attention_backward(meta, qkv, p, inv, att, datt, table, kback, beside=()):
     cap = meta.shape[0]
     sds = jax.ShapeDtypeStruct
     anywhere = pl.BlockSpec(memory_space=pl.ANY)
     shard = (SHARD_ROWS, SHARD_COLS)
-    extra = dict(collective_id=1, has_side_effects=True) if grads else {}
+    more_specs, more_outs, scratch, extra = [], [], [], {}
+    if beside:
+        more_specs = [whole(shard), whole(shard), anywhere]
+        more_outs = [sds(shard, F32), sds(shard, F32), sds((cap + NEAR_CORE + NEAR_CROSS, TW, D), BF16)]
+        scratch = Halving.scratch(SHARD_ROWS // 2) * 4 + [pltpu.SemaphoreType.DMA((5,))]
+        extra = dict(collective_id=1, has_side_effects=True)
     return pl.pallas_call(
         attn_bwd_kernel,
+        input_output_aliases={10: 5} if beside else {},
         grid_spec=pltpu.PrefetchScalarGridSpec(
             num_scalar_prefetch=1,
             grid=(cap,),
             in_specs=[
                 per_window(TW, 3 * D), per_window(HEADS, TW, TW), per_window(TW, D), per_window(TW, D),
                 per_window(TW, D), whole((LANES, 256)), whole((TW, LANES)),
-            ] + [anywhere] * len(grads),
-            out_specs=[per_window(TW, 3 * D), whole((LANES, 256)), whole((2, 8, D))] + [whole(shard)] * len(grads),
-            scratch_shapes=Halving.scratch(SHARD_ROWS) * len(grads),
+            ] + [anywhere] * len(beside),
+            out_specs=[per_window(TW, 3 * D), whole((LANES, 256)), whole((2, 8, D))] + more_specs,
+            scratch_shapes=scratch,
         ),
-        out_shape=[sds((cap, TW, 3 * D), BF16), sds((LANES, 256), F32), sds((2, 8, D), F32)]
-        + [sds(shard, F32)] * len(grads),
+        out_shape=[sds((cap, TW, 3 * D), BF16), sds((LANES, 256), F32), sds((2, 8, D), F32)] + more_outs,
         compiler_params=pltpu.CompilerParams(vmem_limit_bytes=VMEM_LIMIT, **extra),
         cost_estimate=pl.CostEstimate(flops=60_000_000_000, bytes_accessed=80_000_000, transcendentals=0),
-    )(meta, qkv, p, inv, att, datt, table, kback, *grads)
+    )(meta, qkv, p, inv, att, datt, table, kback, *beside)
 
 
 def rel_from(acc):
@@ -562,7 +648,7 @@
         part = lax.dot_general(
             picks[t, : 64 * n], y[t], (((0,), (0,)), ((), ())), preferred_element_type=F32
         )
-        acc_ref[pl.ds(row0 + 4 * q, n)] += part.reshape(n, SIDE, D)
+        acc_ref[pl.ds(row0 + 4 * q, n)] += part.reshape(n, SIDE, D).astype(acc_ref.dtype)
 
 
 def scatter_kernel(meta_ref, y_ref, ext_ref, acc_ref):
@@ -649,17 +735,252 @@
     )(meta, dqkv, wqkv, x, dmix, gain)
 
 
+class SmallSum:
+    def __init__(self, mine, got_band, got_img, sems):
+        self.mine, self.got, self.sems = mine, (got_band, got_img), sems
+
+    @staticmethod
+    def scratch(shape):
+        return [
+            pltpu.VMEM(shape, F32), pltpu.VMEM((3,) + shape, F32), pltpu.VMEM((7,) + shape, F32),
+            pltpu.SemaphoreType.DMA((2, 2, 7)),
+        ]
+
+    def copies(self, k):
+        return [
+            pltpu.make_async_remote_copy(
+                src_ref=self.mine, dst_ref=self.got[k].at[d], send_sem=self.sems.at[k, 0, d],
+                recv_sem=self.sems.at[k, 1, d], device_id=device, device_id_type=MESH,
+            )
+            for d, device in enumerate(peers()[k])
+        ]
+
+    def send(self, k):
+        for copy in self.copies(k):
+            copy.start()
+
+    def add(self, k):
+        copies = self.copies(k)
+        for copy in copies:
+            copy.wait()
+        total = self.mine[...]
+        for d in range(len(copies)):
+            total = total + self.got[k][d]
+        self.mine[...] = total
+
+
+HOME_ROWS = 8
+
+
+def home_kernel(table_ref, *refs):
+    arrays = len(refs) // 2
+    step = pl.program_id(0)
+    per_image = pl.num_programs(0) // 2
+    m = step // per_image
+    top, left = table_ref[m, 25], table_ref[m, 26]
+    first = table_ref[m, 27] + (step - m * per_image) * HOME_ROWS
+    col = iota((SIDE, GRID * STRIDE), 0) + left
+    spot = iota((SIDE, GRID * STRIDE), 1)
+    picks = jnp.where((spot >> 4) * WIN + (spot & 15) == col, 1.0, 0.0)
+    picks = jnp.where((spot & 15) < WIN, picks, 0.0).astype(BF16)
+    for i in range(HOME_ROWS):
+        at = i + first + top
+        r = at // WIN
+        a = pl.multiple_of((at - r * WIN) * STRIDE, STRIDE)
+        slots = [table_ref[m, r * GRID + c] for c in range(GRID)]
+        for n in range(arrays):
+            tokens = jnp.concatenate([refs[n][slot, pl.ds(a, STRIDE)] for slot in slots], axis=0)
+            refs[arrays + n][0, i] = mm(picks, tokens).astype(refs[arrays + n].dtype)
+
+
+def home(table, sources, dtypes, rows):
+    per_image = rows // HOME_ROWS
+    return pl.pallas_call(
+        home_kernel,
+        grid_spec=pltpu.PrefetchScalarGridSpec(
+            num_scalar_prefetch=1,
+            grid=(2 * per_image,),
+            in_specs=[whole(a.shape) for a in sources],
+            out_specs=[
+                pl.BlockSpec((1, HOME_ROWS, SIDE, D), lambda w, meta: (w // per_image, w % per_image, 0, 0))
+                for _ in dtypes
+            ],
+        ),
+        out_shape=[jax.ShapeDtypeStruct((2, rows, SIDE, D), dtype) for dtype in dtypes],
+        compiler_params=pltpu.CompilerParams(vmem_limit_bytes=VMEM_LIMIT),
+        cost_estimate=pl.CostEstimate(flops=500_000_000, bytes_accessed=20_000_000, transcendentals=0),
+    )(table, *sources)
+
+
+def home_table(plan, offsets, band, band_rows):
+    own = np.full((4, 2, WINDOWS), 0, np.int32)
+    for b in range(4):
+        for slot, (m, w) in enumerate(plan[b]):
+            if w >= 0:
+                own[b, m, w] = slot
+        odd, cap = b % 2, len(plan[b])
+        mate = plan[b ^ 1]
+        sent = mate[:3] if (b ^ 1) in (0, 3) else mate[NEAR_CROSS : NEAR_CROSS + NEAR_CORE]
+        for slot, (m, w) in enumerate(sent):
+            own[b, m, w] = cap + slot
+        if b in (1, 2):
+            for slot, (m, w) in enumerate(plan[3 - b][:NEAR_CROSS]):
+                own[b, m, w] = cap + NEAR_CORE + slot
+    rows = jnp.asarray(own)[band]
+    first = jnp.full((2, 1), band_rows, jnp.int32) * band
+    return jnp.concatenate([rows, offsets.astype(jnp.int32), first, jnp.zeros((2, 4), jnp.int32)], axis=1)
+
+
+def last_fused_kernel(
+    meta_ref, dqkv_ref, wqkv_ref, x_ref, dmix_ref, gain_ref, q_ref, bias_ref, sums_ref, fc1_ref, rel_ref,
+    all_ref, shard_ref, total_ref, rels_ref, ln_ref,
+    grad_ref, ln_acc, *rest,
+):
+    w = pl.program_id(0)
+    end = pl.num_programs(0) - 1
+    half = SHARD_ROWS // 2
+    streams = []
+    for n, order in enumerate(ORDERS):
+        own, *got, sems = rest[7 * n : 7 * n + 7]
+
+        def source(x, img, c, n=n):
+            row = pl.multiple_of((2 * x + c) * SHARD_ROWS + n * half, half)
+            return q_ref.at[img, pl.ds(row, half)]
+
+        streams.append(Halving(source, own, got, sems, order, half))
+    one, two = streams
+    rest = rest[14:]
+    small, rel, ln = [SmallSum(*rest[4 * n : 4 * n + 4]) for n in range(3)]
+    back = Homeward(grad_ref, all_ref, rest[12])
+
+    def start():
+        greet()
+        one.first()
+        two.first()
+
+    def prepare():
+        for r in range(2):
+            small.mine[r : r + 1] = jnp.sum(bias_ref[r], axis=0, keepdims=True)
+        for r in range(4):
+            small.mine[2 + r : 3 + r] = jnp.sum(sums_ref[r], axis=0, keepdims=True)
+            small.mine[6 + r : 7 + r] = jnp.sum(fc1_ref[:, D * r : D * r + D], axis=0, keepdims=True)
+        small.mine[10:] = jnp.zeros((6, D), F32)
+        rel.mine[...] = rel_ref[:64] + pltpu.roll(rel_ref[64:], 192, 1)
+        small.send(0)
+        rel.send(0)
+        ln_acc[...] = jnp.zeros_like(ln_acc)
+
+    def done(k):
+        one.step_done(k)
+        two.step_done(k)
+
+    def step(k):
+        one.step(k)
+        two.step(k)
+
+    def first_done():
+        one.first_done()
+        two.first_done()
+        step(0)
+
+    def middle():
+        small.add(0)
+        rel.add(0)
+        small.send(1)
+        rel.send(1)
+
+    def finish():
+        small.add(1)
+        rel.add(1)
+        total_ref[...] = small.mine[...]
+        rels_ref[...] = rel.mine[...]
+
+    timeline(
+        w,
+        {
+            0: [start, prepare],
+            2: [first_done],
+            3: [middle, back.send_core_outer],
+            6: [lambda: done(0), lambda: step(1), finish],
+            8: [lambda: done(1), lambda: step(2), back.send_cross],
+            12: [lambda: done(2), lambda: step(3), back.send_core_inner],
+        },
+    )
+
+    target = token_target(meta_ref, w)
+    dn = jnp.zeros((TW, D), F32)
+    for c in range(3):
+        cols = slice(D * c, D * c + D)
+        dn = dn + mm_nt(dqkv_ref[:, cols], wqkv_ref[:, cols])
+    dn = jnp.where(target >= 0, dn, 0.0)
+    unit, inverse = norm(x_ref[...].astype(F32))
+    ln_acc[0] += fold8(dn * unit)
+    ln_acc[1] += fold8(dn)
+    grad = dmix_ref[...].astype(F32) + norm_back(dn, unit, inverse, gain_ref[...])
+    grad_ref[w] = grad.astype(BF16)
+
+    @pl.when(w == end)
+    def _():
+        back.keep().start()
+        ln.mine[0:1] = jnp.sum(ln_acc[0], axis=0, keepdims=True)
+        ln.mine[1:2] = jnp.sum(ln_acc[1], axis=0, keepdims=True)
+        ln.mine[2:] = jnp.zeros((6, D), F32)
+        ln.send(0)
+        done(3)
+        ln.add(0)
+        ln.send(1)
+        shard_ref[:half] = one.result()
+        shard_ref[half:] = two.result()
+        back.keep().wait()
+        back.finish()
+        ln.add(1)
+        ln_ref[...] = ln.mine[...]
+
+
+def last_fused(meta, dqkv, wqkv, x, dmix, gain, q_grad, bias_sums, sums, fc1_sum, rel_acc):
+    cap = meta.shape[0]
+    sds = jax.ShapeDtypeStruct
+    half = SHARD_ROWS // 2
+    anywhere = pl.BlockSpec(memory_space=pl.ANY)
+    sums_out = [((SHARD_ROWS, SHARD_COLS), F32), ((16, D), F32), ((64, 256), F32), ((8, D), F32)]
+    return pl.pallas_call(
+        last_fused_kernel,
+        grid_spec=pltpu.PrefetchScalarGridSpec(
+            num_scalar_prefetch=1,
+            grid=(cap,),
+            in_specs=[
+                per_window(TW, 3 * D), whole((D, 3 * D)), per_window(TW, D), per_window(TW, D), whole((1, D)),
+                anywhere, whole((2, 8, D)), whole((4, 8, D)), whole((8, FF)), whole((LANES, 256)),
+            ],
+            out_specs=[anywhere] + [whole(shape) for shape, _ in sums_out],
+            scratch_shapes=[pltpu.VMEM((cap, TW, D), BF16), pltpu.VMEM((2, 8, D), F32)]
+            + Halving.scratch(half) * 2
+            + SmallSum.scratch((16, D)) + SmallSum.scratch((64, 256)) + SmallSum.scratch((8, D))
+            + [pltpu.SemaphoreType.DMA((5,))],
+        ),
+        out_shape=[sds((cap + NEAR_CORE + NEAR_CROSS, TW, D), BF16)] + [sds(shape, dtype) for shape, dtype in sums_out],
+        compiler_params=pltpu.CompilerParams(vmem_limit_bytes=VMEM_LIMIT, collective_id=2, has_side_effects=True),
+        cost_estimate=pl.CostEstimate(flops=20_000_000_000, bytes_accessed=50_000_000, transcendentals=0),
+    )(meta, dqkv, wqkv, x, dmix, gain, q_grad, bias_sums, sums, fc1_sum, rel_acc)
+
+
 def window_plan(images, bands):
     lists = [[] for _ in range(bands)]
     if images == 2 and bands == 4:
-        cuts = ((0, 8, 15, 20, 25), (0, 5, 10, 17, 25))
+        spans = (
+            ((0, 5, 8), (0, 0, 5), (1, 0, 5)),
+            ((0, 10, 15), (0, 8, 10), (1, 5, 10)),
+            ((1, 10, 15), (1, 15, 17), (0, 15, 20)),
+            ((1, 17, 20), (1, 20, 25), (0, 20, 25)),
+        )
+        lists = [[(m, w) for m, first, last in row for w in range(first, last)] for row in spans]
     else:
         cuts = [
             [(WINDOWS * b + (bands - 1 if m % 2 else 0)) // bands for b in range(bands + 1)] for m in range(images)
         ]
-    for m in range(images):
-        for b in range(bands):
-            lists[b] += [(m, w) for w in range(cuts[m][b], min(cuts[m][b + 1], WINDOWS))]
+        for m in range(images):
+            for b in range(bands):
+                lists[b] += [(m, w) for w in range(cuts[m][b], min(cuts[m][b + 1], WINDOWS))]
     cap = max(len(item) for item in lists)
     return np.array([item + [(0, -1)] * (cap - len(item)) for item in lists], np.int32)
 
@@ -745,6 +1066,7 @@
     plan = jnp.asarray(window_plan(images, bands))[band]
     image, window = plan[:, 0], plan[:, 1]
     close = near(images, bands, band_rows)
+    fused = close and groups == 8
     ext_per = band_rows + 2 * HALO if close else bands * band_rows + 12
     base = band_rows * band - HALO if close else -6
     live = window >= 0
@@ -753,7 +1075,7 @@
     row = spot // GRID * WIN - offsets[:, 0]
     col = spot % GRID * WIN - offsets[:, 1]
     meta = jnp.stack(
-        [jnp.where(live, image * ext_per + row - base, 0), col, row, live.astype(jnp.int32)], axis=1
+        [jnp.where(live, image * ext_per + row - base, HALO), col, row, live.astype(jnp.int32)], axis=1
     ).astype(jnp.int32)
     cap = meta.shape[0]
     ext_rows = images * ext_per
@@ -765,37 +1087,54 @@
     )
     gext = extend(out_grad, band).reshape(ext_rows, SIDE, D)
     out_win, g, normed2, act, d_pre, d_mixed, d_att, sums, sum_fc1 = feed_forward(
-        meta, gext, x, att, wproj, pb, gain2, shift2, ff, fc1_shift, b2
+        meta, gext, x, att, wproj, pb, gain2, shift2, ff, fc1_shift, b2, NEAR_CORE + NEAR_CROSS if fused else 0
     )
-    out_ext = scatter(meta, out_win, ext_rows).reshape(images, ext_per, SIDE, D)
-    output = collect(out_ext, band, images, band_rows).astype(BF16)
-
     def flat(a):
         return a.reshape(cap * TW, a.shape[-1])
 
     def weight_grad(left, right):
         return jnp.einsum("td,te->de", flat(left), flat(right), preferred_element_type=F32).astype(BF16)
 
-    fused = close and groups == 8
     d_fc2 = weight_grad(g, act)
     d_fc1 = weight_grad(normed2, d_pre)
     d_proj = weight_grad(att, d_mixed)
     d_qkv, rel_acc, bias_sums, *done = attention_backward(
-        meta, qkv, probs, inv, att, d_att, rel_table(rels[0], rels[1], False), kback, (d_fc1, d_fc2) if fused else ()
+        meta, qkv, probs, inv, att, d_att, rel_table(rels[0], rels[1], False), kback,
+        (d_fc1, d_fc2, out_win) if fused else (),
     )
     d_wqkv = weight_grad(normed1, d_qkv)
-    in_ext, sums1 = last_norm(meta, d_qkv, wqkv, x, d_mixed, gain1, ext_rows)
-    input_grad = collect(in_ext.reshape(images, ext_per, SIDE, D), band, images, band_rows)
-
-    def reduce(grad, rows_axis, cols_axis):
-        grad = lax.psum_scatter(grad, cols_axis, scatter_dimension=1, tiled=True)
-        return lax.psum_scatter(grad, rows_axis, scatter_dimension=0, tiled=True).astype(F32)
-
-    g_fc1, g_fc2 = done if fused else (reduce(d_fc1, "band", "img"), reduce(d_fc2, "band", "img"))
-    d_rel_rows, d_rel_cols = rel_from(rel_acc)
-    total = lax.psum(
-        (jnp.sum(sums1, 1), jnp.sum(bias_sums, 1), jnp.sum(sums, 1), jnp.sum(sum_fc1, 0), d_rel_rows, d_rel_cols), axes
-    )
+
+    if fused:
+        q_grad = jnp.concatenate(
+            [d_wqkv.reshape(D, groups, wide), d_proj.reshape(D, groups, share)], axis=2
+        ).transpose(1, 0, 2)
+        g_fc1, g_fc2, all_out = done
+        all_grad, q_shard, total, rel_total, ln_total = last_fused(
+            meta, d_qkv, wqkv, x, d_mixed, gain1, q_grad, bias_sums, sums, sum_fc1, rel_acc
+        )
+        output, input_grad = home(
+            home_table(window_plan(images, bands), pad_offsets, band, band_rows), (all_out, all_grad), (BF16, F32),
+            band_rows,
+        )
+        g_qkv, g_proj = q_shard[:, :wide], q_shard[:, wide:]
+        ln_total = ln_total[:2]
+        bias_total, sum_total, fc1_total = total[:2], total[2:6], total[6:10].reshape(FF)
+        own = rel_total.reshape(HEAD, 2, LANES)[:, :, :RELS].transpose(1, 2, 0)
+        d_rel_rows, d_rel_cols = own[0][::-1], own[1]
+    else:
+        out_ext = scatter(meta, out_win, ext_rows).reshape(images, ext_per, SIDE, D)
+        output = collect(out_ext, band, images, band_rows).astype(BF16)
+        in_ext, sums1 = last_norm(meta, d_qkv, wqkv, x, d_mixed, gain1, ext_rows)
+        input_grad = collect(in_ext.reshape(images, ext_per, SIDE, D), band, images, band_rows)
+
+        def reduce(grad):
+            grad = lax.psum_scatter(grad, "img", scatter_dimension=1, tiled=True)
+            return lax.psum_scatter(grad, "band", scatter_dimension=0, tiled=True).astype(F32)
+
+        g_fc1, g_fc2, g_qkv, g_proj = reduce(d_fc1), reduce(d_fc2), reduce(d_wqkv), reduce(d_proj)
+        ln_total, bias_total, sum_total, fc1_total, d_rel_rows, d_rel_cols = lax.psum(
+            (jnp.sum(sums1, 1), jnp.sum(bias_sums, 1), jnp.sum(sums, 1), jnp.sum(sum_fc1, 0)) + rel_from(rel_acc), axes
+        )
 
     def img_share(vector):
         n = vector.shape[0] // groups
@@ -808,21 +1147,21 @@
     return (
         output,
         input_grad,
-        img_share(total[0][0]),
-        img_share(total[0][1]),
-        reduce(d_wqkv, "band", "img"),
-        img_share(total[1][0]),
-        img_share(total[1][1]),
-        band_share(total[4]),
-        band_share(total[5]),
-        reduce(d_proj, "band", "img"),
-        img_share(total[2][3]),
-        img_share(total[2][1]),
-        img_share(total[2][2]),
+        img_share(ln_total[0]),
+        img_share(ln_total[1]),
+        g_qkv,
+        img_share(bias_total[0]),
+        img_share(bias_total[1]),
+        band_share(d_rel_rows),
+        band_share(d_rel_cols),
+        g_proj,
+        img_share(sum_total[3]),
+        img_share(sum_total[1]),
+        img_share(sum_total[2]),
         g_fc1,
-        img_share(total[3]),
+        img_share(fc1_total),
         g_fc2.T,
-        img_share(total[2][0]),
+        img_share(sum_total[0]),
     )
 
 

time: 693 us -> 586 us (0.85)
  blocking collectives: 45 us -> 0 us
  other arithmetic: 74.4 us -> 36.1 us
  waiting for transfers between devices: 61.2 us -> 45.5 us
    psum x1 -> x0, blocking collectives: 45 us -> none  [shards(): lax.psum((jnp.sum(sums1, 1), jnp.sum(bias_sums, 1), jnp.sum(sums, 1), jnp...]
    select_n x7 -> x1, other arithmetic: 27.4 us -> 0.08 us  [shards(): jnp.where(live, image * ext_per + row - base, HALO)]
    unnamed x8 -> x2, waiting for transfers between devices: 12.1 us -> 0.03 us
    unnamed x50 -> x28, local copies, waits for them, and re-layouts: 21.1 us -> 13.3 us
    add x1 -> x0, other arithmetic: 7.51 us -> none  [collect(): own + jnp.pad(top, ((0, 0), (0, rest), (0, 0), (0, 0)))]
    convert_element_type x1 -> x0, other arithmetic: 7.05 us -> none  [shards(): output = collect(out_ext, band, images, band_rows).astype(BF16)]
  transfers between devices with their start and end apart: 14 -> 6, of which waited for: 3 -> 2; matrix products, arithmetic and copies ran while one was open for 25% -> 10% of each run, Pallas kernels for 31% -> 9%
where the time goes in v3:
time: 586 us; the launch traced here: 577 us
  Pallas kernels  344 us (59%)
  local copies, waits for them, and re-layouts  70.6 us (12%)
  matrix products  62.1 us (11%)
  waiting for transfers between devices  45.5 us (8%)
  other arithmetic  36.1 us (6%)
  between operations  14.6 us (2%)
    pallas_call x1, Pallas kernels, feed_forward(): pl.pallas_call(mlp_kernel, grid_spec=pltpu.PrefetchScalarGridSpec(num_sca...  131 us
    pallas_call x1, Pallas kernels, attention_backward(): pl.pallas_call(attn_bwd_kernel, input_output_aliases={10: 5} if beside el...  80.4 us
    pallas_call x1, Pallas kernels, last_fused(): pl.pallas_call(last_fused_kernel, grid_spec=pltpu.PrefetchScalarGridSpec(...  68.9 us
    dot_general x4, matrix products, weight_grad(): jnp.einsum('td,te->de', flat(left), flat(right), preferred_element_type=F32)  62.1 us
    pallas_call x1, Pallas kernels, attention_forward(): pl.pallas_call(fwd_kernel, grid_spec=pltpu.PrefetchScalarGridSpec(num_sca...  52 us
    all_gather x1, waiting for transfers between devices, shards(): lax.all_gather(jnp.concatenate([w_qkv, small], axis=0), axes, axis=0, til...  34.5 us
    unnamed x28, local copies, waits for them, and re-layouts  13.3 us
  transfers between devices with their start and end apart: 6, of which 2 were waited for; matrix products, arithmetic and copies ran while one was open for 10% of the time, Pallas kernels for 9%

profile of v3, /device:TPU:0, one launch (start us, length us, event | category | flops | bytes accessed | tf_op | source)
XLA Modules:
  0.0 576.5 jit_solution(9087460627095113323)
XLA Ops:
  10.0 6.1 %concatenate.74 = bf16[2016]{0:T(1024)(128)(2,1)S(1)} concatenate(bf16[96]{0:T(256)(128)(2,1)} %param.25, bf16[96]{0:T(256)(128)(2,1)} %param.26, bf16[96]{0:T(256)(128)(2,1)} %param.28, bf16[96]{0:T(256)(128)(2,1)} %param.29, bf16[96]{0:T(256)(128)(2,1)} %param.33, bf16[96]{0:T(256)(128)(2,1)} %param.34, bf16[96]{0:T(256)(128)(2,1)} %param.35, bf16[96]{0:T(256)(128)(2,1)} %param.39, ...), dimensions={0} | concatenate | bytes 8064 | tf_op jit(solution)/shard_map/concatenate | solution.py:1039
  19.0 4.0 slice_select_fusion.1
  23.5 4.2 slice_select_fusion
  37.3 2.7 pad_select_fusion.3
  40.0 2.6 pad_select_fusion.1
  42.7 3.8 pad_maximum_fusion
  46.5 3.8 pad_maximum_fusion.1
  50.3 34.5 %all-gather.8.cloned.1.call-done = bf16[32,200,288]{1,2,0:T(8,128)(2,1)} async-done(((bf16[1,200,288]{1,2,0:T(8,128)(2,1)}), bf16[32,200,288]{1,2,0:T(8,128)(2,1)}) %all-gather.8.cloned.1.call-update) | async-done | bytes 3686416 | tf_op jit(solution)/shard_map/all_gather | solution.py:1047
  90.9 8.4 %copy.124 = bf16[8,4,192,288]{3,0,2,1:T(8,128)(2,1)} copy(bf16[8,4,192,288]{2,3,1,0:T(8,128)(2,1)} %bitcast.88) | data formatting | bytes 7077888
  99.2 8.0 %reshape.154.wqkv_ref = bf16[768,2304]{1,0:T(8,128)(2,1)} reshape(bf16[4,192,8,288]{3,2,1,0:T(8,128)(2,1)} %bitcast.83) | data formatting | bytes 7077888 | tf_op jit(solution)/shard_map/reshape | solution.py:1052
  112.6 52.0 %shard_map.350 = (bf16[13,224,768]{2,1,0:T(8,128)(2,1)}, bf16[13,224,768]{2,1,0:T(8,128)(2,1)}, bf16[13,224,2304]{2,1,0:T(8,128)(2,1)}, bf16[13,12,224,224]{3,2,...) custom-call(s32[13,4]{1,0:T(8,128)} %pad_add_fusion.meta_ref, bf16[80,64,768]{2,1,0:T(8,128)(2,1)} %bitcast.90, ...), custom_call_target="tpu_custom_call" | custom-call | flops 40000000000 | bytes 80000000 | tf_op jit(solution)/shard_map/pallas_call | solution.py:204
  164.6 10.9 %all-gather.6.cloned.1.call-done = bf16[6144,864]{1,0:T(8,128)(2,1)} async-done(((bf16[192,864]{1,0:T(8,128)(2,1)}), bf16[6144,864]{1,0:T(8,128)(2,1)}) %all-gather.6.cloned.1.call-update) | async-done | bytes 10616848 | tf_op jit(solution)/shard_map/all_gather | solution.py:1049
  175.5 7.9 %slice.217.ff_ref = bf16[8,768,768]{2,1,0:T(8,128)(2,1)} slice(bf16[8,768,864]{2,1,0:T(8,128)(2,1)} %bitcast.85), slice={[0:8], [0:768], [0:768]} | slice | bytes 18874368 | tf_op jit(solution)/shard_map/slice | solution.py:1063
  187.1 131.2 %shard_map.351 = (bf16[25,224,768]{2,1,0:T(8,128)(2,1)}, bf16[13,224,768]{2,1,0:T(8,128)(2,1)}, bf16[13,224,768]{2,1,0:T(8,128)(2,1)}, bf16[13,224,3072]{2,1,0:T...) custom-call(s32[13,4]{1,0:T(8,128)} %pad_add_fusion.meta_ref, ...), custom_call_target="tpu_custom_call" | custom-call | flops 60000002048 | bytes 80000000 | tf_op jit(solution)/shard_map/pallas_call | solution.py:290
  318.3 21.2 %bitcast_convert_fusion.rest_1_ = bf16[768,3072]{1,0:T(8,128)(2,1)} fusion(bf16[13,224,768]{2,1,0:T(8,128)(2,1)} %get-tuple-element.53, bf16[13,224,3072]{2,1,0:T(8,128)(2,1)} %get-tuple-element.54), kind=kOutput, calls=%fused_computation.1 | convolution fusion | flops 13742899200 | bytes 27082752 | tf_op jit(solution)/shard_map/td,te->de/dot_general | solution.py:1096
  339.5 17.0 %bitcast_convert_fusion.1.rest_0_ = bf16[768,3072]{1,0:T(8,128)(2,1)} fusion(bf16[13,224,768]{2,1,0:T(8,128)(2,1)S(1)} %copy-done.8, bf16[13,224,3072]{2,1,0:T(8,128)(2,1)S(1)} %copy-done.7), kind=kOutput, calls=%fused_computation.2 | convolution fusion | flops 13742899200 | bytes 27082752 | tf_op jit(solution)/shard_map/td,te->de/dot_general | solution.py:1096
  356.5 80.4 %shard_map.352 = (bf16[13,224,2304]{2,1,0:T(8,128)(2,1)}, f32[128,256]{1,0:T(8,128)}, f32[2,8,768]{2,1,0:T(8,128)}, f32[192,384]{1,0:T(8,128)}, f32[192,384]{1,0:T(8,128)}, /*index=5*/bf16[25,224,768]{2,1,0:T(8,128)(2,1)}) custom-call(s32[13,4]{1,0:T(8,128)} %pad_add_fusion.meta_ref, ...), custom_call_target="tpu_custom_call", output_to_operand_aliasing={{5}: (10, {})} | custom-call | flops 60000002048 | bytes 80000000 | tf_op jit(solution)/shard_map/pallas_call | solution.py:616
  436.9 16.4 %bitcast_convert_fusion.2 = bf16[768,2304]{1,0:T(8,128)(2,1)} fusion(bf16[13,224,768]{2,1,0:T(8,128)(2,1)} %get-tuple-element.59, bf16[13,224,2304]{2,1,0:T(8,128)(2,1)} %get-tuple-element.57.dqkv_ref), kind=kOutput, calls=%fused_computation.5 | convolution fusion | flops 10307174400 | bytes 21430272 | tf_op jit(solution)/shard_map/td,te->de/dot_general | solution.py:1096
  453.3 4.5 copy.118
  457.8 4.1 copy.119
  461.9 7.5 %bitcast_convert_fusion.3 = bf16[768,768]{0,1:T(8,128)(2,1)S(1)} fusion(bf16[13,224,768]{2,1,0:T(8,128)(2,1)} %get-tuple-element.48.att_ref, bf16[13,224,768]{2,1,0:T(8,128)(2,1)} %get-tuple-element.58.dmix_ref), kind=kOutput, calls=%fused_computation.7 | convolution fusion | flops 3435724800 | bytes 10125312 | tf_op jit(solution)/shard_map/td,te->de/dot_general | solution.py:1096
  470.4 5.6 maximum_bitcast_fusion.q_ref
  476.0 68.9 %shard_map.353 = (bf16[25,224,768]{2,1,0:T(8,128)(2,1)}, f32[192,384]{1,0:T(8,128)}, f32[16,768]{1,0:T(8,128)}, f32[64,256]{1,0:T(8,128)}, f32[8,768]{1,0:T(8,128)}) custom-call(s32[13,4]{1,0:T(8,128)} %pad_add_fusion.meta_ref, bf16[13,224,2304]{2,1,0:T(8,128)(2,1)} %get-tuple-element.57.dqkv_ref, bf16[768,2304]{1,0:T(8,128)(2,1)} %reshape.154.wqkv_ref, ...), custom_call_target="tpu_custom_call" | custom-call | flops 20000000000 | bytes 50000000 | tf_op jit(solution)/shard_map/pallas_call | solution.py:946
  555.9 11.4 %shard_map.354 = (bf16[2,16,64,768]{3,2,1,0:T(8,128)(2,1)}, f32[2,16,64,768]{3,2,1,0:T(8,128)}) custom-call(s32[2,32]{1,0:T(2,128)} %add_add_fusion.table_ref, bf16[25,224,768]{2,1,0:T(8,128)(2,1)} %get-tuple-element.56.refs_0_, bf16[25,224,768]{2,1,0:T(8,128)(2,1)} %get-tuple-element.64.refs_1_), custom_call_target="tpu_custom_call" | custom-call | flops 500000000 | bytes 20000000 | tf_op jit(solution)/shard_map/pallas_call | solution.py:798
  (115 shorter events, 44.7 us)
Async XLA Ops:
  7.2 77.7 %all-gather.8.cloned.1.call-start = ((), (), s32[]{:S(2)}) async-start(), calls=%async_computation.1 | async-start | bytes 4866048 | tf_op jit(solution)/shard_map/all_gather | solution.py:1047
  17.1 158.4 %all-gather.6.cloned.1.call-start = ((), (), s32[]{:S(2)}) async-start(), calls=%async_computation | async-start | bytes 11354112 | tf_op jit(solution)/shard_map/all_gather | solution.py:1049
  23.0 4.7 copy-start
  23.0 7.6 %copy-start.1 = (bf16[2,16,64,768]{3,2,1,0:T(8,128)(2,1)S(1)}, bf16[2,16,64,768]{3,2,1,0:T(8,128)(2,1)}, u32[]{:S(2)}) copy-start(bf16[2,16,64,768]{3,2,1,0:T(8,128)(2,1)} %param.40) | copy-start | bytes 9437188
  23.0 14.3 %collective-permute-start = (bf16[2,12,64,768]{3,2,1,0:T(8,128)(2,1)}, bf16[2,12,64,768]{3,2,1,0:T(8,128)(2,1)}, u32[]{:S(2)}, u32[]{:S(2)}) collective-permute-start(bf16[2,12,64,768]{3,2,1,0:T(8,128)(2,1)} %slice_select_fusion.1), channel_id=1, source_target_pairs={{0,1},{1,0},{2,3},{3,2},{4,5},{5,4},{6,7},{7,6},{8,9},{9,8},{10,11... | collective-permute-start | bytes 7077896 | tf_op jit(solution)/shard_map/ppermute | solution.py:1006
  27.7 6.7 %copy-start.3 = (s32[2,2]{1,0:T(2,128)S(1)}, s32[2,2]{1,0:T(2,128)}, u32[]{:S(2)}) copy-start(s32[2,2]{1,0:T(2,128)} %param.24) | copy-start | bytes 52
  27.7 12.3 %collective-permute-start.2 = (bf16[2,12,64,768]{3,2,1,0:T(8,128)(2,1)}, bf16[2,12,64,768]{3,2,1,0:T(8,128)(2,1)}, u32[]{:S(2)}, u32[]{:S(2)}) collective-permute-start(bf16[2,12,64,768]{3,2,1,0:T(8,128)(2,1)} %slice_select_fusion), channel_id=1, source_target_pairs={{0,1},{1,0},{2,3},{3,2},{4,5},{5,4},{6,7},{7,6},{8,9},{9,8},{10,11... | collective-permute-start | bytes 7077896 | tf_op jit(solution)/shard_map/ppermute | solution.py:1006
  28.9 8.4 %collective-permute-start.1 = (bf16[12,64,768]{2,1,0:T(8,128)(2,1)}, bf16[12,64,768]{2,1,0:T(8,128)(2,1)}, u32[]{:S(2)}, u32[]{:S(2)}) collective-permute-start(bf16[12,64,768]{2,1,0:T(8,128)(2,1)} %select_bitcast_fusion.1), channel_id=1, source_target_pairs={{1,2},{2,1},{5,6},{6,5},{9,10},{10,9},{13,14},{14,13},{17,18},{18,... | collective-permute-start | bytes 3538952 | tf_op jit(solution)/shard_map/ppermute | solution.py:1007
  31.8 8.2 %collective-permute-start.3 = (bf16[12,64,768]{2,1,0:T(8,128)(2,1)}, bf16[12,64,768]{2,1,0:T(8,128)(2,1)}, u32[]{:S(2)}, u32[]{:S(2)}) collective-permute-start(bf16[12,64,768]{2,1,0:T(8,128)(2,1)} %select_bitcast_fusion), channel_id=1, source_target_pairs={{1,2},{2,1},{5,6},{6,5},{9,10},{10,9},{13,14},{14,13},{17,18},{18,... | collective-permute-start | bytes 3538952 | tf_op jit(solution)/shard_map/ppermute | solution.py:1007
  42.7 3.8 copy-start.2
  318.3 21.2 %copy-start.7 = (bf16[13,224,3072]{2,1,0:T(8,128)(2,1)S(1)}, bf16[13,224,3072]{2,1,0:T(8,128)(2,1)}, u32[]{:S(2)}) copy-start(bf16[13,224,3072]{2,1,0:T(8,128)(2,1)} %get-tuple-element.52) | copy-start | bytes 53673988
  318.3 21.2 %copy-start.8 = (bf16[13,224,768]{2,1,0:T(8,128)(2,1)S(1)}, bf16[13,224,768]{2,1,0:T(8,128)(2,1)}, u32[]{:S(2)}) copy-start(bf16[13,224,768]{2,1,0:T(8,128)(2,1)} %get-tuple-element.51) | copy-start | bytes 13418500
  555.9 11.4 %copy-start.4 = (f32[192,384]{1,0:T(8,128)S(1)}, f32[192,384]{1,0:T(8,128)}, u32[]{:S(2)}) copy-start(f32[192,384]{1,0:T(8,128)} %get-tuple-element.68) | copy-start | bytes 884740
  555.9 12.1 %copy-start.6 = (f32[192,384]{1,0:T(8,128)S(1)}, f32[192,384]{1,0:T(8,128)}, u32[]{:S(2)}) copy-start(f32[192,384]{1,0:T(8,128)} %get-tuple-element.135) | copy-start | bytes 884740
  555.9 12.9 %copy-start.5 = (f32[192,384]{1,0:T(8,128)S(1)}, f32[192,384]{1,0:T(8,128)}, u32[]{:S(2)}) copy-start(f32[192,384]{1,0:T(8,128)} %get-tuple-element.72) | copy-start | bytes 884740
Sparse Core Ops, SparseCore 0:
  17.3 67.5 all-gather.7
  87.7 87.7 all-gather.5

commit v4 on v3

--- a/solution.py
+++ b/solution.py
@@ -124,20 +124,37 @@
 
 
 def fwd_kernel(
-    meta_ref, rows_ref, gain_ref, shift_ref, wqkv_ref, bias_ref, table_ref, ka_ref, kb_ref,
-    x_ref, n_ref, qkv_ref, p_ref, inv_ref, att_ref,
+    meta_ref, rows_ref, grows_ref, vec_ref, wqkv_ref, table_ref, ka_ref, kb_ref,
+    x_ref, g_ref, n_ref, qkv_ref, p_ref, inv_ref, att_ref, *weights,
 ):
     w = pl.program_id(0)
+    if weights:
+        blocks_ref, (wqkv_ref, wproj_ref) = wqkv_ref, weights
+
+        @pl.when(w == 0)
+        def _():
+            share = D // blocks_ref.shape[0]
+            for b in range(blocks_ref.shape[1]):
+                rows = slice(SHARD_ROWS * b, SHARD_ROWS * b + SHARD_ROWS)
+                parts = [blocks_ref[i, b, :SHARD_ROWS] for i in range(blocks_ref.shape[0])]
+                wqkv_ref[rows] = jnp.concatenate([part[:, : 3 * share] for part in parts], axis=1)
+                wproj_ref[rows] = jnp.concatenate([part[:, 3 * share :] for part in parts], axis=1)
+
     target = token_target(meta_ref, w)
     x = take_window(target, rows_ref)
     x_ref[...] = x.astype(BF16)
+    g_ref[...] = take_window(target, grows_ref).astype(BF16)
     unit, _ = norm(x)
-    normed = jnp.where(target >= 0, unit * gain_ref[...] + shift_ref[...], 0.0).astype(BF16)
+    normed = jnp.where(target >= 0, unit * vec_ref[0:1] + vec_ref[1:2], 0.0).astype(BF16)
     n_ref[...] = normed
     for c in range(9):
         cols = slice(256 * c, 256 * c + 256)
-        y = mm(normed, wqkv_ref[:, cols]) + bias_ref[:, cols]
-        if 3 <= c < 6:
+        y = mm(normed, wqkv_ref[:, cols])
+        if c < 3:
+            y = y + vec_ref[2:3, cols]
+        elif c >= 6:
+            y = y + vec_ref[3:4, 256 * (c - 6) : 256 * (c - 6) + 256]
+        else:
             y = y.astype(BF16).astype(F32) * 0.125
         qkv_ref[:, cols] = y.astype(BF16)
 
@@ -198,8 +215,9 @@
     return jnp.concatenate([wide(rel_rows[::-1]), wide(rel_cols[::-1] if forward else rel_cols)], axis=1)
 
 
-def attention_forward(meta, ext, gain, shift, wqkv, bias, table, ka, kb):
+def attention_forward(meta, ext, gext, vectors, wqkv, table, ka, kb):
     cap = meta.shape[0]
+    weights = [(D, 3 * D), (D, D)] if wqkv.ndim == 4 else []
     sds = jax.ShapeDtypeStruct
     return pl.pallas_call(
         fwd_kernel,
@@ -207,21 +225,21 @@
             num_scalar_prefetch=1,
             grid=(cap,),
             in_specs=[
-                rows_spec(WIN), whole((1, D)), whole((1, D)), whole((D, 3 * D)), whole((1, 3 * D)),
+                rows_spec(WIN), rows_spec(WIN), whole((8, D)), whole(wqkv.shape),
                 whole((LANES, 256)), whole((TW, LANES)), whole((TW, LANES)),
             ],
             out_specs=[
-                per_window(TW, D), per_window(TW, D), per_window(TW, 3 * D),
+                per_window(TW, D), per_window(TW, D), per_window(TW, D), per_window(TW, 3 * D),
                 per_window(HEADS, TW, TW), per_window(TW, D), per_window(TW, D),
-            ],
+            ] + [whole(shape) for shape in weights],
         ),
         out_shape=[
-            sds((cap, TW, D), BF16), sds((cap, TW, D), BF16), sds((cap, TW, 3 * D), BF16),
+            sds((cap, TW, D), BF16), sds((cap, TW, D), BF16), sds((cap, TW, D), BF16), sds((cap, TW, 3 * D), BF16),
             sds((cap, HEADS, TW, TW), BF16), sds((cap, TW, D), F32), sds((cap, TW, D), BF16),
-        ],
+        ] + [sds(shape, BF16) for shape in weights],
         compiler_params=pltpu.CompilerParams(vmem_limit_bytes=VMEM_LIMIT),
         cost_estimate=pl.CostEstimate(flops=40_000_000_000, bytes_accessed=80_000_000, transcendentals=8_000_000),
-    )(meta, ext, gain, shift, wqkv, bias, table, ka, kb)
+    )(meta, ext, gext, vectors, wqkv, table, ka, kb)
 
 
 def phi_parts(u):
@@ -233,31 +251,31 @@
 
 
 def mlp_kernel(
-    meta_ref, grows_ref, x_ref, att_ref, wproj_ref, pbias_ref, gain_ref, shift_ref, ff_ref, b1_ref, b2_ref,
-    out_ref, g_ref, n2_ref, act_ref, dpre_ref, dmix_ref, datt_ref, sums_ref, sum1_ref,
+    g_ref, x_ref, att_ref, wproj_ref, vec_ref, ff_ref, b1_ref,
+    out_ref, n2_ref, act_ref, dpre_ref, dmix_ref, datt_ref, sums_ref, sum1_ref,
     acc_ref, dn_ref,
 ):
-    w = pl.program_id(0)
-
-    @pl.when(w == 0)
+    @pl.when(pl.program_id(0) == 0)
     def _():
         sums_ref[...] = jnp.zeros_like(sums_ref)
         sum1_ref[...] = jnp.zeros_like(sum1_ref)
 
-    target = token_target(meta_ref, w)
-    g = take_window(target, grows_ref)
-    gb = g.astype(BF16)
-    g_ref[...] = gb
+    gb = g_ref[...]
+    g = gb.astype(F32)
     sums_ref[0] += fold8(g)
-    hidden = x_ref[...].astype(F32) + mm(att_ref[...], wproj_ref[...]) + pbias_ref[...]
+    hidden = x_ref[...].astype(F32) + mm(att_ref[...], wproj_ref[...]) + vec_ref[4:5]
     unit, inverse = norm(hidden)
-    n2 = (unit * gain_ref[...] + shift_ref[...]).astype(BF16)
+    n2 = (unit * vec_ref[5:6] + vec_ref[6:7]).astype(BF16)
     n2_ref[...] = n2
-    acc_ref[...] = hidden + b2_ref[...]
-    parts, chunk = ff_ref.shape[0], ff_ref.shape[2] // 2
-    for c in range(parts):
+    acc_ref[...] = hidden + vec_ref[7:8]
+    parts, inner = ff_ref.shape[0], ff_ref.shape[2] // 2
+    join = max(1, 768 // inner)
+    chunk = inner * join
+    for c in range(parts // join):
         cols = slice(chunk * c, chunk * c + chunk)
-        w1, w2t = ff_ref[c, :, :chunk], ff_ref[c, :, chunk:]
+        blocks = range(join * c, join * c + join)
+        w1 = jnp.concatenate([ff_ref[i, :, :inner] for i in blocks], axis=1)
+        w2t = jnp.concatenate([ff_ref[i, :, inner:] for i in blocks], axis=1)
         u = mm(n2, w1) + b1_ref[:, cols]
         dact = mm(gb, w2t)
         cdf, pdf = phi_parts(u)
@@ -277,39 +295,46 @@
     dn = dn_ref[...]
     sums_ref[1] += fold8(dn * unit)
     sums_ref[2] += fold8(dn)
-    dh = g + norm_back(dn, unit, inverse, gain_ref[...])
+    dh = g + norm_back(dn, unit, inverse, vec_ref[5:6])
     dmix = dh.astype(BF16)
     dmix_ref[...] = dmix
     sums_ref[3] += fold8(dh)
     datt_ref[...] = mm_nt(dmix, wproj_ref[...]).astype(BF16)
 
 
-def feed_forward(meta, gext, x, att, wproj, pbias, gain, shift, ff, b1, b2, spare):
-    cap = meta.shape[0]
+def tile_rows(rows):
+    return next(t for t in (416, 448, 224) if rows % t == 0)
+
+
+def feed_forward(g, x, att, wproj, vectors, ff, b1, spare):
+    cap = g.shape[0]
+    rows = cap * TW
+    tile = tile_rows(rows)
     sds = jax.ShapeDtypeStruct
-    return pl.pallas_call(
+
+    def tiled(width):
+        return pl.BlockSpec((tile, width), lambda i: (i, 0))
+
+    def kept(shape):
+        zeros = (0,) * len(shape)
+        return pl.BlockSpec(shape, lambda i: zeros, pipeline_mode=pl.Buffered(1))
+
+    out, *rest = pl.pallas_call(
         mlp_kernel,
-        grid_spec=pltpu.PrefetchScalarGridSpec(
-            num_scalar_prefetch=1,
-            grid=(cap,),
-            in_specs=[
-                rows_spec(WIN), per_window(TW, D), per_window(TW, D), whole((D, D)), whole((1, D)), whole((1, D)),
-                whole((1, D)), whole(ff.shape), whole((1, FF)), whole((1, D)),
-            ],
-            out_specs=[
-                per_window(TW, D), per_window(TW, D), per_window(TW, D), per_window(TW, FF), per_window(TW, FF),
-                per_window(TW, D), per_window(TW, D), whole((4, 8, D)), whole((8, FF)),
-            ],
-            scratch_shapes=[pltpu.VMEM((TW, D), F32), pltpu.VMEM((TW, D), F32)],
-        ),
+        grid=(rows // tile,),
+        in_specs=[
+            tiled(D), tiled(D), tiled(D), kept((D, D)), kept((8, D)), kept(ff.shape), kept((1, FF)),
+        ],
+        out_specs=[tiled(D), tiled(D), tiled(FF), tiled(FF), tiled(D), tiled(D), kept((4, 8, D)), kept((8, FF))],
+        scratch_shapes=[pltpu.VMEM((tile, D), F32), pltpu.VMEM((tile, D), F32)],
         out_shape=[
-            sds((cap + spare, TW, D), BF16), sds((cap, TW, D), BF16), sds((cap, TW, D), BF16), sds((cap, TW, FF), BF16),
-            sds((cap, TW, FF), BF16), sds((cap, TW, D), BF16), sds((cap, TW, D), BF16), sds((4, 8, D), F32),
-            sds((8, FF), F32),
+            sds((rows + spare * TW, D), BF16), sds((rows, D), BF16), sds((rows, FF), BF16), sds((rows, FF), BF16),
+            sds((rows, D), BF16), sds((rows, D), BF16), sds((4, 8, D), F32), sds((8, FF), F32),
         ],
         compiler_params=pltpu.CompilerParams(vmem_limit_bytes=VMEM_LIMIT),
         cost_estimate=pl.CostEstimate(flops=60_000_000_000, bytes_accessed=80_000_000, transcendentals=8_000_000),
-    )(meta, gext, x, att, wproj, pbias, gain, shift, ff, b1, b2)
+    )(g.reshape(rows, D), x.reshape(rows, D), att.reshape(rows, D), wproj, vectors, ff, b1)
+    return out.reshape(cap + spare, TW, D), rest[0], rest[1], rest[2], *[a.reshape(cap, TW, D) for a in rest[3:5]], *rest[5:]
 
 
 MESH = pl.DeviceIdType.MESH
@@ -430,6 +455,24 @@
 ORDERS = (("x", "y", "zh", "zl"), ("y", "x", "zh", "zl"))
 
 
+def wide_source(ref, part):
+    half = SHARD_ROWS // 2
+
+    def source(x, img, c):
+        row = pl.multiple_of((2 * x + c) * SHARD_ROWS + part * half, half)
+        return ref.at[pl.ds(row, half), pl.ds(img * SHARD_COLS, SHARD_COLS)]
+
+    return source
+
+
+def each(group, name, *args):
+    def body():
+        for stream in group:
+            getattr(stream, name)(*args)
+
+    return body
+
+
 def timeline(w, moments):
     for when, bodies in moments.items():
         @pl.when(w == when)
@@ -497,6 +540,176 @@
             self.to_core(NEAR_CROSS, NEAR_CORE).wait_recv()
 
 
+class Gather:
+    def __init__(self, block, out, sems):
+        self.block, self.out, self.sems = block, out, sems
+        img, self.band = lax.axis_index("img"), lax.axis_index("band")
+        self.z, self.y = img // 2, img % 2
+        self.x, self.c = self.band // 2, self.band % 2
+
+    def where(self, dz, fx, fy):
+        img = (self.z + 4 - dz) % 4 * 2 + (1 - self.y if fy else self.y)
+        return img, (1 - self.x if fx else self.x) * 2 + self.c
+
+    def move(self, k, dz, fx, fy, device):
+        img, band = self.where(dz, fx, fy)
+        own = (dz, fx, fy) == (0, 0, 0)
+        return pltpu.make_async_remote_copy(
+            src_ref=self.block if own else self.out.at[img, band], dst_ref=self.out.at[img, band],
+            send_sem=self.sems.at[0, k], recv_sem=self.sems.at[1, k], device_id=device, device_id_type=MESH,
+        )
+
+    def along_z(self, d):
+        return self.move(d - 1, 0, 0, 0, ((self.z + d) % 4 * 2 + self.y, self.band))
+
+    def along_x(self, dz):
+        return self.move(3 + dz, dz, 0, 0, partner("x"))
+
+    def along_y(self, fx, dz):
+        return self.move(7 + 4 * fx + dz, dz, fx, 0, partner("y"))
+
+    def to_core(self, fy, fx, dz):
+        return self.move(15 + 8 * fy + 4 * fx + dz, dz, fx, fy, partner("c"))
+
+    def keep(self):
+        img, band = self.where(0, 0, 0)
+        return pltpu.make_async_copy(self.block, self.out.at[img, band], self.sems.at[0, 31])
+
+    def pass_on(self, dz):
+        self.along_x(dz).start()
+        self.along_y(0, dz).start()
+        self.to_core(0, 0, dz).start()
+
+    def begin(self):
+        self.keep().start()
+        for d in range(1, 4):
+            self.along_z(d).start()
+        self.pass_on(0)
+
+    def run(self):
+        for dz in range(1, 4):
+            self.along_z(dz).wait_recv()
+            self.pass_on(dz)
+        for dz in range(4):
+            self.along_x(dz).wait_recv()
+            self.along_y(1, dz).start()
+            self.to_core(0, 1, dz).start()
+        for fx in range(2):
+            for dz in range(4):
+                self.along_y(fx, dz).wait_recv()
+                self.to_core(1, fx, dz).start()
+        for d in range(1, 4):
+            self.along_z(d).wait_send()
+        for dz in range(4):
+            self.along_x(dz).wait_send()
+            for fx in range(2):
+                self.along_y(fx, dz).wait_send()
+                for fy in range(2):
+                    self.to_core(fy, fx, dz).wait()
+        self.keep().wait()
+
+
+class Edges:
+    def __init__(self, rows, ext, zero, sems):
+        self.rows, self.ext, self.zero, self.sems = rows, ext, zero, sems
+        self.band = lax.axis_index("band")
+        self.own_rows = rows.shape[1]
+
+    def inner(self):
+        return (self.band == 1) | (self.band == 2)
+
+    def keep(self):
+        return pltpu.make_async_copy(self.rows, self.ext.at[:, pl.ds(HALO, self.own_rows)], self.sems.at[0])
+
+    def empty(self):
+        at = self.band // 3 * (HALO + self.own_rows)
+        return [
+            pltpu.make_async_copy(self.zero, self.ext.at[m, pl.ds(at, HALO)], self.sems.at[1 + m]) for m in range(2)
+        ]
+
+    def core(self, sending):
+        odd = self.band % 2
+        far = self.own_rows - HALO
+        there = (1 - odd if sending else odd) * 0 + (odd if sending else 1 - odd) * (HALO + self.own_rows)
+        return pltpu.make_async_remote_copy(
+            src_ref=self.rows.at[:, pl.ds((1 - odd) * far, HALO)], dst_ref=self.ext.at[:, pl.ds(there, HALO)],
+            send_sem=self.sems.at[3], recv_sem=self.sems.at[4], device_id=partner("c"), device_id_type=MESH,
+        )
+
+    def cross(self, sending):
+        img = lax.axis_index("img")
+        m = 2 - self.band
+        far = self.own_rows - HALO
+        to = m if sending else 1 - m
+        there = (1 - to) * (HALO + self.own_rows)
+        return pltpu.make_async_remote_copy(
+            src_ref=self.rows.at[m, pl.ds(m * far, HALO)], dst_ref=self.ext.at[to, pl.ds(there, HALO)],
+            send_sem=self.sems.at[5], recv_sem=self.sems.at[6], device_id=(img, 3 - self.band), device_id_type=MESH,
+        )
+
+    def start(self):
+        pl.when(self.inner())(lambda: self.cross(True).start())
+        self.core(True).start()
+        self.keep().start()
+
+        @pl.when(jnp.logical_not(self.inner()))
+        def _():
+            for copy in self.empty():
+                copy.start()
+
+    def finish(self):
+        self.core(True).wait_send()
+        self.core(False).wait_recv()
+        self.keep().wait()
+
+        @pl.when(self.inner())
+        def _():
+            self.cross(True).wait_send()
+            self.cross(False).wait_recv()
+
+        @pl.when(jnp.logical_not(self.inner()))
+        def _():
+            for copy in self.empty():
+                copy.wait()
+
+
+def entry_kernel(
+    block_ref, x_ref, g_ref, all_ref, xext_ref, gext_ref, zero_ref, xin_ref, gin_ref, lsems, gsems, xsems, esems,
+):
+    loads = [pltpu.make_async_copy(x_ref, xin_ref, lsems.at[0]), pltpu.make_async_copy(g_ref, gin_ref, lsems.at[1])]
+    for load in loads:
+        load.start()
+    zero_ref[...] = jnp.zeros_like(zero_ref)
+    edges = [Edges(xin_ref, xext_ref, zero_ref, xsems), Edges(gin_ref, gext_ref, zero_ref, esems)]
+    greet()
+    gather = Gather(block_ref, all_ref, gsems)
+    gather.begin()
+    for load, item in zip(loads, edges):
+        load.wait()
+        item.start()
+    gather.run()
+    for item in edges:
+        item.finish()
+
+
+def entry(block, x, g):
+    sds = jax.ShapeDtypeStruct
+    ext = sds((2, x.shape[1] + 2 * HALO, SIDE, D), BF16)
+    inside, anywhere = pl.BlockSpec(memory_space=pltpu.VMEM), pl.BlockSpec(memory_space=pl.ANY)
+    return pl.pallas_call(
+        entry_kernel,
+        in_specs=[inside, anywhere, anywhere],
+        out_specs=[anywhere] * 3,
+        out_shape=[sds((8, 4) + block.shape, BF16), ext, ext],
+        scratch_shapes=[
+            pltpu.VMEM((HALO, SIDE, D), BF16), pltpu.VMEM(x.shape, BF16), pltpu.VMEM(x.shape, BF16),
+            pltpu.SemaphoreType.DMA((2,)), pltpu.SemaphoreType.DMA((2, 32)), pltpu.SemaphoreType.DMA((7,)),
+            pltpu.SemaphoreType.DMA((7,)),
+        ],
+        compiler_params=pltpu.CompilerParams(vmem_limit_bytes=VMEM_LIMIT, collective_id=3, has_side_effects=True),
+    )(block, x, g)
+
+
 def attn_bwd_kernel(
     meta_ref, qkv_ref, p_ref, inv_ref, att_ref, datt_ref, table_ref, kback_ref, *rest,
 ):
@@ -505,41 +718,22 @@
         dqkv_ref, rel_ref, bias_ref = rest
         streams = None
     else:
-        fc1_ref, fc2_ref, _, dqkv_ref, rel_ref, bias_ref, sum1_ref, sum2_ref, all_ref = rest[:9]
+        fc1_ref, fc2_ref, dqkv_ref, rel_ref, bias_ref, part_ref, sum2_ref = rest[:7]
         half = SHARD_ROWS // 2
         streams = []
         for n in range(4):
-            own, *got, sems = rest[9 + 7 * n : 16 + 7 * n]
-
-            def source(x, img, c, ref=(fc1_ref, fc2_ref)[n // 2], n=n):
-                row = pl.multiple_of((2 * x + c) * SHARD_ROWS + n % 2 * half, half)
-                return ref.at[pl.ds(row, half), pl.ds(img * SHARD_COLS, SHARD_COLS)]
-
+            own, *got, sems = rest[7 + 7 * n : 14 + 7 * n]
+            source = wide_source(fc2_ref if n < 2 else fc1_ref, n % 2)
             streams.append(Halving(source, own, got, sems, ORDERS[n % 2], half))
         ones, twos = streams[:2], streams[2:]
-        back = Homeward(all_ref, all_ref, rest[37])
-
-        def each(group, name, *args):
-            def body():
-                for stream in group:
-                    getattr(stream, name)(*args)
-            return body
-
         timeline(
             w,
             {
                 0: [greet, each(streams, "first")],
-                2: [
-                    each(ones, "first_done"), each(ones, "step", 0), each(twos, "first_done"),
-                    back.send_core_inner, back.send_core_outer,
-                ],
-                5: [each(ones, "step_done", 0), each(ones, "step", 1)],
-                7: [each(ones, "step_done", 1), each(ones, "step", 2), each(twos, "step", 0)],
-                10: [
-                    each(ones, "step_done", 2), each(ones, "step", 3), each(twos, "step_done", 0), each(twos, "step", 1),
-                    back.send_cross,
-                ],
-                12: [each(ones, "step_done", 3), each(twos, "step_done", 1), each(twos, "step", 2)],
+                2: [each(ones, "first_done"), each(ones, "step", 0), each(twos, "first_done")],
+                5: [each(ones, "step_done", 0), each(ones, "step", 1), each(twos, "step", 0)],
+                7: [each(ones, "step_done", 1), each(ones, "step", 2)],
+                10: [each(twos, "step_done", 0), each(twos, "step", 1), each(ones, "step_done", 2), each(ones, "step", 3)],
             },
         )
 
@@ -592,14 +786,12 @@
     if streams:
         @pl.when(w == pl.num_programs(0) - 1)
         def _():
-            sum1_ref[:half] = ones[0].result()
-            sum1_ref[half:] = ones[1].result()
-            each(twos, "step_done", 2)()
-            each(twos, "step", 3)()
-            back.finish()
-            each(twos, "step_done", 3)()
-            sum2_ref[:half] = twos[0].result()
-            sum2_ref[half:] = twos[1].result()
+            each(ones, "step_done", 3)()
+            sum2_ref[:half] = ones[0].result()
+            sum2_ref[half:] = ones[1].result()
+            each(twos, "step_done", 1)()
+            for n, stream in enumerate(twos):
+                part_ref[n] = stream.own[stream.at["x"], :, :, stream.at["y"]]
 
 
 def attention_backward(meta, qkv, p, inv, att, datt, table, kback, beside=()):
@@ -609,13 +801,13 @@
     shard = (SHARD_ROWS, SHARD_COLS)
     more_specs, more_outs, scratch, extra = [], [], [], {}
     if beside:
-        more_specs = [whole(shard), whole(shard), anywhere]
-        more_outs = [sds(shard, F32), sds(shard, F32), sds((cap + NEAR_CORE + NEAR_CROSS, TW, D), BF16)]
-        scratch = Halving.scratch(SHARD_ROWS // 2) * 4 + [pltpu.SemaphoreType.DMA((5,))]
+        part = (2, 2, 2, SHARD_ROWS // 2, SHARD_COLS)
+        more_specs = [whole(part), whole(shard)]
+        more_outs = [sds(part, BF16), sds(shard, F32)]
+        scratch = Halving.scratch(SHARD_ROWS // 2) * 4
         extra = dict(collective_id=1, has_side_effects=True)
     return pl.pallas_call(
         attn_bwd_kernel,
-        input_output_aliases={10: 5} if beside else {},
         grid_spec=pltpu.PrefetchScalarGridSpec(
             num_scalar_prefetch=1,
             grid=(cap,),
@@ -704,7 +896,7 @@
     unit, inverse = norm(x_ref[...].astype(F32))
     sums_ref[0] += fold8(dn * unit)
     sums_ref[1] += fold8(dn)
-    grad = dmix_ref[...].astype(F32) + norm_back(dn, unit, inverse, gain_ref[...])
+    grad = dmix_ref[...].astype(F32) + norm_back(dn, unit, inverse, gain_ref[0:1])
     put_window(target, grad.astype(BF16), acc_ref, meta_ref[w, 0])
 
     @pl.when(w == pl.num_programs(0) - 1)
@@ -724,7 +916,7 @@
             num_scalar_prefetch=1,
             grid=(cap,),
             in_specs=[
-                per_window(TW, 3 * D), whole((D, 3 * D)), per_window(TW, D), per_window(TW, D), whole((1, D)),
+                per_window(TW, 3 * D), whole((D, 3 * D)), per_window(TW, D), per_window(TW, D), whole((8, D)),
             ],
             out_specs=[whole((ext_rows, SIDE, D)), whole((2, 8, D))],
             scratch_shapes=[pltpu.VMEM((ext_rows, SIDE, D), F32)],
@@ -772,13 +964,50 @@
 HOME_ROWS = 8
 
 
-def home_kernel(table_ref, *refs):
-    arrays = len(refs) // 2
+def home_kernel(
+    table_ref, own_ref, core_ref, cross_ref, grad_ref, total_ref, ln_ref, rel_ref, q_ref, fc2_ref,
+    output_ref, input_grad_ref, vec_refs, b1_ref, relr_ref, relc_ref, wq_ref, wp_ref, w2_ref,
+    out_ref, sems,
+):
     step = pl.program_id(0)
     per_image = pl.num_programs(0) // 2
     m = step // per_image
     top, left = table_ref[m, 25], table_ref[m, 26]
     first = table_ref[m, 27] + (step - m * per_image) * HOME_ROWS
+    group, band = table_ref[m, 28], table_ref[m, 29]
+
+    @pl.when(step == 0)
+    def _():
+        cap = own_ref.shape[0]
+        loads = [
+            pltpu.make_async_copy(ref, out_ref.at[pl.ds(at, ref.shape[0])], sems.at[n])
+            for n, (ref, at) in enumerate(((own_ref, 0), (core_ref, cap), (cross_ref, cap + NEAR_CORE)))
+        ]
+        for load in loads:
+            load.start()
+        share = vec_refs[0].shape[1]
+
+        def cut(rows, width):
+            mine = jnp.zeros((rows.shape[0], width), F32)
+            for i in range(rows.shape[1] // width):
+                mine = mine + jnp.where(group % (rows.shape[1] // width) == i, rows[:, width * i : width * i + width], 0.0)
+            return mine
+
+        ln, total = cut(ln_ref[...], share), cut(total_ref[...], share)
+        for ref, row in zip(vec_refs, (ln[0:1], ln[1:2], total[0:1], total[1:2], total[5:6], total[3:4], total[4:5], total[2:3])):
+            ref[...] = row
+        b1_ref[...] = cut(total_ref[pl.ds(6 + group // 2, 1)], SHARD_COLS)
+        features = relr_ref.shape[1]
+        turned = rel_ref[pl.ds(pl.multiple_of(band * features, features), features)].T
+        for j in range(RELS):
+            relr_ref[j : j + 1] = turned[RELS - 1 - j : RELS - j]
+        relc_ref[...] = turned[LANES : LANES + RELS]
+        wq_ref[...] = q_ref[:, : 3 * share]
+        wp_ref[...] = q_ref[:, 3 * share :]
+        w2_ref[...] = fc2_ref[...].T
+        for load in loads:
+            load.wait()
+
     col = iota((SIDE, GRID * STRIDE), 0) + left
     spot = iota((SIDE, GRID * STRIDE), 1)
     picks = jnp.where((spot >> 4) * WIN + (spot & 15) == col, 1.0, 0.0)
@@ -788,31 +1017,36 @@
         r = at // WIN
         a = pl.multiple_of((at - r * WIN) * STRIDE, STRIDE)
         slots = [table_ref[m, r * GRID + c] for c in range(GRID)]
-        for n in range(arrays):
-            tokens = jnp.concatenate([refs[n][slot, pl.ds(a, STRIDE)] for slot in slots], axis=0)
-            refs[arrays + n][0, i] = mm(picks, tokens).astype(refs[arrays + n].dtype)
-
-
-def home(table, sources, dtypes, rows):
+        for source, target in ((out_ref, output_ref), (grad_ref, input_grad_ref)):
+            tokens = jnp.concatenate([source[slot, pl.ds(a, STRIDE)] for slot in slots], axis=0)
+            target[0, i] = mm(picks, tokens).astype(target.dtype)
+
+
+def home(table, sources, rows):
     per_image = rows // HOME_ROWS
+    sds = jax.ShapeDtypeStruct
+    tiled = pl.BlockSpec((1, HOME_ROWS, SIDE, D), lambda w, meta: (w // per_image, w % per_image, 0, 0))
+    shapes = [[(1, D // 8)] * 8, (1, FF // 8)] + [(RELS, HEAD // 4)] * 2 + [
+        (SHARD_ROWS, 3 * D // 8), (SHARD_ROWS, D // 8), (SHARD_COLS, SHARD_ROWS),
+    ]
+    is_shape = lambda shape: isinstance(shape, tuple)
     return pl.pallas_call(
         home_kernel,
         grid_spec=pltpu.PrefetchScalarGridSpec(
             num_scalar_prefetch=1,
             grid=(2 * per_image,),
-            in_specs=[whole(a.shape) for a in sources],
-            out_specs=[
-                pl.BlockSpec((1, HOME_ROWS, SIDE, D), lambda w, meta: (w // per_image, w % per_image, 0, 0))
-                for _ in dtypes
-            ],
+            in_specs=[pl.BlockSpec(memory_space=pl.ANY)] * 3 + [whole(a.shape) for a in sources[3:]],
+            scratch_shapes=[pltpu.VMEM(sources[3].shape, BF16), pltpu.SemaphoreType.DMA((3,))],
+            out_specs=[tiled, tiled] + jax.tree.map(whole, shapes, is_leaf=is_shape),
         ),
-        out_shape=[jax.ShapeDtypeStruct((2, rows, SIDE, D), dtype) for dtype in dtypes],
+        out_shape=[sds((2, rows, SIDE, D), BF16), sds((2, rows, SIDE, D), F32)]
+        + jax.tree.map(lambda shape: sds(shape, F32), shapes, is_leaf=is_shape),
         compiler_params=pltpu.CompilerParams(vmem_limit_bytes=VMEM_LIMIT),
         cost_estimate=pl.CostEstimate(flops=500_000_000, bytes_accessed=20_000_000, transcendentals=0),
     )(table, *sources)
 
 
-def home_table(plan, offsets, band, band_rows):
+def home_table(plan, offsets, group, band, band_rows):
     own = np.full((4, 2, WINDOWS), 0, np.int32)
     for b in range(4):
         for slot, (m, w) in enumerate(plan[b]):
@@ -828,13 +1062,14 @@
                 own[b, m, w] = cap + NEAR_CORE + slot
     rows = jnp.asarray(own)[band]
     first = jnp.full((2, 1), band_rows, jnp.int32) * band
-    return jnp.concatenate([rows, offsets.astype(jnp.int32), first, jnp.zeros((2, 4), jnp.int32)], axis=1)
+    spot = jnp.broadcast_to(jnp.stack([group, band]).astype(jnp.int32), (2, 2))
+    return jnp.concatenate([rows, offsets.astype(jnp.int32), first, spot, jnp.zeros((2, 2), jnp.int32)], axis=1)
 
 
 def last_fused_kernel(
-    meta_ref, dqkv_ref, wqkv_ref, x_ref, dmix_ref, gain_ref, q_ref, bias_ref, sums_ref, fc1_ref, rel_ref,
+    meta_ref, dqkv_ref, wqkv_ref, x_ref, dmix_ref, gain_ref, dwq_ref, dwp_ref, bias_ref, sums_ref, fc1_ref, rel_ref,
     all_ref, shard_ref, total_ref, rels_ref, ln_ref,
-    grad_ref, ln_acc, *rest,
+    grad_ref, ln_acc, q_ref, *rest,
 ):
     w = pl.program_id(0)
     end = pl.num_programs(0) - 1
@@ -848,15 +1083,19 @@
             return q_ref.at[img, pl.ds(row, half)]
 
         streams.append(Halving(source, own, got, sems, order, half))
-    one, two = streams
     rest = rest[14:]
     small, rel, ln = [SmallSum(*rest[4 * n : 4 * n + 4]) for n in range(3)]
     back = Homeward(grad_ref, all_ref, rest[12])
 
     def start():
+        groups = q_ref.shape[0]
+        wide, share = 3 * D // groups, D // groups
+        for i in range(groups):
+            q_ref[i] = jnp.concatenate(
+                [dwq_ref[:, wide * i : wide * i + wide], dwp_ref[:, share * i : share * i + share]], axis=1
+            )
         greet()
-        one.first()
-        two.first()
+        each(streams, "first")()
 
     def prepare():
         for r in range(2):
@@ -870,19 +1109,6 @@
         rel.send(0)
         ln_acc[...] = jnp.zeros_like(ln_acc)
 
-    def done(k):
-        one.step_done(k)
-        two.step_done(k)
-
-    def step(k):
-        one.step(k)
-        two.step(k)
-
-    def first_done():
-        one.first_done()
-        two.first_done()
-        step(0)
-
     def middle():
         small.add(0)
         rel.add(0)
@@ -899,11 +1125,11 @@
         w,
         {
             0: [start, prepare],
-            2: [first_done],
+            2: [each(streams, "first_done"), each(streams, "step", 0)],
             3: [middle, back.send_core_outer],
-            6: [lambda: done(0), lambda: step(1), finish],
-            8: [lambda: done(1), lambda: step(2), back.send_cross],
-            12: [lambda: done(2), lambda: step(3), back.send_core_inner],
+            6: [each(streams, "step_done", 0), each(streams, "step", 1), finish],
+            8: [each(streams, "step_done", 1), each(streams, "step", 2), back.send_cross],
+            12: [each(streams, "step_done", 2), each(streams, "step", 3), back.send_core_inner],
         },
     )
 
@@ -916,7 +1142,7 @@
     unit, inverse = norm(x_ref[...].astype(F32))
     ln_acc[0] += fold8(dn * unit)
     ln_acc[1] += fold8(dn)
-    grad = dmix_ref[...].astype(F32) + norm_back(dn, unit, inverse, gain_ref[...])
+    grad = dmix_ref[...].astype(F32) + norm_back(dn, unit, inverse, gain_ref[0:1])
     grad_ref[w] = grad.astype(BF16)
 
     @pl.when(w == end)
@@ -926,18 +1152,18 @@
         ln.mine[1:2] = jnp.sum(ln_acc[1], axis=0, keepdims=True)
         ln.mine[2:] = jnp.zeros((6, D), F32)
         ln.send(0)
-        done(3)
+        each(streams, "step_done", 3)()
         ln.add(0)
         ln.send(1)
-        shard_ref[:half] = one.result()
-        shard_ref[half:] = two.result()
+        for n, stream in enumerate(streams):
+            shard_ref[half * n : half * n + half] = stream.result()
         back.keep().wait()
         back.finish()
         ln.add(1)
         ln_ref[...] = ln.mine[...]
 
 
-def last_fused(meta, dqkv, wqkv, x, dmix, gain, q_grad, bias_sums, sums, fc1_sum, rel_acc):
+def last_fused(meta, dqkv, wqkv, x, dmix, gain, dwq, dwp, bias_sums, sums, fc1_sum, rel_acc):
     cap = meta.shape[0]
     sds = jax.ShapeDtypeStruct
     half = SHARD_ROWS // 2
@@ -949,11 +1175,13 @@
             num_scalar_prefetch=1,
             grid=(cap,),
             in_specs=[
-                per_window(TW, 3 * D), whole((D, 3 * D)), per_window(TW, D), per_window(TW, D), whole((1, D)),
-                anywhere, whole((2, 8, D)), whole((4, 8, D)), whole((8, FF)), whole((LANES, 256)),
+                per_window(TW, 3 * D), whole((D, 3 * D)), per_window(TW, D), per_window(TW, D), whole((8, D)),
+                whole((D, 3 * D)), whole((D, D)), whole((2, 8, D)), whole((4, 8, D)), whole((8, FF)), whole((LANES, 256)),
             ],
             out_specs=[anywhere] + [whole(shape) for shape, _ in sums_out],
-            scratch_shapes=[pltpu.VMEM((cap, TW, D), BF16), pltpu.VMEM((2, 8, D), F32)]
+            scratch_shapes=[
+                pltpu.VMEM((cap, TW, D), BF16), pltpu.VMEM((2, 8, D), F32), pltpu.VMEM((8, D, SHARD_COLS), BF16)
+            ]
             + Halving.scratch(half) * 2
             + SmallSum.scratch((16, D)) + SmallSum.scratch((64, 256)) + SmallSum.scratch((8, D))
             + [pltpu.SemaphoreType.DMA((5,))],
@@ -961,7 +1189,7 @@
         out_shape=[sds((cap + NEAR_CORE + NEAR_CROSS, TW, D), BF16)] + [sds(shape, dtype) for shape, dtype in sums_out],
         compiler_params=pltpu.CompilerParams(vmem_limit_bytes=VMEM_LIMIT, collective_id=2, has_side_effects=True),
         cost_estimate=pl.CostEstimate(flops=20_000_000_000, bytes_accessed=50_000_000, transcendentals=0),
-    )(meta, dqkv, wqkv, x, dmix, gain, q_grad, bias_sums, sums, fc1_sum, rel_acc)
+    )(meta, dqkv, wqkv, x, dmix, gain, dwq, dwp, bias_sums, sums, fc1_sum, rel_acc)
 
 
 def window_plan(images, bands):
@@ -1036,37 +1264,35 @@
     axes = ("img", "band")
 
     part, wide = w_qkv.shape
+    close = near(images, bands, band_rows)
+    fused = close and groups == 8
     small = jnp.concatenate(
         [
             ln1_gain, ln1_bias, q_bias, v_bias, proj_bias, ln2_gain, ln2_bias, fc2_bias, fc1_bias,
             rel_rows.reshape(-1), rel_cols.reshape(-1),
         ]
     )
-    small_rows = -(-small.shape[0] // (wide * 8)) * 8
-    small = jnp.pad(small, (0, small_rows * wide - small.shape[0])).reshape(small_rows, wide)
-    first = lax.all_gather(jnp.concatenate([w_qkv, small], axis=0), axes, axis=0, tiled=False)
-    first = first.reshape(groups, bands, part + small_rows, wide)
-    second = lax.all_gather(
-        jnp.concatenate([w_fc1, w_fc2.T, w_proj], axis=1), axes, axis=0, tiled=False
-    ).reshape(groups, bands * part, -1)
-    wqkv = first[:, :, :part].transpose(1, 2, 0, 3).reshape(D, 3 * D)
-    tail = first[:, :, part:].reshape(groups, bands, small_rows * wide)
+    block_cols = wide + w_proj.shape[1]
+    small_rows = -(-small.shape[0] // (block_cols * 16)) * 16
+    small = jnp.pad(small, (0, small_rows * block_cols - small.shape[0])).reshape(small_rows, block_cols)
+    block = jnp.concatenate([jnp.concatenate([w_qkv, w_proj], axis=1), small], axis=0)
+    if fused:
+        first, ext, gext = entry(block, image_tokens, out_grad)
+    else:
+        first = lax.all_gather(block, axes, axis=0, tiled=False).reshape(groups, bands, part + small_rows, block_cols)
+        ext, gext = extend(image_tokens, band), extend(out_grad, band)
+    ff = lax.all_gather(jnp.concatenate([w_fc1, w_fc2.T], axis=1), axes, axis=0, tiled=False).reshape(
+        groups, bands * part, -1
+    )
+    tail = first[:, :, part:].reshape(groups, bands, small_rows * block_cols)
     share = D // groups
-    vectors = tail[:, 0, : 8 * share].reshape(groups, 8, share).transpose(1, 0, 2).reshape(8, 1, D).astype(F32)
+    vectors = tail[:, 0, : 8 * share].reshape(groups, 8, share).transpose(1, 0, 2).reshape(8, D).astype(F32)
     fc1_shift = tail[:, 0, 8 * share : 8 * share + FF // groups].reshape(1, FF).astype(F32)
     at = 8 * share + FF // groups
     rels = tail[0, :, at : at + 2 * RELS * (HEAD // bands)].reshape(bands, 2, RELS, HEAD // bands)
     rels = rels.transpose(1, 2, 0, 3).reshape(2, RELS, HEAD)
-    gain1, shift1, qb, vb, pb, gain2, shift2, b2 = [vectors[i] for i in range(8)]
-    bias = jnp.concatenate([qb, jnp.zeros_like(qb), vb], axis=1)
-    inner = FF // groups
-    ff = second[:, :, : 2 * inner]
-    wproj = second[:, :, 2 * inner :].transpose(1, 0, 2).reshape(D, D)
-
     plan = jnp.asarray(window_plan(images, bands))[band]
     image, window = plan[:, 0], plan[:, 1]
-    close = near(images, bands, band_rows)
-    fused = close and groups == 8
     ext_per = band_rows + 2 * HALO if close else bands * band_rows + 12
     base = band_rows * band - HALO if close else -6
     live = window >= 0
@@ -1081,50 +1307,68 @@
     ext_rows = images * ext_per
 
     ka, kb, kback = key_constants()
-    ext = extend(image_tokens, band).reshape(ext_rows, SIDE, D)
-    x, normed1, qkv, probs, inv, att = attention_forward(
-        meta, ext, gain1, shift1, wqkv, bias, rel_table(rels[0], rels[1], True), ka, kb
+    ext, gext = ext.reshape(ext_rows, SIDE, D), gext.reshape(ext_rows, SIDE, D)
+    if not fused:
+        weights = first[:, :, :part].transpose(1, 2, 0, 3)
+        wqkv, wproj = weights[..., :wide].reshape(D, 3 * D), weights[..., wide:].reshape(D, D)
+    x, g, normed1, qkv, probs, inv, att, *weights = attention_forward(
+        meta, ext, gext, vectors, first if fused else wqkv, rel_table(rels[0], rels[1], True), ka, kb
     )
-    gext = extend(out_grad, band).reshape(ext_rows, SIDE, D)
-    out_win, g, normed2, act, d_pre, d_mixed, d_att, sums, sum_fc1 = feed_forward(
-        meta, gext, x, att, wproj, pb, gain2, shift2, ff, fc1_shift, b2, NEAR_CORE + NEAR_CROSS if fused else 0
+    if fused:
+        wqkv, wproj = weights
+    out_win, normed2, act, d_pre, d_mixed, d_att, sums, sum_fc1 = feed_forward(
+        g, x, att, wproj, vectors, ff, fc1_shift, 0
     )
+
     def flat(a):
-        return a.reshape(cap * TW, a.shape[-1])
+        return a.reshape(-1, a.shape[-1])
 
     def weight_grad(left, right):
         return jnp.einsum("td,te->de", flat(left), flat(right), preferred_element_type=F32).astype(BF16)
 
+    if fused:
+        inner = (band == 1) | (band == 2)
+        to_core = lax.dynamic_slice_in_dim(out_win, jnp.where(inner, NEAR_CROSS, 0), NEAR_CORE, 0)
+        core_out = lax.ppermute(to_core, "band", CORE)
+        cross_out = lax.ppermute(out_win[:NEAR_CROSS], "band", CROSS)
     d_fc2 = weight_grad(g, act)
     d_fc1 = weight_grad(normed2, d_pre)
     d_proj = weight_grad(att, d_mixed)
+    if fused:
+        d_fc1, d_fc2, core_out, cross_out = lax.optimization_barrier((d_fc1, d_fc2, core_out, cross_out))
     d_qkv, rel_acc, bias_sums, *done = attention_backward(
         meta, qkv, probs, inv, att, d_att, rel_table(rels[0], rels[1], False), kback,
-        (d_fc1, d_fc2, out_win) if fused else (),
+        (d_fc1, d_fc2) if fused else (),
     )
     d_wqkv = weight_grad(normed1, d_qkv)
 
     if fused:
-        q_grad = jnp.concatenate(
-            [d_wqkv.reshape(D, groups, wide), d_proj.reshape(D, groups, share)], axis=2
-        ).transpose(1, 0, 2)
-        g_fc1, g_fc2, all_out = done
+        partial, g_fc2 = done
+
+        def fold(value, axis, bit, step):
+            mine = lax.dynamic_index_in_dim(value, bit, axis, keepdims=False)
+            other = lax.dynamic_index_in_dim(value, 1 - bit, axis, keepdims=False)
+            came = lax.ppermute(other, "img", [(i, i ^ step) for i in range(groups)])
+            return mine.astype(F32) + came.astype(F32)
+
+        partial = fold(partial, 1, group // 4, 4).astype(BF16)
+        g_fc1 = fold(partial, 1, group // 2 % 2, 2).reshape(part, FF // groups)
         all_grad, q_shard, total, rel_total, ln_total = last_fused(
-            meta, d_qkv, wqkv, x, d_mixed, gain1, q_grad, bias_sums, sums, sum_fc1, rel_acc
-        )
-        output, input_grad = home(
-            home_table(window_plan(images, bands), pad_offsets, band, band_rows), (all_out, all_grad), (BF16, F32),
-            band_rows,
-        )
-        g_qkv, g_proj = q_shard[:, :wide], q_shard[:, wide:]
-        ln_total = ln_total[:2]
-        bias_total, sum_total, fc1_total = total[:2], total[2:6], total[6:10].reshape(FF)
-        own = rel_total.reshape(HEAD, 2, LANES)[:, :, :RELS].transpose(1, 2, 0)
-        d_rel_rows, d_rel_cols = own[0][::-1], own[1]
+            meta, d_qkv, wqkv, x, d_mixed, vectors, d_wqkv, d_proj, bias_sums, sums, sum_fc1, rel_acc
+        )
+        output, input_grad, shares, b1_share, d_rel_rows, d_rel_cols, g_qkv, g_proj, g_fc2 = home(
+            home_table(window_plan(images, bands), pad_offsets, group, band, band_rows),
+            (out_win, core_out, cross_out, all_grad, total, ln_total, rel_total, q_shard, g_fc2), band_rows,
+        )
+        ln1g, ln1b, qb, vb, pb, ln2g, ln2b, b2 = [share.reshape(-1) for share in shares]
+        return (
+            output, input_grad, ln1g, ln1b, g_qkv, qb, vb, d_rel_rows, d_rel_cols, g_proj, pb, ln2g, ln2b, g_fc1,
+            b1_share.reshape(-1), g_fc2, b2,
+        )
     else:
         out_ext = scatter(meta, out_win, ext_rows).reshape(images, ext_per, SIDE, D)
         output = collect(out_ext, band, images, band_rows).astype(BF16)
-        in_ext, sums1 = last_norm(meta, d_qkv, wqkv, x, d_mixed, gain1, ext_rows)
+        in_ext, sums1 = last_norm(meta, d_qkv, wqkv, x, d_mixed, vectors, ext_rows)
         input_grad = collect(in_ext.reshape(images, ext_per, SIDE, D), band, images, band_rows)
 
         def reduce(grad):

time: 586 us -> 482 us (0.82)
  local copies, waits for them, and re-layouts: 70.6 us -> 19.1 us
  waiting for transfers between devices: 45.5 us -> 0.05 us
  other arithmetic: 36.1 us -> 8.66 us
  Pallas kernels: 344 us -> 367 us
    all_gather x2 -> x1, waiting for transfers between devices: 45.5 us -> 0.02 us  [shards(): lax.all_gather(jnp.concatenate([w_fc1, w_fc2.T], axis=1), axes, axis=0, t...]
    select_n x6 -> x0, other arithmetic: 16 us -> none  [the longest x2 8.28 us: extend(): from_core = lax.ppermute(jnp.where(odd, top, bottom), 'band', CORE)]
    reshape x9 -> x2, local copies, waits for them, and re-layouts: 15.8 us -> 0.11 us  [the longest x1 0.09 us: shards(): tail = first[:, :, part:].reshape(groups, bands, small_rows * block_cols)]
    pallas_call x2 -> x3, Pallas kernels: 212 us -> 226 us  [the longest x1 92.9 us: feed_forward(): pl.pallas_call(mlp_kernel, grid=(rows // tile,), in_specs=[tiled(D), tile...]
    slice x8 -> x2, local copies, waits for them, and re-layouts: 15 us -> 1.16 us  [the longest x1 1.05 us: shards(): tail = first[:, :, part:].reshape(groups, bands, small_rows * block_cols)]
    concatenate x5 -> x2, other arithmetic: 10.7 us -> 3.42 us  [the longest x1 1.72 us: shards(): jnp.concatenate([w_fc1, w_fc2.T], axis=1)]
    unnamed x28 -> x29, local copies, waits for them, and re-layouts: 13.3 us -> 6.44 us
    pallas_call x1, Pallas kernels: 52 us -> 58.5 us  [attention_forward(): pl.pallas_call(fwd_kernel, grid_spec=pltpu.PrefetchScalarGridSpec(num_sca...]
  transfers between devices with their start and end apart: 6 -> 5, of which waited for: 2 -> 0; matrix products, arithmetic and copies ran while one was open for 10% -> 14% of each run, Pallas kernels for 9% -> 43%
where the time goes in v4:
time: 482 us; the launch traced here: 476 us
  Pallas kernels  367 us (76%)
  matrix products  62.5 us (13%)
  local copies, waits for them, and re-layouts  19.1 us (4%)
  between operations  14.7 us (3%)
  other arithmetic  8.66 us (2%)
    pallas_call x1, Pallas kernels, feed_forward(): pl.pallas_call(mlp_kernel, grid=(rows // tile,), in_specs=[tiled(D), tile...  92.9 us
    pallas_call x1, Pallas kernels, last_fused(): pl.pallas_call(last_fused_kernel, grid_spec=pltpu.PrefetchScalarGridSpec(...  69.9 us
    pallas_call x1, Pallas kernels, attention_backward(): pl.pallas_call(attn_bwd_kernel, grid_spec=pltpu.PrefetchScalarGridSpec(nu...  69 us
    pallas_call x1, Pallas kernels, entry(): pl.pallas_call(entry_kernel, in_specs=[inside, anywhere, anywhere], out_s...  63.8 us
    dot_general x4, matrix products, weight_grad(): jnp.einsum('td,te->de', flat(left), flat(right), preferred_element_type=F32)  62.5 us
    pallas_call x1, Pallas kernels, attention_forward(): pl.pallas_call(fwd_kernel, grid_spec=pltpu.PrefetchScalarGridSpec(num_sca...  58.5 us
    pallas_call x1, Pallas kernels, home(): pl.pallas_call(home_kernel, grid_spec=pltpu.PrefetchScalarGridSpec(num_sc...  12.8 us
  transfers between devices with their start and end apart: 5, of which 0 were waited for; matrix products, arithmetic and copies ran while one was open for 14% of the time, Pallas kernels for 43%

profile of v4, /device:TPU:0, one launch (start us, length us, event | category | flops | bytes accessed | tf_op | source)
XLA Modules:
  0.0 475.9 jit_solution(6893312471004550831)
XLA Ops:
  7.2 1.7 pad_maximum_fusion
  9.0 0.8 copy.75
  9.9 0.8 copy.76
  10.7 6.1 %concatenate.65 = bf16[2016]{0:T(1024)(128)(2,1)S(1)} concatenate(bf16[96]{0:T(256)(128)(2,1)} %param.25, bf16[96]{0:T(256)(128)(2,1)} %param.26, bf16[96]{0:T(256)(128)(2,1)} %param.28, bf16[96]{0:T(256)(128)(2,1)} %param.29, bf16[96]{0:T(256)(128)(2,1)} %param.33, bf16[96]{0:T(256)(128)(2,1)} %param.34, bf16[96]{0:T(256)(128)(2,1)} %param.35, bf16[96]{0:T(256)(128)(2,1)} %param.39, ...), dimensions={0} | concatenate | bytes 8064 | tf_op jit(solution)/shard_map/concatenate | solution.py:1269
  16.9 1.7 pad_maximum_fusion.1.block_ref
  18.6 63.8 %shard_map.350 = (bf16[8,4,208,384]{3,2,1,0:T(8,128)(2,1)}, bf16[2,40,64,768]{3,2,1,0:T(8,128)(2,1)}, bf16[2,40,64,768]{3,2,1,0:T(8,128)(2,1)}) custom-call(bf16[208,384]{1,0:T(8,128)(2,1)} %pad_maximum_fusion.1.block_ref, bf16[2,16,64,768]{3,2,1,0:T(8,128)(2,1)} %x_ref.1, bf16[2,16,64,768]{3,2,1,0:T(8,128)(2,1)} %g_ref.1), custom_call_target="tpu_custom_call" | custom-call | tf_op jit(solution)/shard_map/pallas_call | solution.py:699
  82.4 1.0 slice.44
  89.4 0.8 fusion.2.table_ref
  90.9 58.5 %shard_map.351 = (bf16[13,224,768]{2,1,0:T(8,128)(2,1)}, bf16[13,224,768]{2,1,0:T(8,128)(2,1)}, bf16[13,224,768]{2,1,0:T(8,128)(2,1)}, bf16[13,224,2304]{2,1,0:T...) custom-call(s32[13,4]{1,0:T(8,128)} %pad_add_fusion.meta_ref, ...), custom_call_target="tpu_custom_call" | custom-call | flops 40000000000 | bytes 80000000 | tf_op jit(solution)/shard_map/pallas_call | solution.py:222
  149.4 92.9 %shard_map.352 = (bf16[2912,768]{1,0:T(8,128)(2,1)}, bf16[2912,768]{1,0:T(8,128)(2,1)}, bf16[2912,3072]{1,0:T(8,128)(2,1)}, bf16[2912,3072]{1,0:T(8,128)(2,1)}, ...) custom-call(bf16[2912,768]{1,0:T(8,128)(2,1)} %bitcast.91, ...), custom_call_target="tpu_custom_call" | custom-call | flops 60000002048 | bytes 80000000 | tf_op jit(solution)/shard_map/pallas_call | solution.py:322
  242.4 21.0 %convolution_convert_fusion.rest_1_ = bf16[768,3072]{1,0:T(8,128)(2,1)} fusion(bf16[2912,768]{1,0:T(8,128)(2,1)} %bitcast.92, bf16[2912,3072]{1,0:T(8,128)(2,1)} %get-tuple-element.77), kind=kOutput, calls=%fused_computation.2 | convolution fusion | flops 13742899200 | bytes 27082752 | tf_op jit(solution)/shard_map/td,te->de/dot_general | solution.py:1327
  264.2 0.9 collective-permute-start.1
  265.1 5.1 %convolution_convert_fusion.2.dwp_ref = bf16[768,768]{1,0:T(8,128)(2,1)} fusion(bf16[2912,768]{1,0:T(8,128)(2,1)S(1)} %bitcast.89, bf16[2912,768]{1,0:T(8,128)(2,1)S(1)} %bitcast.85), kind=kOutput, calls=%fused_computation.4 | convolution fusion | flops 3435724800 | bytes 10125312 | tf_op jit(solution)/shard_map/td,te->de/dot_general | solution.py:1327
  270.2 19.8 %convolution_convert_fusion.1.rest_0_ = bf16[768,3072]{1,0:T(8,128)(2,1)} fusion(bf16[2912,768]{1,0:T(8,128)(2,1)S(1)} %bitcast.94, bf16[2912,3072]{1,0:T(8,128)(2,1)} %get-tuple-element.76), kind=kOutput, calls=%fused_computation.3 | convolution fusion | flops 13742899200 | bytes 27082752 | tf_op jit(solution)/shard_map/td,te->de/dot_general | solution.py:1327
  290.1 69.0 %shard_map.353 = (bf16[13,224,2304]{2,1,0:T(8,128)(2,1)}, f32[128,256]{1,0:T(8,128)}, f32[2,8,768]{2,1,0:T(8,128)}, bf16[2,2,2,96,384]{4,3,2,1,0:T(8,128)(2,1)}, f32[192,384]{1,0:T(8,128)}) custom-call(s32[13,4]{1,0:T(8,128)} %pad_add_fusion.meta_ref, bf16[13,224,2304]{2,1,0:T(8,128)(2,1)} %get-tuple-element.80.qkv_ref, ...), custom_call_target="tpu_custom_call" | custom-call | flops 60000002048 | bytes 80000000 | tf_op jit(solution)/shard_map/pallas_call | solution.py:809
  359.1 1.0 dynamic-slice_bitcast_fusion
  360.5 16.6 %bitcast_convert_fusion.dwq_ref = bf16[768,2304]{1,0:T(8,128)(2,1)} fusion(bf16[13,224,768]{2,1,0:T(8,128)(2,1)} %get-tuple-element.89, bf16[13,224,2304]{2,1,0:T(8,128)(2,1)} %get-tuple-element.86.dqkv_ref), kind=kOutput, calls=%fused_computation.1 | convolution fusion | flops 10307174400 | bytes 21430272 | tf_op jit(solution)/shard_map/td,te->de/dot_general | solution.py:1327
  377.3 2.1 collective-permute-start.3
  379.3 69.9 %shard_map.354 = (bf16[25,224,768]{2,1,0:T(8,128)(2,1)}, f32[192,384]{1,0:T(8,128)}, f32[16,768]{1,0:T(8,128)}, f32[64,256]{1,0:T(8,128)}, f32[8,768]{1,0:T(8,128)}) custom-call(s32[13,4]{1,0:T(8,128)} %pad_add_fusion.meta_ref, bf16[13,224,2304]{2,1,0:T(8,128)(2,1)} %get-tuple-element.86.dqkv_ref, bf16[768,2304]{1,0:T(8,128)(2,1)} %get-tuple-element.87.wqkv_ref, ...), custom_call_target="tpu_custom_call" | custom-call | flops 20000000000 | bytes 50000000 | tf_op jit(solution)/shard_map/pallas_call | solution.py:1172
  449.3 12.8 %shard_map.355 = (bf16[2,16,64,768]{3,2,1,0:T(8,128)(2,1)}, f32[2,16,64,768]{3,2,1,0:T(8,128)}, f32[1,96]{1,0:T(1,128)}, f32[1,96]{1,0:T(1,128)}, f32[1,96]{1,0:...) custom-call(s32[2,32]{1,0:T(2,128)} %concatenate.63.table_ref, ...), custom_call_target="tpu_custom_call" | custom-call | flops 500000000 | bytes 20000000 | tf_op jit(solution)/shard_map/pallas_call | solution.py:1033
  462.1 1.9 copy.82
  463.9 1.4 copy.80
  465.3 1.4 copy.81
  466.7 1.3 reduce.2
  (78 shorter events, 8.9 us)
Async XLA Ops:
  7.2 142.2 %all-gather.3.cloned.1.call-start = ((), (), s32[]{:S(2)}) async-start(), calls=%async_computation | async-start | bytes 9732096 | tf_op jit(solution)/shard_map/all_gather | solution.py:1284
  9.0 75.7 %copy-start.1 = (s32[2,2]{1,0:T(2,128)S(1)}, s32[2,2]{1,0:T(2,128)}, u32[]{:S(2)}) copy-start(s32[2,2]{1,0:T(2,128)} %param.24) | copy-start | bytes 52
  242.4 22.7 %slice-start = ((s8[4472832]{0:T(1024)(128)(4,1)}), s8[4194304]{0:T(1024)(128)(4,1)S(1)}, s32[]{:S(2)}) async-start(s8[4472832]{0:T(1024)(128)(4,1)} %bitcast.84), calls=%async_computation.1 | async-start | bytes 8388608
  242.4 22.7 %slice-start.2 = ((s8[4472832]{0:T(1024)(128)(4,1)}), s8[4194304]{0:T(1024)(128)(4,1)S(1)}, s32[]{:S(2)}) async-start(s8[4472832]{0:T(1024)(128)(4,1)} %bitcast.87), calls=%async_computation.3 | async-start | bytes 8388608
  242.4 21.1 %copy-start = (bf16[2912,768]{1,0:T(8,128)(2,1)S(1)}, bf16[2912,768]{1,0:T(8,128)(2,1)}, u32[]{:S(2)}) copy-start(bf16[2912,768]{1,0:T(8,128)(2,1)} %get-tuple-element.74) | copy-start | bytes 13418500
  242.4 22.7 %slice-start.1 = ((s8[4472832]{0:T(1024)(128)(4,1)}), s8[278528]{0:T(1024)(128)(4,1)S(1)}, s32[]{:S(2)}) async-start(s8[4472832]{0:T(1024)(128)(4,1)} %bitcast.84), calls=%async_computation.2 | async-start | bytes 557056
  242.4 22.7 %slice-start.3 = ((s8[4472832]{0:T(1024)(128)(4,1)}), s8[278528]{0:T(1024)(128)(4,1)S(1)}, s32[]{:S(2)}) async-start(s8[4472832]{0:T(1024)(128)(4,1)} %bitcast.87), calls=%async_computation.4 | async-start | bytes 557056
  263.5 6.7 %slice-start.4 = ((s8[4472832]{0:T(1024)(128)(4,1)}), s8[4194304]{0:T(1024)(128)(4,1)S(1)}, s32[]{:S(2)}) async-start(s8[4472832]{0:T(1024)(128)(4,1)} %bitcast.93), calls=%async_computation.5 | async-start | bytes 8388608
  263.7 26.3 %collective-permute-start = (bf16[7,224,768]{2,1,0:T(8,128)(2,1)S(1)}, bf16[7,224,768]{2,1,0:T(8,128)(2,1)S(1)}, u32[]{:S(2)}, u32[]{:S(2)}) collective-permute-start(bf16[7,224,768]{2,1,0:T(8,128)(2,1)S(1)} %constant_dynamic-slice_fusion), channel_id=1, source_target_pairs={{0,1},{1,0},{2,3},{3,2},{4,5},{5,4},{6,7},{7,6},{8,9},{9,8},{10,11... | collective-permute-start | bytes 7225352 | tf_op jit(solution)/shard_map/ppermute | solution.py:1332
  264.2 25.9 %collective-permute-start.1 = (bf16[5,224,768]{2,1,0:T(8,128)(2,1)S(1)}, bf16[5,224,768]{2,1,0:T(8,128)(2,1)S(1)}, u32[]{:S(2)}, u32[]{:S(2)}) collective-permute-start(bf16[5,224,768]{2,1,0:T(8,128)(2,1)S(1)} %bitcast.60), channel_id=1, source_target_pairs={{1,2},{2,1},{5,6},{6,5},{9,10},{10,9},{13,14},{14,13},{17,18},{18,... | collective-permute-start | bytes 5160968 | tf_op jit(solution)/shard_map/ppermute | solution.py:1333
  265.1 5.1 %slice-start.5 = ((s8[4472832]{0:T(1024)(128)(4,1)}), s8[278528]{0:T(1024)(128)(4,1)S(1)}, s32[]{:S(2)}) async-start(s8[4472832]{0:T(1024)(128)(4,1)} %bitcast.93), calls=%async_computation.6 | async-start | bytes 557056
  290.0 69.0 %copy-start.3 = (bf16[5,224,768]{2,1,0:T(8,128)(2,1)}, bf16[5,224,768]{2,1,0:T(8,128)(2,1)S(1)}, u32[]{:S(2)}) copy-start(bf16[5,224,768]{2,1,0:T(8,128)(2,1)S(1)} %collective-permute-done.1.cross_ref) | copy-start | bytes 5160964
  290.0 69.0 %copy-start.2 = (bf16[7,224,768]{2,1,0:T(8,128)(2,1)}, bf16[7,224,768]{2,1,0:T(8,128)(2,1)S(1)}, u32[]{:S(2)}) copy-start(bf16[7,224,768]{2,1,0:T(8,128)(2,1)S(1)} %collective-permute-done.core_ref) | copy-start | bytes 7225348
  360.1 17.0 %collective-permute-start.2 = (bf16[2,2,96,384]{3,2,1,0:T(8,128)(2,1)S(1)}, bf16[2,2,96,384]{3,2,1,0:T(8,128)(2,1)S(1)}, u32[]{:S(2)}, u32[]{:S(2)}) collective-permute-start(bf16[2,2,96,384]{3,2,1,0:T(8,128)(2,1)S(1)} %dynamic-slice_bitcast_fusion), channel_id=1, source_target_pairs={{0,16},{4,20},{8,24},{12,28},{16,0},{20,4},{24,8},{28,12},{1,17},{... | collective-permute-start | bytes 884744 | tf_op jit(solution)/shard_map/ppermute | solution.py:1351
  360.5 16.6 %copy-start.4 = (bf16[2,2,2,96,384]{4,3,2,1,0:T(8,128)(2,1)S(1)}, bf16[2,2,2,96,384]{4,3,2,1,0:T(8,128)(2,1)}, u32[]{:S(2)}) copy-start(bf16[2,2,2,96,384]{4,3,2,1,0:T(8,128)(2,1)} %get-tuple-element.113) | copy-start | bytes 1769476
  377.3 90.7 %collective-permute-start.3 = (bf16[2,96,384]{2,1,0:T(8,128)(2,1)S(1)}, bf16[2,96,384]{2,1,0:T(8,128)(2,1)S(1)}, u32[]{:S(2)}, u32[]{:S(2)}) collective-permute-start(bf16[2,96,384]{2,1,0:T(8,128)(2,1)S(1)} %dynamic-slice_bitcast_fusion.1), channel_id=1, source_target_pairs={{0,8},{4,12},{8,0},{12,4},{16,24},{20,28},{24,16},{28,20},{1,9},{5... | collective-permute-start | bytes 442376 | tf_op jit(solution)/shard_map/ppermute | solution.py:1351
Sparse Core Ops, SparseCore 0:
  11.5 99.2 all-gather.2

commit v5 on v4

--- a/solution.py
+++ b/solution.py
@@ -77,11 +77,11 @@
     return jnp.sum(x.reshape(x.shape[0] // 8, 8, x.shape[1]), axis=0)
 
 
-def roll_rows(x, sign):
+def roll_rows(x, forward):
     out = []
     for a in range(WIN):
         piece = x[STRIDE * a : STRIDE * a + STRIDE]
-        by = (sign * (13 - a)) % LANES
+        by = (a - 13) % LANES if forward else a
         out.append(pltpu.roll(piece, by, 1) if by else piece)
     return jnp.concatenate(out, axis=0)
 
@@ -98,7 +98,7 @@
     lane = iota((TW, LANES), 1)
     low_half = lane < 64
     rc = mm(q, table)
-    both = jnp.where((lane & 31) < 16, roll_rows(rc[:, :LANES], -1), roll_cols(rc[:, LANES:], 3))
+    both = jnp.where((lane & 31) < 16, roll_rows(rc[:, :LANES], True), roll_cols(rc[:, LANES:], 3))
     high = both.astype(BF16)
     rest = (both - high.astype(F32)).astype(BF16)
     extra = jnp.where((lane & 63) < 32, high, rest)
@@ -193,7 +193,7 @@
         base[t[real], off + kr[real]] = 1.0
         base[t[real], off + 16 + kc[real]] = 1.0
     back = np.zeros_like(base)
-    back[t[real], kr[real]] = 1.0
+    back[t[real], 13 - kr[real]] = 1.0
     back[t[real], 16 + 13 - kc[real]] = 1.0
     base[~real, 14] = -1e30
     none = np.zeros_like(base)
@@ -205,14 +205,15 @@
 
 def rel_table(rel_rows, rel_cols, forward):
     def wide(rel):
-        turned = jnp.pad(rel.T, ((0, 0), (0, 32 - RELS)))
+        turned = jnp.pad(rel, ((0, 0), (0, 32 - RELS)))
         twice = jnp.concatenate([turned, turned], axis=1)
         none = jnp.zeros_like(twice)
         return jnp.concatenate(
             [jnp.concatenate([twice, none], 1), jnp.concatenate([none, twice], 1)], 0
         )
 
-    return jnp.concatenate([wide(rel_rows[::-1]), wide(rel_cols[::-1] if forward else rel_cols)], axis=1)
+    turn = (lambda rel: rel[:, ::-1]) if forward else (lambda rel: rel)
+    return jnp.concatenate([wide(turn(rel_rows)), wide(turn(rel_cols))], axis=1)
 
 
 def attention_forward(meta, ext, gext, vectors, wqkv, table, ka, kb):
@@ -269,7 +270,7 @@
     n2_ref[...] = n2
     acc_ref[...] = hidden + vec_ref[7:8]
     parts, inner = ff_ref.shape[0], ff_ref.shape[2] // 2
-    join = max(1, 768 // inner)
+    join = max(1, 1536 // inner)
     chunk = inner * join
     for c in range(parts // join):
         cols = slice(chunk * c, chunk * c + chunk)
@@ -586,10 +587,11 @@
             self.along_z(d).start()
         self.pass_on(0)
 
-    def run(self):
+    def run(self, then):
         for dz in range(1, 4):
             self.along_z(dz).wait_recv()
             self.pass_on(dz)
+        then()
         for dz in range(4):
             self.along_x(dz).wait_recv()
             self.along_y(1, dz).start()
@@ -609,6 +611,9 @@
         self.keep().wait()
 
 
+CROSS_HALO = 10
+
+
 class Edges:
     def __init__(self, rows, ext, zero, sems):
         self.rows, self.ext, self.zero, self.sems = rows, ext, zero, sems
@@ -630,7 +635,7 @@
     def core(self, sending):
         odd = self.band % 2
         far = self.own_rows - HALO
-        there = (1 - odd if sending else odd) * 0 + (odd if sending else 1 - odd) * (HALO + self.own_rows)
+        there = (odd if sending else 1 - odd) * (HALO + self.own_rows)
         return pltpu.make_async_remote_copy(
             src_ref=self.rows.at[:, pl.ds((1 - odd) * far, HALO)], dst_ref=self.ext.at[:, pl.ds(there, HALO)],
             send_sem=self.sems.at[3], recv_sem=self.sems.at[4], device_id=partner("c"), device_id_type=MESH,
@@ -639,16 +644,18 @@
     def cross(self, sending):
         img = lax.axis_index("img")
         m = 2 - self.band
-        far = self.own_rows - HALO
+        far = self.own_rows - CROSS_HALO
         to = m if sending else 1 - m
-        there = (1 - to) * (HALO + self.own_rows)
+        there = to * (HALO - CROSS_HALO) + (1 - to) * (HALO + self.own_rows)
         return pltpu.make_async_remote_copy(
-            src_ref=self.rows.at[m, pl.ds(m * far, HALO)], dst_ref=self.ext.at[to, pl.ds(there, HALO)],
+            src_ref=self.rows.at[m, pl.ds(m * far, CROSS_HALO)], dst_ref=self.ext.at[to, pl.ds(there, CROSS_HALO)],
             send_sem=self.sems.at[5], recv_sem=self.sems.at[6], device_id=(img, 3 - self.band), device_id_type=MESH,
         )
 
+    def start_cross(self):
+        pl.when(self.inner())(lambda: self.cross(True).start())
+
     def start(self):
-        pl.when(self.inner())(lambda: self.cross(True).start())
         self.core(True).start()
         self.keep().start()
 
@@ -671,6 +678,30 @@
         def _():
             for copy in self.empty():
                 copy.wait()
+
+
+def pack_kernel(wqkv_ref, wproj_ref, small_ref, relr_ref, relc_ref, w1_ref, w2t_ref, block_ref, ff_ref):
+    rows, wide = wqkv_ref.shape
+    block_ref[:rows, :wide] = wqkv_ref[...]
+    block_ref[:rows, wide:] = wproj_ref[...]
+    parts = [ref[...] for ref in (small_ref, relr_ref, relc_ref)]
+    rest = block_ref.shape[1] - sum(part.shape[1] for part in parts)
+    block_ref[rows:] = jnp.concatenate(parts + [jnp.zeros((small_ref.shape[0], rest), BF16)], axis=1)
+    inner = w1_ref.shape[1]
+    ff_ref[:, :inner] = w1_ref[...]
+    ff_ref[:, inner:] = w2t_ref[...]
+
+
+def pack(wqkv, wproj, small, relr, relc, w1, w2t):
+    rows = wqkv.shape[0]
+    return pl.pallas_call(
+        pack_kernel,
+        out_shape=[
+            jax.ShapeDtypeStruct((rows + small.shape[0], wqkv.shape[1] + wproj.shape[1]), BF16),
+            jax.ShapeDtypeStruct((rows, 2 * w1.shape[1]), BF16),
+        ],
+        cost_estimate=pl.CostEstimate(flops=0, bytes_accessed=1_000_000, transcendentals=0),
+    )(wqkv, wproj, small, relr, relc, w1, w2t)
 
 
 def entry_kernel(
@@ -684,10 +715,14 @@
     greet()
     gather = Gather(block_ref, all_ref, gsems)
     gather.begin()
-    for load, item in zip(loads, edges):
-        load.wait()
-        item.start()
-    gather.run()
+
+    def next_edges(n):
+        loads[n].wait()
+        edges[n].start_cross()
+        edges[n].start()
+
+    next_edges(0)
+    gather.run(lambda: next_edges(1))
     for item in edges:
         item.finish()
 
@@ -770,7 +805,7 @@
         dq = jnp.where(low_half, dqx[0][:, :LANES], dqx[1][:, :LANES])
         drc = jnp.where(low_half, dqx[0][:, LANES:], dqx[1][:, LANES:])
         part = lane & 63
-        rows = roll_rows(jnp.where(part < 16, drc, 0.0), 1)
+        rows = roll_rows(jnp.where(part < 16, drc, 0.0), False)
         cols_part = roll_cols(jnp.where((part >= 16) & (part < 32), drc, 0.0), LANES - 16)
         skew = jnp.concatenate([rows, cols_part], axis=1).astype(BF16)
         dq = dq + mm_nt(skew, table_ref[...])
@@ -829,7 +864,7 @@
         own = block[:64, :32] + block[64:, 64:96]
         return own[:, :RELS].T
 
-    return one(acc[:, :LANES])[::-1], one(acc[:, LANES:])
+    return one(acc[:, :LANES]), one(acc[:, LANES:])
 
 
 def put_window(target, y, acc_ref, row0):
@@ -928,21 +963,21 @@
 
 
 class SmallSum:
-    def __init__(self, mine, got_band, got_img, sems):
-        self.mine, self.got, self.sems = mine, (got_band, got_img), sems
+    def __init__(self, mine, got_band, got_img, sems, part):
+        self.mine, self.got, self.sems, self.part = mine, (got_band, got_img), sems, part
 
     @staticmethod
-    def scratch(shape):
+    def scratch(shape, part):
         return [
-            pltpu.VMEM(shape, F32), pltpu.VMEM((3,) + shape, F32), pltpu.VMEM((7,) + shape, F32),
+            pltpu.VMEM(shape, F32), pltpu.VMEM((3,) + shape, F32), pltpu.VMEM((7,) + part, F32),
             pltpu.SemaphoreType.DMA((2, 2, 7)),
         ]
 
     def copies(self, k):
         return [
             pltpu.make_async_remote_copy(
-                src_ref=self.mine, dst_ref=self.got[k].at[d], send_sem=self.sems.at[k, 0, d],
-                recv_sem=self.sems.at[k, 1, d], device_id=device, device_id_type=MESH,
+                src_ref=self.part(device[0]) if k else self.mine, dst_ref=self.got[k].at[d],
+                send_sem=self.sems.at[k, 0, d], recv_sem=self.sems.at[k, 1, d], device_id=device, device_id_type=MESH,
             )
             for d, device in enumerate(peers()[k])
         ]
@@ -951,22 +986,36 @@
         for copy in self.copies(k):
             copy.start()
 
-    def add(self, k):
-        copies = self.copies(k)
-        for copy in copies:
+    def add(self):
+        for copy in self.copies(0):
             copy.wait()
-        total = self.mine[...]
-        for d in range(len(copies)):
-            total = total + self.got[k][d]
-        self.mine[...] = total
+        self.mine[...] = self.mine[...] + self.got[0][0] + self.got[0][1] + self.got[0][2]
+
+    def result(self):
+        for copy in self.copies(1):
+            copy.wait()
+        total = self.part(lax.axis_index("img"))[...]
+        for d in range(7):
+            total = total + self.got[1][d]
+        return total
+
+
+def deal(rows_ref, parts_ref, rows, wide):
+    groups = parts_ref.shape[0]
+    share = D // groups
+    for i in range(groups):
+        parts_ref[i, :rows, :share] = rows_ref[:rows, share * i : share * i + share]
+        for k in range(wide):
+            at = share * (wide * i + k)
+            parts_ref[i, rows + k : rows + k + 1, :share] = rows_ref[rows + at // D : rows + at // D + 1, at % D : at % D + share]
 
 
 HOME_ROWS = 8
 
 
 def home_kernel(
-    table_ref, own_ref, core_ref, cross_ref, grad_ref, total_ref, ln_ref, rel_ref, q_ref, fc2_ref,
-    output_ref, input_grad_ref, vec_refs, b1_ref, relr_ref, relc_ref, wq_ref, wp_ref, w2_ref,
+    table_ref, own_ref, core_ref, cross_ref, grad_ref, total_ref, ln_ref, rel_ref, q_ref,
+    output_ref, input_grad_ref, vec_refs, b1_ref, relr_ref, relc_ref, wq_ref, wp_ref,
     out_ref, sems,
 ):
     step = pl.program_id(0)
@@ -974,7 +1023,6 @@
     m = step // per_image
     top, left = table_ref[m, 25], table_ref[m, 26]
     first = table_ref[m, 27] + (step - m * per_image) * HOME_ROWS
-    group, band = table_ref[m, 28], table_ref[m, 29]
 
     @pl.when(step == 0)
     def _():
@@ -986,25 +1034,14 @@
         for load in loads:
             load.start()
         share = vec_refs[0].shape[1]
-
-        def cut(rows, width):
-            mine = jnp.zeros((rows.shape[0], width), F32)
-            for i in range(rows.shape[1] // width):
-                mine = mine + jnp.where(group % (rows.shape[1] // width) == i, rows[:, width * i : width * i + width], 0.0)
-            return mine
-
-        ln, total = cut(ln_ref[...], share), cut(total_ref[...], share)
+        ln, total = ln_ref[:, :share], total_ref[:, :share]
         for ref, row in zip(vec_refs, (ln[0:1], ln[1:2], total[0:1], total[1:2], total[5:6], total[3:4], total[4:5], total[2:3])):
             ref[...] = row
-        b1_ref[...] = cut(total_ref[pl.ds(6 + group // 2, 1)], SHARD_COLS)
-        features = relr_ref.shape[1]
-        turned = rel_ref[pl.ds(pl.multiple_of(band * features, features), features)].T
-        for j in range(RELS):
-            relr_ref[j : j + 1] = turned[RELS - 1 - j : RELS - j]
-        relc_ref[...] = turned[LANES : LANES + RELS]
+        b1_ref[...] = jnp.concatenate([total[6 + k : 7 + k] for k in range(4)], axis=1)
+        relr_ref[...] = rel_ref[:, :RELS]
+        relc_ref[...] = rel_ref[:, LANES : LANES + RELS]
         wq_ref[...] = q_ref[:, : 3 * share]
         wp_ref[...] = q_ref[:, 3 * share :]
-        w2_ref[...] = fc2_ref[...].T
         for load in loads:
             load.wait()
 
@@ -1026,8 +1063,8 @@
     per_image = rows // HOME_ROWS
     sds = jax.ShapeDtypeStruct
     tiled = pl.BlockSpec((1, HOME_ROWS, SIDE, D), lambda w, meta: (w // per_image, w % per_image, 0, 0))
-    shapes = [[(1, D // 8)] * 8, (1, FF // 8)] + [(RELS, HEAD // 4)] * 2 + [
-        (SHARD_ROWS, 3 * D // 8), (SHARD_ROWS, D // 8), (SHARD_COLS, SHARD_ROWS),
+    shapes = [[(1, D // 8)] * 8, (1, FF // 8)] + [(HEAD // 4, RELS)] * 2 + [
+        (SHARD_ROWS, 3 * D // 8), (SHARD_ROWS, D // 8),
     ]
     is_shape = lambda shape: isinstance(shape, tuple)
     return pl.pallas_call(
@@ -1046,7 +1083,7 @@
     )(table, *sources)
 
 
-def home_table(plan, offsets, group, band, band_rows):
+def home_table(plan, offsets, band, band_rows):
     own = np.full((4, 2, WINDOWS), 0, np.int32)
     for b in range(4):
         for slot, (m, w) in enumerate(plan[b]):
@@ -1062,8 +1099,7 @@
                 own[b, m, w] = cap + NEAR_CORE + slot
     rows = jnp.asarray(own)[band]
     first = jnp.full((2, 1), band_rows, jnp.int32) * band
-    spot = jnp.broadcast_to(jnp.stack([group, band]).astype(jnp.int32), (2, 2))
-    return jnp.concatenate([rows, offsets.astype(jnp.int32), first, spot, jnp.zeros((2, 2), jnp.int32)], axis=1)
+    return jnp.concatenate([rows, offsets.astype(jnp.int32), first, jnp.zeros((2, 4), jnp.int32)], axis=1)
 
 
 def last_fused_kernel(
@@ -1084,8 +1120,13 @@
 
         streams.append(Halving(source, own, got, sems, order, half))
     rest = rest[14:]
-    small, rel, ln = [SmallSum(*rest[4 * n : 4 * n + 4]) for n in range(3)]
-    back = Homeward(grad_ref, all_ref, rest[12])
+    small_parts, ln_parts = rest[12:14]
+    features = HEAD // 4
+    own_features = pl.ds(pl.multiple_of(lax.axis_index("band") * features, features), features)
+    small = SmallSum(*rest[:4], lambda i: small_parts.at[i])
+    rel = SmallSum(*rest[4:8], lambda i: rest[4].at[own_features])
+    ln = SmallSum(*rest[8:12], lambda i: ln_parts.at[i])
+    back = Homeward(grad_ref, all_ref, rest[14])
 
     def start():
         groups = q_ref.shape[0]
@@ -1104,22 +1145,23 @@
             small.mine[2 + r : 3 + r] = jnp.sum(sums_ref[r], axis=0, keepdims=True)
             small.mine[6 + r : 7 + r] = jnp.sum(fc1_ref[:, D * r : D * r + D], axis=0, keepdims=True)
         small.mine[10:] = jnp.zeros((6, D), F32)
+        small_parts[...] = jnp.zeros_like(small_parts)
+        ln_parts[...] = jnp.zeros_like(ln_parts)
         rel.mine[...] = rel_ref[:64] + pltpu.roll(rel_ref[64:], 192, 1)
         small.send(0)
         rel.send(0)
         ln_acc[...] = jnp.zeros_like(ln_acc)
 
     def middle():
-        small.add(0)
-        rel.add(0)
+        small.add()
+        rel.add()
+        deal(small.mine, small_parts, 6, 4)
         small.send(1)
         rel.send(1)
 
     def finish():
-        small.add(1)
-        rel.add(1)
-        total_ref[...] = small.mine[...]
-        rels_ref[...] = rel.mine[...]
+        total_ref[...] = small.result()
+        rels_ref[...] = rel.result()
 
     timeline(
         w,
@@ -1153,14 +1195,14 @@
         ln.mine[2:] = jnp.zeros((6, D), F32)
         ln.send(0)
         each(streams, "step_done", 3)()
-        ln.add(0)
+        ln.add()
+        deal(ln.mine, ln_parts, 2, 0)
         ln.send(1)
         for n, stream in enumerate(streams):
             shard_ref[half * n : half * n + half] = stream.result()
         back.keep().wait()
         back.finish()
-        ln.add(1)
-        ln_ref[...] = ln.mine[...]
+        ln_ref[...] = ln.result()
 
 
 def last_fused(meta, dqkv, wqkv, x, dmix, gain, dwq, dwp, bias_sums, sums, fc1_sum, rel_acc):
@@ -1168,7 +1210,7 @@
     sds = jax.ShapeDtypeStruct
     half = SHARD_ROWS // 2
     anywhere = pl.BlockSpec(memory_space=pl.ANY)
-    sums_out = [((SHARD_ROWS, SHARD_COLS), F32), ((16, D), F32), ((64, 256), F32), ((8, D), F32)]
+    sums_out = [((SHARD_ROWS, SHARD_COLS), F32), ((16, LANES), F32), ((HEAD // 4, 256), F32), ((8, LANES), F32)]
     return pl.pallas_call(
         last_fused_kernel,
         grid_spec=pltpu.PrefetchScalarGridSpec(
@@ -1183,8 +1225,9 @@
                 pltpu.VMEM((cap, TW, D), BF16), pltpu.VMEM((2, 8, D), F32), pltpu.VMEM((8, D, SHARD_COLS), BF16)
             ]
             + Halving.scratch(half) * 2
-            + SmallSum.scratch((16, D)) + SmallSum.scratch((64, 256)) + SmallSum.scratch((8, D))
-            + [pltpu.SemaphoreType.DMA((5,))],
+            + SmallSum.scratch((16, D), (16, LANES)) + SmallSum.scratch((HEAD, 256), (HEAD // 4, 256))
+            + SmallSum.scratch((8, D), (8, LANES))
+            + [pltpu.VMEM((8, 16, LANES), F32), pltpu.VMEM((8, 8, LANES), F32), pltpu.SemaphoreType.DMA((5,))],
         ),
         out_shape=[sds((cap + NEAR_CORE + NEAR_CROSS, TW, D), BF16)] + [sds(shape, dtype) for shape, dtype in sums_out],
         compiler_params=pltpu.CompilerParams(vmem_limit_bytes=VMEM_LIMIT, collective_id=2, has_side_effects=True),
@@ -1266,31 +1309,30 @@
     part, wide = w_qkv.shape
     close = near(images, bands, band_rows)
     fused = close and groups == 8
-    small = jnp.concatenate(
-        [
-            ln1_gain, ln1_bias, q_bias, v_bias, proj_bias, ln2_gain, ln2_bias, fc2_bias, fc1_bias,
-            rel_rows.reshape(-1), rel_cols.reshape(-1),
-        ]
-    )
+    share = D // groups
+    vector_rows = [ln1_gain, ln1_bias, q_bias, v_bias, proj_bias, ln2_gain, ln2_bias, fc2_bias]
+    small = jnp.concatenate([v[None] for v in vector_rows] + [fc1_bias.reshape(4, share), jnp.zeros((4, share), BF16)])
     block_cols = wide + w_proj.shape[1]
-    small_rows = -(-small.shape[0] // (block_cols * 16)) * 16
-    small = jnp.pad(small, (0, small_rows * block_cols - small.shape[0])).reshape(small_rows, block_cols)
-    block = jnp.concatenate([jnp.concatenate([w_qkv, w_proj], axis=1), small], axis=0)
+    small_rows = 16
     if fused:
+        block, ff_block = pack(w_qkv, w_proj, small, rel_rows.T, rel_cols.T, w_fc1, w_fc2.T)
         first, ext, gext = entry(block, image_tokens, out_grad)
     else:
+        features = rel_rows.shape[1]
+        rest = jnp.zeros((small_rows, block_cols - share - 2 * RELS), BF16)
+        tables = [jnp.pad(rel.T, ((0, small_rows - features), (0, 0))) for rel in (rel_rows, rel_cols)]
+        block = jnp.concatenate(
+            [jnp.concatenate([w_qkv, w_proj], axis=1), jnp.concatenate([small, *tables, rest], axis=1)], axis=0
+        )
+        ff_block = jnp.concatenate([w_fc1, w_fc2.T], axis=1)
         first = lax.all_gather(block, axes, axis=0, tiled=False).reshape(groups, bands, part + small_rows, block_cols)
         ext, gext = extend(image_tokens, band), extend(out_grad, band)
-    ff = lax.all_gather(jnp.concatenate([w_fc1, w_fc2.T], axis=1), axes, axis=0, tiled=False).reshape(
-        groups, bands * part, -1
-    )
-    tail = first[:, :, part:].reshape(groups, bands, small_rows * block_cols)
-    share = D // groups
-    vectors = tail[:, 0, : 8 * share].reshape(groups, 8, share).transpose(1, 0, 2).reshape(8, D).astype(F32)
-    fc1_shift = tail[:, 0, 8 * share : 8 * share + FF // groups].reshape(1, FF).astype(F32)
-    at = 8 * share + FF // groups
-    rels = tail[0, :, at : at + 2 * RELS * (HEAD // bands)].reshape(bands, 2, RELS, HEAD // bands)
-    rels = rels.transpose(1, 2, 0, 3).reshape(2, RELS, HEAD)
+    ff = lax.all_gather(ff_block, axes, axis=0, tiled=False).reshape(groups, bands * part, -1)
+    tail = first[:, :, part:]
+    vectors = tail[:, 0, :8, :share].transpose(1, 0, 2).reshape(8, D).astype(F32)
+    fc1_shift = tail[:, 0, 8:12, :share].reshape(1, FF).astype(F32)
+    features = HEAD // bands
+    rels = [tail[0, :, :features, at : at + RELS].reshape(HEAD, RELS) for at in (share, share + RELS)]
     plan = jnp.asarray(window_plan(images, bands))[band]
     image, window = plan[:, 0], plan[:, 1]
     ext_per = band_rows + 2 * HALO if close else bands * band_rows + 12
@@ -1356,14 +1398,14 @@
         all_grad, q_shard, total, rel_total, ln_total = last_fused(
             meta, d_qkv, wqkv, x, d_mixed, vectors, d_wqkv, d_proj, bias_sums, sums, sum_fc1, rel_acc
         )
-        output, input_grad, shares, b1_share, d_rel_rows, d_rel_cols, g_qkv, g_proj, g_fc2 = home(
-            home_table(window_plan(images, bands), pad_offsets, group, band, band_rows),
-            (out_win, core_out, cross_out, all_grad, total, ln_total, rel_total, q_shard, g_fc2), band_rows,
+        output, input_grad, shares, b1_share, d_rel_rows, d_rel_cols, g_qkv, g_proj = home(
+            home_table(window_plan(images, bands), pad_offsets, band, band_rows),
+            (out_win, core_out, cross_out, all_grad, total, ln_total, rel_total, q_shard), band_rows,
         )
         ln1g, ln1b, qb, vb, pb, ln2g, ln2b, b2 = [share.reshape(-1) for share in shares]
         return (
-            output, input_grad, ln1g, ln1b, g_qkv, qb, vb, d_rel_rows, d_rel_cols, g_proj, pb, ln2g, ln2b, g_fc1,
-            b1_share.reshape(-1), g_fc2, b2,
+            output, input_grad, ln1g, ln1b, g_qkv, qb, vb, d_rel_rows.T, d_rel_cols.T, g_proj, pb, ln2g, ln2b, g_fc1,
+            b1_share.reshape(-1), g_fc2.T, b2,
         )
     else:
         out_ext = scatter(meta, out_win, ext_rows).reshape(images, ext_per, SIDE, D)

time: 482 us -> 451 us (0.936)
  Pallas kernels: 367 us -> 342 us
  local copies, waits for them, and re-layouts: 19.1 us -> 9.59 us
  starting transfers between devices: 3.85 us -> 9.89 us
    pallas_call x1, Pallas kernels: 63.8 us -> 48.9 us  [entry(): pl.pallas_call(entry_kernel, in_specs=[inside, anywhere, anywhere], out_s...]
    pallas_call x1, Pallas kernels: 69.9 us -> 60.5 us  [last_fused(): pl.pallas_call(last_fused_kernel, grid_spec=pltpu.PrefetchScalarGridSpec(...]
    ppermute x1, starting transfers between devices: 0.44 us -> 5.95 us  [shards(): core_out = lax.ppermute(to_core, 'band', CORE)]
    unnamed x29 -> x27, local copies, waits for them, and re-layouts: 6.44 us -> 0.96 us
  transfers between devices with their start and end apart: 5 -> 5, of which waited for: 0 -> 0; matrix products, arithmetic and copies ran while one was open for 14% -> 12% of each run, Pallas kernels for 43% -> 41%
where the time goes in v5:
time: 451 us; the launch traced here: 445 us
  Pallas kernels  342 us (76%)
  matrix products  62.5 us (14%)
  between operations  14.7 us (3%)
  starting transfers between devices  9.89 us (2%)
  local copies, waits for them, and re-layouts  9.59 us (2%)
  other arithmetic  6.58 us (1%)
    pallas_call x1, Pallas kernels, feed_forward(): pl.pallas_call(mlp_kernel, grid=(rows // tile,), in_specs=[tiled(D), tile...  90.6 us
    pallas_call x1, Pallas kernels, attention_backward(): pl.pallas_call(attn_bwd_kernel, grid_spec=pltpu.PrefetchScalarGridSpec(nu...  68.1 us
    dot_general x4, matrix products, weight_grad(): jnp.einsum('td,te->de', flat(left), flat(right), preferred_element_type=F32)  62.5 us
    pallas_call x1, Pallas kernels, last_fused(): pl.pallas_call(last_fused_kernel, grid_spec=pltpu.PrefetchScalarGridSpec(...  60.5 us
    pallas_call x1, Pallas kernels, attention_forward(): pl.pallas_call(fwd_kernel, grid_spec=pltpu.PrefetchScalarGridSpec(num_sca...  58.9 us
    pallas_call x1, Pallas kernels, entry(): pl.pallas_call(entry_kernel, in_specs=[inside, anywhere, anywhere], out_s...  48.9 us
    pallas_call x1, Pallas kernels, home(): pl.pallas_call(home_kernel, grid_spec=pltpu.PrefetchScalarGridSpec(num_sc...  12.7 us
  transfers between devices with their start and end apart: 5, of which 0 were waited for; matrix products, arithmetic and copies ran while one was open for 12% of the time, Pallas kernels for 41%

profile of v5, /device:TPU:0, one launch (start us, length us, event | category | flops | bytes accessed | tf_op | source)
XLA Modules:
  0.0 444.9 jit_solution(2171821226582378221)
XLA Ops:
  7.2 0.8 reshape.122
  8.0 2.0 concatenate.61.small_ref
  10.0 1.9 shard_map.350
  11.9 48.9 %shard_map.351 = (bf16[8,4,208,384]{3,2,1,0:T(8,128)(2,1)}, bf16[2,40,64,768]{3,2,1,0:T(8,128)(2,1)}, bf16[2,40,64,768]{3,2,1,0:T(8,128)(2,1)}) custom-call(bf16[208,384]{1,0:T(8,128)(2,1)} %get-tuple-element.68.block_ref, bf16[2,16,64,768]{3,2,1,0:T(8,128)(2,1)} %x_ref.1, bf16[2,16,64,768]{3,2,1,0:T(8,128)(2,1)} %g_ref.1), custom_call_target="tpu_custom_call" | custom-call | tf_op jit(solution)/shard_map/pallas_call | solution.py:734
  60.8 0.9 fusion.20
  63.7 0.7 convert_bitcast_fusion
  65.1 0.7 slice_convert_fusion
  68.0 0.8 fusion.2.table_ref
  68.8 0.8 fusion.4.table_ref
  70.2 58.9 %shard_map.352 = (bf16[13,224,768]{2,1,0:T(8,128)(2,1)}, bf16[13,224,768]{2,1,0:T(8,128)(2,1)}, bf16[13,224,768]{2,1,0:T(8,128)(2,1)}, bf16[13,224,2304]{2,1,0:T...) custom-call(s32[13,4]{1,0:T(8,128)} %pad_add_fusion.meta_ref, ...), custom_call_target="tpu_custom_call" | custom-call | flops 40000000000 | bytes 80000000 | tf_op jit(solution)/shard_map/pallas_call | solution.py:223
  129.1 90.6 %shard_map.353 = (bf16[2912,768]{1,0:T(8,128)(2,1)}, bf16[2912,768]{1,0:T(8,128)(2,1)}, bf16[2912,3072]{1,0:T(8,128)(2,1)}, bf16[2912,3072]{1,0:T(8,128)(2,1)}, ...) custom-call(bf16[2912,768]{1,0:T(8,128)(2,1)} %bitcast.107, ...), custom_call_target="tpu_custom_call" | custom-call | flops 60000002048 | bytes 80000000 | tf_op jit(solution)/shard_map/pallas_call | solution.py:323
  219.8 21.0 %convolution_convert_fusion.rest_1_ = bf16[768,3072]{1,0:T(8,128)(2,1)} fusion(bf16[2912,768]{1,0:T(8,128)(2,1)} %bitcast.108, bf16[2912,3072]{1,0:T(8,128)(2,1)} %get-tuple-element.80), kind=kOutput, calls=%fused_computation.2 | convolution fusion | flops 13742899200 | bytes 27082752 | tf_op jit(solution)/shard_map/td,te->de/dot_general | solution.py:1369
  241.1 5.9 %collective-permute-start = (bf16[7,224,768]{2,1,0:T(8,128)(2,1)S(1)}, bf16[7,224,768]{2,1,0:T(8,128)(2,1)S(1)}, u32[]{:S(2)}, u32[]{:S(2)}) collective-permute-start(bf16[7,224,768]{2,1,0:T(8,128)(2,1)S(1)} %constant_dynamic-slice_fusion), channel_id=1, source_target_pairs={{0,1},{1,0},{2,3},{3,2},{4,5},{5,4},{6,7},{7,6},{8,9},{9,8},{10,11... | collective-permute-start | bytes 7225352 | tf_op jit(solution)/shard_map/ppermute | solution.py:1374
  247.0 0.8 collective-permute-start.1
  247.9 5.1 %convolution_convert_fusion.2.dwp_ref = bf16[768,768]{1,0:T(8,128)(2,1)} fusion(bf16[2912,768]{1,0:T(8,128)(2,1)S(1)} %bitcast.105, bf16[2912,768]{1,0:T(8,128)(2,1)S(1)} %bitcast.101), kind=kOutput, calls=%fused_computation.4 | convolution fusion | flops 3435724800 | bytes 10125312 | tf_op jit(solution)/shard_map/td,te->de/dot_general | solution.py:1369
  252.9 19.8 %convolution_convert_fusion.1.rest_0_ = bf16[768,3072]{1,0:T(8,128)(2,1)} fusion(bf16[2912,768]{1,0:T(8,128)(2,1)S(1)} %bitcast.110, bf16[2912,3072]{1,0:T(8,128)(2,1)} %get-tuple-element.79), kind=kOutput, calls=%fused_computation.3 | convolution fusion | flops 13742899200 | bytes 27082752 | tf_op jit(solution)/shard_map/td,te->de/dot_general | solution.py:1369
  272.8 68.1 %shard_map.354 = (bf16[13,224,2304]{2,1,0:T(8,128)(2,1)}, f32[128,256]{1,0:T(8,128)}, f32[2,8,768]{2,1,0:T(8,128)}, bf16[2,2,2,96,384]{4,3,2,1,0:T(8,128)(2,1)}, f32[192,384]{1,0:T(8,128)}) custom-call(s32[13,4]{1,0:T(8,128)} %pad_add_fusion.meta_ref, bf16[13,224,2304]{2,1,0:T(8,128)(2,1)} %get-tuple-element.83.qkv_ref, ...), custom_call_target="tpu_custom_call" | custom-call | flops 60000002048 | bytes 80000000 | tf_op jit(solution)/shard_map/pallas_call | solution.py:844
  340.9 1.0 dynamic-slice_bitcast_fusion
  342.1 16.6 %bitcast_convert_fusion.dwq_ref = bf16[768,2304]{1,0:T(8,128)(2,1)} fusion(bf16[13,224,768]{2,1,0:T(8,128)(2,1)} %get-tuple-element.92, bf16[13,224,2304]{2,1,0:T(8,128)(2,1)} %get-tuple-element.89.dqkv_ref), kind=kOutput, calls=%fused_computation.1 | convolution fusion | flops 10307174400 | bytes 21430272 | tf_op jit(solution)/shard_map/td,te->de/dot_general | solution.py:1369
  358.8 3.0 collective-permute-start.3
  361.9 60.5 %shard_map.355 = (bf16[25,224,768]{2,1,0:T(8,128)(2,1)}, f32[192,384]{1,0:T(8,128)}, f32[16,128]{1,0:T(8,128)}, f32[16,256]{1,0:T(8,128)}, f32[8,128]{1,0:T(8,128)}) custom-call(s32[13,4]{1,0:T(8,128)} %pad_add_fusion.meta_ref, bf16[13,224,2304]{2,1,0:T(8,128)(2,1)} %get-tuple-element.89.dqkv_ref, bf16[768,2304]{1,0:T(8,128)(2,1)} %get-tuple-element.90.wqkv_ref, ...), custom_call_target="tpu_custom_call" | custom-call | flops 20000000000 | bytes 50000000 | tf_op jit(solution)/shard_map/pallas_call | solution.py:1214
  422.4 12.7 %shard_map.356 = (bf16[2,16,64,768]{3,2,1,0:T(8,128)(2,1)}, f32[2,16,64,768]{3,2,1,0:T(8,128)}, f32[1,96]{1,0:T(1,128)}, f32[1,96]{1,0:T(1,128)}, f32[1,96]{1,0:...) custom-call(s32[2,32]{1,0:T(2,128)} %add_add_fusion.table_ref, ...), custom_call_target="tpu_custom_call" | custom-call | flops 500000000 | bytes 20000000 | tf_op jit(solution)/shard_map/pallas_call | solution.py:1070
  435.1 1.3 reduce.1
  436.4 0.7 convert_add_fusion.1
  (66 shorter events, 6.8 us)
Async XLA Ops:
  7.2 55.8 %copy-start.1 = (s32[2,2]{1,0:T(2,128)S(1)}, s32[2,2]{1,0:T(2,128)}, u32[]{:S(2)}) copy-start(s32[2,2]{1,0:T(2,128)} %param.24) | copy-start | bytes 52
  7.2 121.9 %all-gather.3.cloned.1.call-start = ((), (), s32[]{:S(2)}) async-start(), calls=%async_computation | async-start | bytes 9732096 | tf_op jit(solution)/shard_map/all_gather | solution.py:1330
  219.7 28.1 %slice-start = ((s8[4472832]{0:T(1024)(128)(4,1)}), s8[4194304]{0:T(1024)(128)(4,1)S(1)}, s32[]{:S(2)}) async-start(s8[4472832]{0:T(1024)(128)(4,1)} %bitcast.100), calls=%async_computation.1 | async-start | bytes 8388608
  219.7 28.1 %slice-start.2 = ((s8[4472832]{0:T(1024)(128)(4,1)}), s8[4194304]{0:T(1024)(128)(4,1)S(1)}, s32[]{:S(2)}) async-start(s8[4472832]{0:T(1024)(128)(4,1)} %bitcast.103), calls=%async_computation.3 | async-start | bytes 8388608
  219.7 21.1 %copy-start = (bf16[2912,768]{1,0:T(8,128)(2,1)S(1)}, bf16[2912,768]{1,0:T(8,128)(2,1)}, u32[]{:S(2)}) copy-start(bf16[2912,768]{1,0:T(8,128)(2,1)} %get-tuple-element.77) | copy-start | bytes 13418500
  219.7 28.1 %slice-start.1 = ((s8[4472832]{0:T(1024)(128)(4,1)}), s8[278528]{0:T(1024)(128)(4,1)S(1)}, s32[]{:S(2)}) async-start(s8[4472832]{0:T(1024)(128)(4,1)} %bitcast.100), calls=%async_computation.2 | async-start | bytes 557056
  219.7 28.1 %slice-start.3 = ((s8[4472832]{0:T(1024)(128)(4,1)}), s8[278528]{0:T(1024)(128)(4,1)S(1)}, s32[]{:S(2)}) async-start(s8[4472832]{0:T(1024)(128)(4,1)} %bitcast.103), calls=%async_computation.4 | async-start | bytes 557056
  240.9 12.0 %slice-start.4 = ((s8[4472832]{0:T(1024)(128)(4,1)}), s8[278528]{0:T(1024)(128)(4,1)S(1)}, s32[]{:S(2)}) async-start(s8[4472832]{0:T(1024)(128)(4,1)} %bitcast.109), calls=%async_computation.5 | async-start | bytes 557056
  241.1 31.7 %collective-permute-start = (bf16[7,224,768]{2,1,0:T(8,128)(2,1)S(1)}, bf16[7,224,768]{2,1,0:T(8,128)(2,1)S(1)}, u32[]{:S(2)}, u32[]{:S(2)}) collective-permute-start(bf16[7,224,768]{2,1,0:T(8,128)(2,1)S(1)} %constant_dynamic-slice_fusion), channel_id=1, source_target_pairs={{0,1},{1,0},{2,3},{3,2},{4,5},{5,4},{6,7},{7,6},{8,9},{9,8},{10,11... | collective-permute-start | bytes 7225352 | tf_op jit(solution)/shard_map/ppermute | solution.py:1374
  247.0 25.7 %collective-permute-start.1 = (bf16[5,224,768]{2,1,0:T(8,128)(2,1)S(1)}, bf16[5,224,768]{2,1,0:T(8,128)(2,1)S(1)}, u32[]{:S(2)}, u32[]{:S(2)}) collective-permute-start(bf16[5,224,768]{2,1,0:T(8,128)(2,1)S(1)} %bitcast.67), channel_id=1, source_target_pairs={{1,2},{2,1},{5,6},{6,5},{9,10},{10,9},{13,14},{14,13},{17,18},{18,... | collective-permute-start | bytes 5160968 | tf_op jit(solution)/shard_map/ppermute | solution.py:1375
  247.8 5.1 %slice-start.5 = ((s8[4472832]{0:T(1024)(128)(4,1)}), s8[4194304]{0:T(1024)(128)(4,1)S(1)}, s32[]{:S(2)}) async-start(s8[4472832]{0:T(1024)(128)(4,1)} %bitcast.109), calls=%async_computation.6 | async-start | bytes 8388608
  272.8 68.2 %copy-start.3 = (bf16[5,224,768]{2,1,0:T(8,128)(2,1)}, bf16[5,224,768]{2,1,0:T(8,128)(2,1)S(1)}, u32[]{:S(2)}) copy-start(bf16[5,224,768]{2,1,0:T(8,128)(2,1)S(1)} %collective-permute-done.1.cross_ref) | copy-start | bytes 5160964
  272.8 68.2 %copy-start.2 = (bf16[7,224,768]{2,1,0:T(8,128)(2,1)}, bf16[7,224,768]{2,1,0:T(8,128)(2,1)S(1)}, u32[]{:S(2)}) copy-start(bf16[7,224,768]{2,1,0:T(8,128)(2,1)S(1)} %collective-permute-done.core_ref) | copy-start | bytes 7225348
  341.9 16.8 %collective-permute-start.2 = (bf16[2,2,96,384]{3,2,1,0:T(8,128)(2,1)S(1)}, bf16[2,2,96,384]{3,2,1,0:T(8,128)(2,1)S(1)}, u32[]{:S(2)}, u32[]{:S(2)}) collective-permute-start(bf16[2,2,96,384]{3,2,1,0:T(8,128)(2,1)S(1)} %dynamic-slice_bitcast_fusion), channel_id=1, source_target_pairs={{0,16},{4,20},{8,24},{12,28},{16,0},{20,4},{24,8},{28,12},{1,17},{... | collective-permute-start | bytes 884744 | tf_op jit(solution)/shard_map/ppermute | solution.py:1393
  342.1 16.6 %copy-start.4 = (bf16[2,2,2,96,384]{4,3,2,1,0:T(8,128)(2,1)S(1)}, bf16[2,2,2,96,384]{4,3,2,1,0:T(8,128)(2,1)}, u32[]{:S(2)}) copy-start(bf16[2,2,2,96,384]{4,3,2,1,0:T(8,128)(2,1)} %get-tuple-element.115) | copy-start | bytes 1769476
  358.8 77.5 %collective-permute-start.3 = (bf16[2,96,384]{2,1,0:T(8,128)(2,1)S(1)}, bf16[2,96,384]{2,1,0:T(8,128)(2,1)S(1)}, u32[]{:S(2)}, u32[]{:S(2)}) collective-permute-start(bf16[2,96,384]{2,1,0:T(8,128)(2,1)S(1)} %dynamic-slice_bitcast_fusion.1), channel_id=1, source_target_pairs={{0,8},{4,12},{8,0},{12,4},{16,24},{20,28},{24,16},{28,20},{1,9},{5... | collective-permute-start | bytes 442376 | tf_op jit(solution)/shard_map/ppermute | solution.py:1393
  422.4 14.7 %copy-start.5 = (f32[192,384]{1,0:T(8,128)S(1)}, f32[192,384]{1,0:T(8,128)}, u32[]{:S(2)}) copy-start(f32[192,384]{1,0:T(8,128)} %get-tuple-element.117) | copy-start | bytes 884740
Sparse Core Ops, SparseCore 0:
  12.1 94.2 all-gather.2

commit v6 on v5

--- a/solution.py
+++ b/solution.py
@@ -405,7 +405,7 @@
 
         def add(i, _):
             spot = (i // 8, i // 4 % 2, i // 2 % 2, i % 2)
-            self.own[spot] = (self.own[spot].astype(F32) + self.got[0][spot].astype(F32)).astype(BF16)
+            self.own[spot] = self.own[spot] + self.got[0][spot]
             return 0
 
         lax.fori_loop(0, 16, add, 0)
@@ -442,7 +442,7 @@
         def add(i, _):
             bits = {axis: (i // 2 ** (len(free) - 1 - j)) % 2 for j, axis in enumerate(free)}
             spot = tuple(bits[axis] if axis in bits else self.at[axis] for axis in self.AXES)
-            self.own[spot] = (self.own[spot].astype(F32) + self.got[k + 1][tuple(bits[axis] for axis in free)].astype(F32)).astype(BF16)
+            self.own[spot] = self.own[spot] + self.got[k + 1][tuple(bits[axis] for axis in free)]
             return 0
 
         if k < 3:
@@ -793,15 +793,19 @@
         q_t = q.astype(F32).T.astype(BF16)
         zero = jnp.zeros_like(v)
         dqx, dv_t, dk_t = [], [], []
+        dps, dss = [], []
+        for h in range(2):
+            mine = low_half if h == 0 else ~low_half
+            dps.append(mm_nt(da_low, jnp.where(mine, v, zero)))
         for h in range(2):
             mine = low_half if h == 0 else ~low_half
             centre = jnp.sum(jnp.where(mine, prod, 0.0), axis=-1, keepdims=True)
-            dp = mm_nt(da_low, jnp.where(mine, v, zero))
             e = p_ref[2 * p + h]
-            ds = (e.astype(F32) * (dp - centre)).astype(BF16)
-            dqx.append(mm(ds, keys))
-            dv_t.append(mm(da_t[64 * h : 64 * h + 64], e))
-            dk_t.append(mm(q_t[64 * h : 64 * h + 64], ds))
+            dss.append((e.astype(F32) * (dps[h] - centre)).astype(BF16))
+        for h in range(2):
+            dqx.append(mm(dss[h], keys))
+            dv_t.append(mm(da_t[64 * h : 64 * h + 64], p_ref[2 * p + h]))
+            dk_t.append(mm(q_t[64 * h : 64 * h + 64], dss[h]))
         dq = jnp.where(low_half, dqx[0][:, :LANES], dqx[1][:, :LANES])
         drc = jnp.where(low_half, dqx[0][:, LANES:], dqx[1][:, LANES:])
         part = lane & 63

time: 451 us -> 445 us (0.987)
  Pallas kernels: 342 us -> 336 us
    pallas_call x1, Pallas kernels: 68.1 us -> 62.7 us  [attention_backward(): pl.pallas_call(attn_bwd_kernel, grid_spec=pltpu.PrefetchScalarGridSpec(nu...]
where the time goes in v6:
time: 445 us; the launch traced here: 439 us
  Pallas kernels  336 us (76%)
  matrix products  62.5 us (14%)
  between operations  14.9 us (3%)
  starting transfers between devices  9.84 us (2%)
  local copies, waits for them, and re-layouts  9.59 us (2%)
  other arithmetic  6.58 us (1%)
    pallas_call x1, Pallas kernels, feed_forward(): pl.pallas_call(mlp_kernel, grid=(rows // tile,), in_specs=[tiled(D), tile...  90.3 us
    pallas_call x1, Pallas kernels, attention_backward(): pl.pallas_call(attn_bwd_kernel, grid_spec=pltpu.PrefetchScalarGridSpec(nu...  62.7 us
    dot_general x4, matrix products, weight_grad(): jnp.einsum('td,te->de', flat(left), flat(right), preferred_element_type=F32)  62.5 us
    pallas_call x1, Pallas kernels, last_fused(): pl.pallas_call(last_fused_kernel, grid_spec=pltpu.PrefetchScalarGridSpec(...  60.5 us
    pallas_call x1, Pallas kernels, attention_forward(): pl.pallas_call(fwd_kernel, grid_spec=pltpu.PrefetchScalarGridSpec(num_sca...  58.9 us
    pallas_call x1, Pallas kernels, entry(): pl.pallas_call(entry_kernel, in_specs=[inside, anywhere, anywhere], out_s...  48.9 us
    pallas_call x1, Pallas kernels, home(): pl.pallas_call(home_kernel, grid_spec=pltpu.PrefetchScalarGridSpec(num_sc...  12.7 us
  transfers between devices with their start and end apart: 5, of which 0 were waited for; matrix products, arithmetic and copies ran while one was open for 12% of the time, Pallas kernels for 41%

profile of v6, /device:TPU:0, one launch (start us, length us, event | category | flops | bytes accessed | tf_op | source)
XLA Modules:
  0.0 439.3 jit_solution(17238297043069813251)
XLA Ops:
  7.2 0.8 reshape.122
  8.0 2.0 concatenate.61.small_ref
  10.0 1.9 shard_map.350
  11.9 48.9 %shard_map.351 = (bf16[8,4,208,384]{3,2,1,0:T(8,128)(2,1)}, bf16[2,40,64,768]{3,2,1,0:T(8,128)(2,1)}, bf16[2,40,64,768]{3,2,1,0:T(8,128)(2,1)}) custom-call(bf16[208,384]{1,0:T(8,128)(2,1)} %get-tuple-element.68.block_ref, bf16[2,16,64,768]{3,2,1,0:T(8,128)(2,1)} %x_ref.1, bf16[2,16,64,768]{3,2,1,0:T(8,128)(2,1)} %g_ref.1), custom_call_target="tpu_custom_call" | custom-call | tf_op jit(solution)/shard_map/pallas_call | solution.py:734
  60.8 0.9 fusion.20
  63.7 0.7 convert_bitcast_fusion
  65.1 0.7 slice_convert_fusion
  68.0 0.8 fusion.2.table_ref
  68.8 0.8 fusion.4.table_ref
  70.2 58.9 %shard_map.352 = (bf16[13,224,768]{2,1,0:T(8,128)(2,1)}, bf16[13,224,768]{2,1,0:T(8,128)(2,1)}, bf16[13,224,768]{2,1,0:T(8,128)(2,1)}, bf16[13,224,2304]{2,1,0:T...) custom-call(s32[13,4]{1,0:T(8,128)} %pad_add_fusion.meta_ref, ...), custom_call_target="tpu_custom_call" | custom-call | flops 40000000000 | bytes 80000000 | tf_op jit(solution)/shard_map/pallas_call | solution.py:223
  129.1 90.3 %shard_map.353 = (bf16[2912,768]{1,0:T(8,128)(2,1)}, bf16[2912,768]{1,0:T(8,128)(2,1)}, bf16[2912,3072]{1,0:T(8,128)(2,1)}, bf16[2912,3072]{1,0:T(8,128)(2,1)}, ...) custom-call(bf16[2912,768]{1,0:T(8,128)(2,1)} %bitcast.107, ...), custom_call_target="tpu_custom_call" | custom-call | flops 60000002048 | bytes 80000000 | tf_op jit(solution)/shard_map/pallas_call | solution.py:323
  219.4 21.1 %convolution_convert_fusion.rest_1_ = bf16[768,3072]{1,0:T(8,128)(2,1)} fusion(bf16[2912,768]{1,0:T(8,128)(2,1)} %bitcast.108, bf16[2912,3072]{1,0:T(8,128)(2,1)} %get-tuple-element.80), kind=kOutput, calls=%fused_computation.2 | convolution fusion | flops 13742899200 | bytes 27082752 | tf_op jit(solution)/shard_map/td,te->de/dot_general | solution.py:1373
  240.8 5.9 %collective-permute-start = (bf16[7,224,768]{2,1,0:T(8,128)(2,1)S(1)}, bf16[7,224,768]{2,1,0:T(8,128)(2,1)S(1)}, u32[]{:S(2)}, u32[]{:S(2)}) collective-permute-start(bf16[7,224,768]{2,1,0:T(8,128)(2,1)S(1)} %constant_dynamic-slice_fusion), channel_id=1, source_target_pairs={{0,1},{1,0},{2,3},{3,2},{4,5},{5,4},{6,7},{7,6},{8,9},{9,8},{10,11... | collective-permute-start | bytes 7225352 | tf_op jit(solution)/shard_map/ppermute | solution.py:1378
  246.7 0.8 collective-permute-start.1
  247.6 5.1 %convolution_convert_fusion.2.dwp_ref = bf16[768,768]{1,0:T(8,128)(2,1)} fusion(bf16[2912,768]{1,0:T(8,128)(2,1)S(1)} %bitcast.105, bf16[2912,768]{1,0:T(8,128)(2,1)S(1)} %bitcast.101), kind=kOutput, calls=%fused_computation.4 | convolution fusion | flops 3435724800 | bytes 10125312 | tf_op jit(solution)/shard_map/td,te->de/dot_general | solution.py:1373
  252.6 19.9 %convolution_convert_fusion.1.rest_0_ = bf16[768,3072]{1,0:T(8,128)(2,1)} fusion(bf16[2912,768]{1,0:T(8,128)(2,1)S(1)} %bitcast.110, bf16[2912,3072]{1,0:T(8,128)(2,1)} %get-tuple-element.79), kind=kOutput, calls=%fused_computation.3 | convolution fusion | flops 13742899200 | bytes 27082752 | tf_op jit(solution)/shard_map/td,te->de/dot_general | solution.py:1373
  272.5 62.7 %shard_map.354 = (bf16[13,224,2304]{2,1,0:T(8,128)(2,1)}, f32[128,256]{1,0:T(8,128)}, f32[2,8,768]{2,1,0:T(8,128)}, bf16[2,2,2,96,384]{4,3,2,1,0:T(8,128)(2,1)}, f32[192,384]{1,0:T(8,128)}) custom-call(s32[13,4]{1,0:T(8,128)} %pad_add_fusion.meta_ref, bf16[13,224,2304]{2,1,0:T(8,128)(2,1)} %get-tuple-element.83.qkv_ref, ...), custom_call_target="tpu_custom_call" | custom-call | flops 60000002048 | bytes 80000000 | tf_op jit(solution)/shard_map/pallas_call | solution.py:848
  335.3 1.0 dynamic-slice_bitcast_fusion
  336.4 16.4 %bitcast_convert_fusion.dwq_ref = bf16[768,2304]{1,0:T(8,128)(2,1)} fusion(bf16[13,224,768]{2,1,0:T(8,128)(2,1)} %get-tuple-element.92, bf16[13,224,2304]{2,1,0:T(8,128)(2,1)} %get-tuple-element.89.dqkv_ref), kind=kOutput, calls=%fused_computation.1 | convolution fusion | flops 10307174400 | bytes 21430272 | tf_op jit(solution)/shard_map/td,te->de/dot_general | solution.py:1373
  353.0 3.0 collective-permute-start.3
  356.0 60.5 %shard_map.355 = (bf16[25,224,768]{2,1,0:T(8,128)(2,1)}, f32[192,384]{1,0:T(8,128)}, f32[16,128]{1,0:T(8,128)}, f32[16,256]{1,0:T(8,128)}, f32[8,128]{1,0:T(8,128)}) custom-call(s32[13,4]{1,0:T(8,128)} %pad_add_fusion.meta_ref, bf16[13,224,2304]{2,1,0:T(8,128)(2,1)} %get-tuple-element.89.dqkv_ref, bf16[768,2304]{1,0:T(8,128)(2,1)} %get-tuple-element.90.wqkv_ref, ...), custom_call_target="tpu_custom_call" | custom-call | flops 20000000000 | bytes 50000000 | tf_op jit(solution)/shard_map/pallas_call | solution.py:1218
  416.5 12.7 %shard_map.356 = (bf16[2,16,64,768]{3,2,1,0:T(8,128)(2,1)}, f32[2,16,64,768]{3,2,1,0:T(8,128)}, f32[1,96]{1,0:T(1,128)}, f32[1,96]{1,0:T(1,128)}, f32[1,96]{1,0:...) custom-call(s32[2,32]{1,0:T(2,128)} %add_add_fusion.table_ref, ...), custom_call_target="tpu_custom_call" | custom-call | flops 500000000 | bytes 20000000 | tf_op jit(solution)/shard_map/pallas_call | solution.py:1074
  429.2 1.3 reduce.1
  430.5 0.7 convert_add_fusion.1
  (66 shorter events, 6.7 us)
Async XLA Ops:
  7.2 55.8 %copy-start.1 = (s32[2,2]{1,0:T(2,128)S(1)}, s32[2,2]{1,0:T(2,128)}, u32[]{:S(2)}) copy-start(s32[2,2]{1,0:T(2,128)} %param.24) | copy-start | bytes 52
  7.2 121.9 %all-gather.3.cloned.1.call-start = ((), (), s32[]{:S(2)}) async-start(), calls=%async_computation | async-start | bytes 9732096 | tf_op jit(solution)/shard_map/all_gather | solution.py:1334
  219.4 28.1 %slice-start = ((s8[4472832]{0:T(1024)(128)(4,1)}), s8[4194304]{0:T(1024)(128)(4,1)S(1)}, s32[]{:S(2)}) async-start(s8[4472832]{0:T(1024)(128)(4,1)} %bitcast.100), calls=%async_computation.1 | async-start | bytes 8388608
  219.4 28.1 %slice-start.2 = ((s8[4472832]{0:T(1024)(128)(4,1)}), s8[4194304]{0:T(1024)(128)(4,1)S(1)}, s32[]{:S(2)}) async-start(s8[4472832]{0:T(1024)(128)(4,1)} %bitcast.103), calls=%async_computation.3 | async-start | bytes 8388608
  219.4 21.1 %copy-start = (bf16[2912,768]{1,0:T(8,128)(2,1)S(1)}, bf16[2912,768]{1,0:T(8,128)(2,1)}, u32[]{:S(2)}) copy-start(bf16[2912,768]{1,0:T(8,128)(2,1)} %get-tuple-element.77) | copy-start | bytes 13418500
  219.4 28.1 %slice-start.1 = ((s8[4472832]{0:T(1024)(128)(4,1)}), s8[278528]{0:T(1024)(128)(4,1)S(1)}, s32[]{:S(2)}) async-start(s8[4472832]{0:T(1024)(128)(4,1)} %bitcast.100), calls=%async_computation.2 | async-start | bytes 557056
  219.4 28.1 %slice-start.3 = ((s8[4472832]{0:T(1024)(128)(4,1)}), s8[278528]{0:T(1024)(128)(4,1)S(1)}, s32[]{:S(2)}) async-start(s8[4472832]{0:T(1024)(128)(4,1)} %bitcast.103), calls=%async_computation.4 | async-start | bytes 557056
  240.6 12.0 %slice-start.4 = ((s8[4472832]{0:T(1024)(128)(4,1)}), s8[278528]{0:T(1024)(128)(4,1)S(1)}, s32[]{:S(2)}) async-start(s8[4472832]{0:T(1024)(128)(4,1)} %bitcast.109), calls=%async_computation.5 | async-start | bytes 557056
  240.8 31.7 %collective-permute-start = (bf16[7,224,768]{2,1,0:T(8,128)(2,1)S(1)}, bf16[7,224,768]{2,1,0:T(8,128)(2,1)S(1)}, u32[]{:S(2)}, u32[]{:S(2)}) collective-permute-start(bf16[7,224,768]{2,1,0:T(8,128)(2,1)S(1)} %constant_dynamic-slice_fusion), channel_id=1, source_target_pairs={{0,1},{1,0},{2,3},{3,2},{4,5},{5,4},{6,7},{7,6},{8,9},{9,8},{10,11... | collective-permute-start | bytes 7225352 | tf_op jit(solution)/shard_map/ppermute | solution.py:1378
  246.7 25.8 %collective-permute-start.1 = (bf16[5,224,768]{2,1,0:T(8,128)(2,1)S(1)}, bf16[5,224,768]{2,1,0:T(8,128)(2,1)S(1)}, u32[]{:S(2)}, u32[]{:S(2)}) collective-permute-start(bf16[5,224,768]{2,1,0:T(8,128)(2,1)S(1)} %bitcast.67), channel_id=1, source_target_pairs={{1,2},{2,1},{5,6},{6,5},{9,10},{10,9},{13,14},{14,13},{17,18},{18,... | collective-permute-start | bytes 5160968 | tf_op jit(solution)/shard_map/ppermute | solution.py:1379
  247.6 5.1 %slice-start.5 = ((s8[4472832]{0:T(1024)(128)(4,1)}), s8[4194304]{0:T(1024)(128)(4,1)S(1)}, s32[]{:S(2)}) async-start(s8[4472832]{0:T(1024)(128)(4,1)} %bitcast.109), calls=%async_computation.6 | async-start | bytes 8388608
  272.5 62.7 %copy-start.3 = (bf16[5,224,768]{2,1,0:T(8,128)(2,1)}, bf16[5,224,768]{2,1,0:T(8,128)(2,1)S(1)}, u32[]{:S(2)}) copy-start(bf16[5,224,768]{2,1,0:T(8,128)(2,1)S(1)} %collective-permute-done.1.cross_ref) | copy-start | bytes 5160964
  272.5 62.8 %copy-start.2 = (bf16[7,224,768]{2,1,0:T(8,128)(2,1)}, bf16[7,224,768]{2,1,0:T(8,128)(2,1)S(1)}, u32[]{:S(2)}) copy-start(bf16[7,224,768]{2,1,0:T(8,128)(2,1)S(1)} %collective-permute-done.core_ref) | copy-start | bytes 7225348
  336.3 16.5 %collective-permute-start.2 = (bf16[2,2,96,384]{3,2,1,0:T(8,128)(2,1)S(1)}, bf16[2,2,96,384]{3,2,1,0:T(8,128)(2,1)S(1)}, u32[]{:S(2)}, u32[]{:S(2)}) collective-permute-start(bf16[2,2,96,384]{3,2,1,0:T(8,128)(2,1)S(1)} %dynamic-slice_bitcast_fusion), channel_id=1, source_target_pairs={{0,16},{4,20},{8,24},{12,28},{16,0},{20,4},{24,8},{28,12},{1,17},{... | collective-permute-start | bytes 884744 | tf_op jit(solution)/shard_map/ppermute | solution.py:1397
  336.4 16.5 %copy-start.4 = (bf16[2,2,2,96,384]{4,3,2,1,0:T(8,128)(2,1)S(1)}, bf16[2,2,2,96,384]{4,3,2,1,0:T(8,128)(2,1)}, u32[]{:S(2)}) copy-start(bf16[2,2,2,96,384]{4,3,2,1,0:T(8,128)(2,1)} %get-tuple-element.115) | copy-start | bytes 1769476
  353.0 77.5 %collective-permute-start.3 = (bf16[2,96,384]{2,1,0:T(8,128)(2,1)S(1)}, bf16[2,96,384]{2,1,0:T(8,128)(2,1)S(1)}, u32[]{:S(2)}, u32[]{:S(2)}) collective-permute-start(bf16[2,96,384]{2,1,0:T(8,128)(2,1)S(1)} %dynamic-slice_bitcast_fusion.1), channel_id=1, source_target_pairs={{0,8},{4,12},{8,0},{12,4},{16,24},{20,28},{24,16},{28,20},{1,9},{5... | collective-permute-start | bytes 442376 | tf_op jit(solution)/shard_map/ppermute | solution.py:1397
  416.5 14.7 %copy-start.5 = (f32[192,384]{1,0:T(8,128)S(1)}, f32[192,384]{1,0:T(8,128)}, u32[]{:S(2)}) copy-start(f32[192,384]{1,0:T(8,128)} %get-tuple-element.117) | copy-start | bytes 884740
Sparse Core Ops, SparseCore 0:
  12.1 94.2 all-gather.2

commit v7 on v6

--- a/solution.py
+++ b/solution.py
@@ -768,7 +768,7 @@
                 2: [each(ones, "first_done"), each(ones, "step", 0), each(twos, "first_done")],
                 5: [each(ones, "step_done", 0), each(ones, "step", 1), each(twos, "step", 0)],
                 7: [each(ones, "step_done", 1), each(ones, "step", 2)],
-                10: [each(twos, "step_done", 0), each(twos, "step", 1), each(ones, "step_done", 2), each(ones, "step", 3)],
+                11: [each(twos, "step_done", 0), each(twos, "step", 1), each(ones, "step_done", 2), each(ones, "step", 3)],
             },
         )
 

time: 445 us -> 443 us (level)
  transfers between devices with their start and end apart: 5 -> 5, of which waited for: 0 -> 0; matrix products, arithmetic and copies ran while one was open for 12% -> 12% of each run, Pallas kernels for 41% -> 42%
where the time goes in v7:
time: 443 us; the launch traced here: 437 us
  Pallas kernels  334 us (75%)
  matrix products  62.4 us (14%)
  between operations  14.9 us (3%)
  local copies, waits for them, and re-layouts  9.59 us (2%)
  starting transfers between devices  9.46 us (2%)
  other arithmetic  6.58 us (1%)
    pallas_call x1, Pallas kernels, feed_forward(): pl.pallas_call(mlp_kernel, grid=(rows // tile,), in_specs=[tiled(D), tile...  90.3 us
    dot_general x4, matrix products, weight_grad(): jnp.einsum('td,te->de', flat(left), flat(right), preferred_element_type=F32)  62.4 us
    pallas_call x1, Pallas kernels, last_fused(): pl.pallas_call(last_fused_kernel, grid_spec=pltpu.PrefetchScalarGridSpec(...  61.1 us
    pallas_call x1, Pallas kernels, attention_backward(): pl.pallas_call(attn_bwd_kernel, grid_spec=pltpu.PrefetchScalarGridSpec(nu...  60.4 us
    pallas_call x1, Pallas kernels, attention_forward(): pl.pallas_call(fwd_kernel, grid_spec=pltpu.PrefetchScalarGridSpec(num_sca...  58.9 us
    pallas_call x1, Pallas kernels, entry(): pl.pallas_call(entry_kernel, in_specs=[inside, anywhere, anywhere], out_s...  48.9 us
    pallas_call x1, Pallas kernels, home(): pl.pallas_call(home_kernel, grid_spec=pltpu.PrefetchScalarGridSpec(num_sc...  12.7 us
  transfers between devices with their start and end apart: 5, of which 0 were waited for; matrix products, arithmetic and copies ran while one was open for 12% of the time, Pallas kernels for 42%

profile of v7, /device:TPU:0, one launch (start us, length us, event | category | flops | bytes accessed | tf_op | source)
XLA Modules:
  0.0 437.1 jit_solution(15796944945017819540)
XLA Ops:
  7.2 0.8 reshape.122
  8.0 2.0 concatenate.61.small_ref
  10.0 1.9 shard_map.350
  11.9 48.9 %shard_map.351 = (bf16[8,4,208,384]{3,2,1,0:T(8,128)(2,1)}, bf16[2,40,64,768]{3,2,1,0:T(8,128)(2,1)}, bf16[2,40,64,768]{3,2,1,0:T(8,128)(2,1)}) custom-call(bf16[208,384]{1,0:T(8,128)(2,1)} %get-tuple-element.68.block_ref, bf16[2,16,64,768]{3,2,1,0:T(8,128)(2,1)} %x_ref.1, bf16[2,16,64,768]{3,2,1,0:T(8,128)(2,1)} %g_ref.1), custom_call_target="tpu_custom_call" | custom-call | tf_op jit(solution)/shard_map/pallas_call | solution.py:734
  60.8 0.9 fusion.20
  63.7 0.7 convert_bitcast_fusion
  68.0 0.8 fusion.2.table_ref
  68.8 0.8 fusion.4.table_ref
  70.2 58.9 %shard_map.352 = (bf16[13,224,768]{2,1,0:T(8,128)(2,1)}, bf16[13,224,768]{2,1,0:T(8,128)(2,1)}, bf16[13,224,768]{2,1,0:T(8,128)(2,1)}, bf16[13,224,2304]{2,1,0:T...) custom-call(s32[13,4]{1,0:T(8,128)} %pad_add_fusion.meta_ref, ...), custom_call_target="tpu_custom_call" | custom-call | flops 40000000000 | bytes 80000000 | tf_op jit(solution)/shard_map/pallas_call | solution.py:223
  129.1 90.3 %shard_map.353 = (bf16[2912,768]{1,0:T(8,128)(2,1)}, bf16[2912,768]{1,0:T(8,128)(2,1)}, bf16[2912,3072]{1,0:T(8,128)(2,1)}, bf16[2912,3072]{1,0:T(8,128)(2,1)}, ...) custom-call(bf16[2912,768]{1,0:T(8,128)(2,1)} %bitcast.107, ...), custom_call_target="tpu_custom_call" | custom-call | flops 60000002048 | bytes 80000000 | tf_op jit(solution)/shard_map/pallas_call | solution.py:323
  219.4 21.1 %convolution_convert_fusion.rest_1_ = bf16[768,3072]{1,0:T(8,128)(2,1)} fusion(bf16[2912,768]{1,0:T(8,128)(2,1)} %bitcast.108, bf16[2912,3072]{1,0:T(8,128)(2,1)} %get-tuple-element.80), kind=kOutput, calls=%fused_computation.2 | convolution fusion | flops 13742899200 | bytes 27082752 | tf_op jit(solution)/shard_map/td,te->de/dot_general | solution.py:1373
  240.8 5.9 %collective-permute-start = (bf16[7,224,768]{2,1,0:T(8,128)(2,1)S(1)}, bf16[7,224,768]{2,1,0:T(8,128)(2,1)S(1)}, u32[]{:S(2)}, u32[]{:S(2)}) collective-permute-start(bf16[7,224,768]{2,1,0:T(8,128)(2,1)S(1)} %constant_dynamic-slice_fusion), channel_id=1, source_target_pairs={{0,1},{1,0},{2,3},{3,2},{4,5},{5,4},{6,7},{7,6},{8,9},{9,8},{10,11... | collective-permute-start | bytes 7225352 | tf_op jit(solution)/shard_map/ppermute | solution.py:1378
  246.7 0.8 collective-permute-start.1
  247.6 5.1 %convolution_convert_fusion.2.dwp_ref = bf16[768,768]{1,0:T(8,128)(2,1)} fusion(bf16[2912,768]{1,0:T(8,128)(2,1)S(1)} %bitcast.105, bf16[2912,768]{1,0:T(8,128)(2,1)S(1)} %bitcast.101), kind=kOutput, calls=%fused_computation.4 | convolution fusion | flops 3435724800 | bytes 10125312 | tf_op jit(solution)/shard_map/td,te->de/dot_general | solution.py:1373
  252.6 19.9 %convolution_convert_fusion.1.rest_0_ = bf16[768,3072]{1,0:T(8,128)(2,1)} fusion(bf16[2912,768]{1,0:T(8,128)(2,1)S(1)} %bitcast.110, bf16[2912,3072]{1,0:T(8,128)(2,1)} %get-tuple-element.79), kind=kOutput, calls=%fused_computation.3 | convolution fusion | flops 13742899200 | bytes 27082752 | tf_op jit(solution)/shard_map/td,te->de/dot_general | solution.py:1373
  272.5 60.4 %shard_map.354 = (bf16[13,224,2304]{2,1,0:T(8,128)(2,1)}, f32[128,256]{1,0:T(8,128)}, f32[2,8,768]{2,1,0:T(8,128)}, bf16[2,2,2,96,384]{4,3,2,1,0:T(8,128)(2,1)}, f32[192,384]{1,0:T(8,128)}) custom-call(s32[13,4]{1,0:T(8,128)} %pad_add_fusion.meta_ref, bf16[13,224,2304]{2,1,0:T(8,128)(2,1)} %get-tuple-element.83.qkv_ref, ...), custom_call_target="tpu_custom_call" | custom-call | flops 60000002048 | bytes 80000000 | tf_op jit(solution)/shard_map/pallas_call | solution.py:848
  332.9 1.0 dynamic-slice_bitcast_fusion
  333.9 1.2 collective-permute-start.2
  335.1 16.4 %bitcast_convert_fusion.dwq_ref = bf16[768,2304]{1,0:T(8,128)(2,1)} fusion(bf16[13,224,768]{2,1,0:T(8,128)(2,1)} %get-tuple-element.92, bf16[13,224,2304]{2,1,0:T(8,128)(2,1)} %get-tuple-element.89.dqkv_ref), kind=kOutput, calls=%fused_computation.1 | convolution fusion | flops 10307174400 | bytes 21430272 | tf_op jit(solution)/shard_map/td,te->de/dot_general | solution.py:1373
  351.7 1.5 collective-permute-start.3
  353.2 61.1 %shard_map.355 = (bf16[25,224,768]{2,1,0:T(8,128)(2,1)}, f32[192,384]{1,0:T(8,128)}, f32[16,128]{1,0:T(8,128)}, f32[16,256]{1,0:T(8,128)}, f32[8,128]{1,0:T(8,128)}) custom-call(s32[13,4]{1,0:T(8,128)} %pad_add_fusion.meta_ref, bf16[13,224,2304]{2,1,0:T(8,128)(2,1)} %get-tuple-element.89.dqkv_ref, bf16[768,2304]{1,0:T(8,128)(2,1)} %get-tuple-element.90.wqkv_ref, ...), custom_call_target="tpu_custom_call" | custom-call | flops 20000000000 | bytes 50000000 | tf_op jit(solution)/shard_map/pallas_call | solution.py:1218
  414.4 12.7 %shard_map.356 = (bf16[2,16,64,768]{3,2,1,0:T(8,128)(2,1)}, f32[2,16,64,768]{3,2,1,0:T(8,128)}, f32[1,96]{1,0:T(1,128)}, f32[1,96]{1,0:T(1,128)}, f32[1,96]{1,0:...) custom-call(s32[2,32]{1,0:T(2,128)} %add_add_fusion.table_ref, ...), custom_call_target="tpu_custom_call" | custom-call | flops 500000000 | bytes 20000000 | tf_op jit(solution)/shard_map/pallas_call | solution.py:1074
  427.1 1.3 reduce.1
  428.3 0.7 convert_add_fusion.1
  (66 shorter events, 7.4 us)
Async XLA Ops:
  7.2 55.8 %copy-start.1 = (s32[2,2]{1,0:T(2,128)S(1)}, s32[2,2]{1,0:T(2,128)}, u32[]{:S(2)}) copy-start(s32[2,2]{1,0:T(2,128)} %param.24) | copy-start | bytes 52
  7.2 121.9 %all-gather.3.cloned.1.call-start = ((), (), s32[]{:S(2)}) async-start(), calls=%async_computation | async-start | bytes 9732096 | tf_op jit(solution)/shard_map/all_gather | solution.py:1334
  219.4 28.1 %slice-start = ((s8[4472832]{0:T(1024)(128)(4,1)}), s8[4194304]{0:T(1024)(128)(4,1)S(1)}, s32[]{:S(2)}) async-start(s8[4472832]{0:T(1024)(128)(4,1)} %bitcast.100), calls=%async_computation.1 | async-start | bytes 8388608
  219.4 28.1 %slice-start.2 = ((s8[4472832]{0:T(1024)(128)(4,1)}), s8[4194304]{0:T(1024)(128)(4,1)S(1)}, s32[]{:S(2)}) async-start(s8[4472832]{0:T(1024)(128)(4,1)} %bitcast.103), calls=%async_computation.3 | async-start | bytes 8388608
  219.4 21.1 %copy-start = (bf16[2912,768]{1,0:T(8,128)(2,1)S(1)}, bf16[2912,768]{1,0:T(8,128)(2,1)}, u32[]{:S(2)}) copy-start(bf16[2912,768]{1,0:T(8,128)(2,1)} %get-tuple-element.77) | copy-start | bytes 13418500
  219.4 28.1 %slice-start.1 = ((s8[4472832]{0:T(1024)(128)(4,1)}), s8[278528]{0:T(1024)(128)(4,1)S(1)}, s32[]{:S(2)}) async-start(s8[4472832]{0:T(1024)(128)(4,1)} %bitcast.100), calls=%async_computation.2 | async-start | bytes 557056
  219.4 28.1 %slice-start.3 = ((s8[4472832]{0:T(1024)(128)(4,1)}), s8[278528]{0:T(1024)(128)(4,1)S(1)}, s32[]{:S(2)}) async-start(s8[4472832]{0:T(1024)(128)(4,1)} %bitcast.103), calls=%async_computation.4 | async-start | bytes 557056
  240.6 12.0 %slice-start.4 = ((s8[4472832]{0:T(1024)(128)(4,1)}), s8[278528]{0:T(1024)(128)(4,1)S(1)}, s32[]{:S(2)}) async-start(s8[4472832]{0:T(1024)(128)(4,1)} %bitcast.109), calls=%async_computation.5 | async-start | bytes 557056
  240.8 31.7 %collective-permute-start = (bf16[7,224,768]{2,1,0:T(8,128)(2,1)S(1)}, bf16[7,224,768]{2,1,0:T(8,128)(2,1)S(1)}, u32[]{:S(2)}, u32[]{:S(2)}) collective-permute-start(bf16[7,224,768]{2,1,0:T(8,128)(2,1)S(1)} %constant_dynamic-slice_fusion), channel_id=1, source_target_pairs={{0,1},{1,0},{2,3},{3,2},{4,5},{5,4},{6,7},{7,6},{8,9},{9,8},{10,11... | collective-permute-start | bytes 7225352 | tf_op jit(solution)/shard_map/ppermute | solution.py:1378
  246.7 25.8 %collective-permute-start.1 = (bf16[5,224,768]{2,1,0:T(8,128)(2,1)S(1)}, bf16[5,224,768]{2,1,0:T(8,128)(2,1)S(1)}, u32[]{:S(2)}, u32[]{:S(2)}) collective-permute-start(bf16[5,224,768]{2,1,0:T(8,128)(2,1)S(1)} %bitcast.67), channel_id=1, source_target_pairs={{1,2},{2,1},{5,6},{6,5},{9,10},{10,9},{13,14},{14,13},{17,18},{18,... | collective-permute-start | bytes 5160968 | tf_op jit(solution)/shard_map/ppermute | solution.py:1379
  247.6 5.1 %slice-start.5 = ((s8[4472832]{0:T(1024)(128)(4,1)}), s8[4194304]{0:T(1024)(128)(4,1)S(1)}, s32[]{:S(2)}) async-start(s8[4472832]{0:T(1024)(128)(4,1)} %bitcast.109), calls=%async_computation.6 | async-start | bytes 8388608
  272.5 60.4 %copy-start.3 = (bf16[5,224,768]{2,1,0:T(8,128)(2,1)}, bf16[5,224,768]{2,1,0:T(8,128)(2,1)S(1)}, u32[]{:S(2)}) copy-start(bf16[5,224,768]{2,1,0:T(8,128)(2,1)S(1)} %collective-permute-done.1.cross_ref) | copy-start | bytes 5160964
  272.5 60.4 %copy-start.2 = (bf16[7,224,768]{2,1,0:T(8,128)(2,1)}, bf16[7,224,768]{2,1,0:T(8,128)(2,1)S(1)}, u32[]{:S(2)}) copy-start(bf16[7,224,768]{2,1,0:T(8,128)(2,1)S(1)} %collective-permute-done.core_ref) | copy-start | bytes 7225348
  333.9 17.6 %collective-permute-start.2 = (bf16[2,2,96,384]{3,2,1,0:T(8,128)(2,1)S(1)}, bf16[2,2,96,384]{3,2,1,0:T(8,128)(2,1)S(1)}, u32[]{:S(2)}, u32[]{:S(2)}) collective-permute-start(bf16[2,2,96,384]{3,2,1,0:T(8,128)(2,1)S(1)} %dynamic-slice_bitcast_fusion), channel_id=1, source_target_pairs={{0,16},{4,20},{8,24},{12,28},{16,0},{20,4},{24,8},{28,12},{1,17},{... | collective-permute-start | bytes 884744 | tf_op jit(solution)/shard_map/ppermute | solution.py:1397
  335.1 16.4 %copy-start.4 = (bf16[2,2,2,96,384]{4,3,2,1,0:T(8,128)(2,1)S(1)}, bf16[2,2,2,96,384]{4,3,2,1,0:T(8,128)(2,1)}, u32[]{:S(2)}) copy-start(bf16[2,2,2,96,384]{4,3,2,1,0:T(8,128)(2,1)} %get-tuple-element.115) | copy-start | bytes 1769476
  351.7 76.6 %collective-permute-start.3 = (bf16[2,96,384]{2,1,0:T(8,128)(2,1)S(1)}, bf16[2,96,384]{2,1,0:T(8,128)(2,1)S(1)}, u32[]{:S(2)}, u32[]{:S(2)}) collective-permute-start(bf16[2,96,384]{2,1,0:T(8,128)(2,1)S(1)} %dynamic-slice_bitcast_fusion.1), channel_id=1, source_target_pairs={{0,8},{4,12},{8,0},{12,4},{16,24},{20,28},{24,16},{28,20},{1,9},{5... | collective-permute-start | bytes 442376 | tf_op jit(solution)/shard_map/ppermute | solution.py:1397
  414.4 14.7 %copy-start.5 = (f32[192,384]{1,0:T(8,128)S(1)}, f32[192,384]{1,0:T(8,128)}, u32[]{:S(2)}) copy-start(f32[192,384]{1,0:T(8,128)} %get-tuple-element.117) | copy-start | bytes 884740
Sparse Core Ops, SparseCore 0:
  12.1 94.2 all-gather.2
